TPU v7x, 32 devices: a whole 2x2x4 slice. The times are simulated.
32 devices in a mesh: dp: 8 (over z, y), seq: 4 (over x, core).
Axes of the slice: x: 2, y: 2, z: 4, core: 2. Of those that a mesh axis runs over, the one named last changes fastest.
Arguments:
- queries: bfloat16 [8, 512, 6144], P('dp', 'seq'), may hold values from -6 to 6
- keys: bfloat16 [8, 512, 768], P('dp', 'seq'), may hold values from -6 to 6
- values: bfloat16 [8, 512, 768], P('dp', 'seq'), may hold values from -6 to 6
- segments: int32 [8, 512], P('dp'), may hold values from 0 to 1, never falling along the last dimension, each value on 1 to 384 neighbouring positions
Outputs:
- attended: bfloat16 [8, 512, 6144], P('dp', 'seq')
- query_factor: float32 [48], replicated
- key_head_factor: float32 [6], replicated
Inputs may be any that keep to these rules, and one draw needn't show every extreme that they name: `segments`: each row's ids never fall; a document holds at most 384 positions, and some document holds exactly 384.
All inputs are finite; a program needn't handle non-finite values.
Results may differ from a plain program's by a relative error of at most 0.0046.
Values may be sent and summed in bfloat16 or wider, within the bound.
No kernel may reach another device: no remote copies, remote signals or barrier semaphores. Data moves between devices by JAX's collectives and lax.ppermute only.
A program may use at most 64 MiB of HBM per device.

v0:
```python
import jax
import jax.numpy as jnp
from jax import lax
from jax.sharding import PartitionSpec as P

QUERY_HEADS = 48
KEY_VALUE_HEADS = 6
HEAD_SIZE = 128
DOCUMENT_LIMIT = 384


clip_level = 6.0


def passed_along(x, axis, by):
    devices = lax.axis_size(axis)
    pairs = [(i, i + by) for i in range(devices) if 0 <= i + by < devices]
    return lax.ppermute(x, axis, pairs)


def attend(query_block, key_block, value_block, query_pos, key_pos, doc_ids):
    scale = query_block.shape[-1] ** (-0.5)
    logits = (
        jnp.einsum("qcgd,kcd->cgqk", query_block, key_block, preferred_element_type=jnp.float32)
        * scale
    )
    query_doc = jnp.take(doc_ids, query_pos)
    key_doc = jnp.take(doc_ids, jnp.maximum(key_pos, 0))
    valid = (
        (key_pos[None, :] <= query_pos[:, None])
        & (key_pos[None, :] >= 0)
        & (key_doc[None, :] == query_doc[:, None])
    )
    logits = jnp.where(valid, logits, -1e30)
    largest = jnp.max(logits, axis=-1, keepdims=True)
    expo = jnp.exp(logits - largest)
    total = jnp.sum(expo, axis=-1, keepdims=True)
    weights = (expo / total).astype(jnp.bfloat16)
    mixed = jnp.einsum(
        "cgqk,kcd->qcgd", weights, value_block, preferred_element_type=jnp.float32
    ).astype(jnp.bfloat16)
    return (mixed, jnp.max(largest[..., 0], axis=-1))


def clip_factors(head_max):
    query_group = QUERY_HEADS // KEY_VALUE_HEADS
    clipped_logits = clip_level / jnp.maximum(head_max, clip_level)
    key_head_factor = jnp.sqrt(
        jnp.min(clipped_logits.reshape(KEY_VALUE_HEADS, query_group), axis=1)
    )
    query_factor = clipped_logits / jnp.repeat(key_head_factor, query_group)
    return (query_factor, key_head_factor)


def local(queries, keys, values, segments):
    query_group = QUERY_HEADS // KEY_VALUE_HEADS
    rank_index = lax.axis_index("seq")
    rows_per_shard = queries.shape[1]
    doc_ids = segments[0]
    reach = (DOCUMENT_LIMIT - 1 + rows_per_shard - 1) // rows_per_shard
    own_pairs = jnp.concatenate([keys[0], values[0]], axis=1)
    earlier = []
    for distance in range(reach, 0, -1):
        earlier.append(passed_along(own_pairs, "seq", distance))
    window = jnp.concatenate(earlier + [own_pairs], axis=0)
    window_rows = window.shape[0]
    key_heads = window[:, : KEY_VALUE_HEADS * HEAD_SIZE].reshape(
        window_rows, KEY_VALUE_HEADS, HEAD_SIZE
    )
    value_heads = window[:, KEY_VALUE_HEADS * HEAD_SIZE :].reshape(
        window_rows, KEY_VALUE_HEADS, HEAD_SIZE
    )
    query_head_list = queries[0].reshape(rows_per_shard, KEY_VALUE_HEADS, query_group, HEAD_SIZE)
    query_pos = jnp.arange(rows_per_shard, dtype=jnp.int32) + rank_index * rows_per_shard
    key_pos = jnp.arange(window_rows, dtype=jnp.int32) + (rank_index - reach) * rows_per_shard
    pieces = []
    maxima = []
    for column in range(KEY_VALUE_HEADS):
        mixed, largest = attend(
            query_head_list[:, column : column + 1],
            key_heads[:, column : column + 1],
            value_heads[:, column : column + 1],
            query_pos,
            key_pos,
            doc_ids,
        )
        pieces.append(mixed)
        maxima.append(largest)
    attended = jnp.concatenate(pieces, axis=1).reshape(rows_per_shard, QUERY_HEADS * HEAD_SIZE)
    candidates = jnp.concatenate(maxima, axis=0).reshape(QUERY_HEADS)
    head_max = lax.pmax(candidates, ("dp", "seq"))
    query_factor, key_head_factor = clip_factors(head_max)
    return (attended[None], query_factor, key_head_factor)


def solution(mesh):
    in_specs = (P("dp", "seq", None), P("dp", "seq", None), P("dp", "seq", None), P("dp", None))
    out_specs = (P("dp", "seq", None), P(), P())
    return jax.shard_map(local, mesh=mesh, in_specs=in_specs, out_specs=out_specs, check_vma=False)
```

profile of v0, /device:TPU:0, one launch (start us, length us, event | category | flops | bytes accessed | tf_op | source)
XLA Modules:
  0.0 79.2 jit_solution(9244278209751972243)
XLA Ops:
  0.6 0.0 copy-start
  0.6 0.0 copy-start.1
  0.7 1.2 %copy.16 = bf16[1,128,768]{1,2,0:T(8,128)(2,1)S(1)} copy(bf16[1,128,768]{2,1,0:T(8,128)(2,1)} %param.10) | data formatting | bytes 393216 | tf_op args[2]
  1.9 1.1 %copy.15 = bf16[1,128,768]{1,2,0:T(8,128)(2,1)S(1)} copy(bf16[1,128,768]{2,1,0:T(8,128)(2,1)} %param.9) | data formatting | bytes 393216 | tf_op args[1]
  3.0 0.8 pad_maximum_fusion
  3.7 3.1 %collective-permute-start.2 = (bf16[128,1536]{0,1:T(8,128)(2,1)}, bf16[128,1536]{0,1:T(8,128)(2,1)}, u32[]{:S(2)}, u32[]{:S(2)}) collective-permute-start(bf16[128,1536]{0,1:T(8,128)(2,1)} %pad_maximum_fusion), channel_id=1, source_target_pairs={{0,1},{1,2},{2,3},{4,5},{5,6},{6,7},{8,9},{9,10},{10,11},{12,13},{... | collective-permute-start | bytes 1179656 | tf_op jit(solution)/shard_map/ppermute | solution.py:18
  6.8 4.4 %collective-permute-start.1 = (bf16[128,1536]{0,1:T(8,128)(2,1)}, bf16[128,1536]{0,1:T(8,128)(2,1)}, u32[]{:S(2)}, u32[]{:S(2)}) collective-permute-start(bf16[128,1536]{0,1:T(8,128)(2,1)} %pad_maximum_fusion), channel_id=1, source_target_pairs={{0,2},{1,3},{4,6},{5,7},{8,10},{9,11},{12,14},{13,15},{16,18},{17,... | collective-permute-start | bytes 1179656 | tf_op jit(solution)/shard_map/ppermute | solution.py:18
  11.3 2.0 %collective-permute-start = (bf16[128,1536]{0,1:T(8,128)(2,1)}, bf16[128,1536]{0,1:T(8,128)(2,1)}, u32[]{:S(2)}, u32[]{:S(2)}) collective-permute-start(bf16[128,1536]{0,1:T(8,128)(2,1)} %pad_maximum_fusion), channel_id=1, source_target_pairs={{0,3},{4,7},{8,11},{12,15},{16,19},{20,23},{24,27},{28,31}} | collective-permute-start | bytes 1179656 | tf_op jit(solution)/shard_map/ppermute | solution.py:18
  13.3 0.0 copy-done
  13.3 1.3 %gather_fusion.1 = s32[128]{0:T(128)S(1)} fusion(s32[512]{0:T(512)S(1)} %bitcast.194, s32[1024]{0:T(1024)S(1)} %pad_clamp_fusion), kind=kCustom, calls=%fused_computation.1.clone | custom fusion | bytes 1536 | tf_op jit(solution)/shard_map/jit(_take)/gather | solution.py:27
  14.6 3.5 %gather_fusion = s32[512]{0:T(512)S(1)} fusion(s32[512]{0:T(512)S(1)} %bitcast.193, s32[1024]{0:T(1024)S(1)} %pad_clamp_fusion.1), kind=kCustom, calls=%fused_computation.clone | custom fusion | bytes 6144 | tf_op jit(solution)/shard_map/jit(_take)/gather | solution.py:28
  18.2 0.5 fusion.25
  18.7 0.0 copy-done.1
  18.7 0.9 %copy.18 = bf16[1,128,6144]{1,2,0:T(8,128)(2,1)S(1)} copy(bf16[1,128,6144]{2,1,0:T(8,128)(2,1)S(1)} %copy-done.1) | data formatting | bytes 3145728 | tf_op args[0]
  19.6 0.9 %compare_and_fusion = pred[128,512]{0,1:T(8,128)(4,1)S(1)} fusion(s32[128]{0:T(128)S(1)} %and_select_fusion, s32[128]{0:T(128)S(1)} %iota_add_fusion.1, s32[512]{0:T(512)S(1)} %compare_select_fusion.1, s32[512]{0:T(512)S(1)} %iota_add_fusion, pred[512]{0:T(512)(128)(4,1)} %fusion.25), kind=kLoop, calls=%fused_computation.58 | loop fusion | flops 262144 | bytes 71168 | tf_op jit(solution)/shard_map/and | solution.py:30
  20.5 0.0 collective-permute-done.2
  20.5 0.0 collective-permute-done.1
  20.6 5.7 %collective-permute-done = bf16[128,1536]{0,1:T(8,128)(2,1)} collective-permute-done((bf16[128,1536]{0,1:T(8,128)(2,1)}, bf16[128,1536]{0,1:T(8,128)(2,1)}, u32[]{:S(2)}, u32[]{:S(2)}) %collective-permute-start) | collective-permute-done | bytes 393248 | tf_op jit(solution)/shard_map/ppermute | solution.py:18
  26.2 1.5 %maximum_maximum_fusion = bf16[512,1536]{0,1:T(8,128)(2,1)S(1)} fusion(bf16[128,768]{0,1:T(8,128)(2,1)S(1)} %bitcast.196, bf16[128,768]{0,1:T(8,128)(2,1)S(1)} %bitcast.198, bf16[128,1536]{0,1:T(8,128)(2,1)} %collective-permute-done.2, bf16[128,1536]{0,1:T(8,128)(2,1)} %collective-permute-done.1, bf16[128,1536]{0,1:T(8,128)(2,1)} %collective-permute-done), kind=kLoop, calls=%fused_computation.26 | loop fusion | flops 7864320 | bytes 3145728 | tf_op jit(solution)/shard_map/concatenate | solution.py:65
  27.7 0.1 fusion.32
  27.8 0.5 fusion.33
  28.3 0.5 fusion.34
  28.8 0.5 fusion.35
  29.2 0.5 fusion.36
  29.7 0.5 fusion.37
  30.2 0.5 fusion.38
  30.6 0.8 %fusion.30 = (f32[8]{0:T(128)S(1)}, f32[8,128]{1,0:T(8,128)S(1)}, f32[8,128]{1,0:T(8,128)S(1)}, f32[8]{0:T(128)S(1)}) fusion(f32[1,8,128,512]{2,3,1,0:T(8,128)S(1)} %get-tuple-element.28, f32[8,128]{1,0:T(8,128)S(1)} %get-tuple-element.27, f32[1,8,128,512]{2,3,1,0:T(8,128)S(1)} %get-tuple-element.26, f32[8,128]{1,0:T(8,128)S(1)} %get-tuple-element.25), kind=kLoop, calls=%fused_computation.86 | loop fusion | flops 3143664 | bytes 4210752 | tf_op jit(solution)/shard_map/reduce_max | solution.py:42
  31.5 0.5 fusion.7
  32.0 0.6 fusion.9
  32.6 0.9 %fusion.28 = (f32[8]{0:T(128)S(1)}, f32[8,128]{1,0:T(8,128)S(1)}, f32[8,128]{1,0:T(8,128)S(1)}, f32[8]{0:T(128)S(1)}) fusion(f32[1,8,128,512]{2,3,1,0:T(8,128)S(1)} %get-tuple-element.32, f32[8,128]{1,0:T(8,128)S(1)} %get-tuple-element.31, f32[1,8,128,512]{2,3,1,0:T(8,128)S(1)} %get-tuple-element.30, f32[8,128]{1,0:T(8,128)S(1)} %get-tuple-element.29), kind=kLoop, calls=%fused_computation.84 | loop fusion | flops 3143664 | bytes 4210752 | tf_op jit(solution)/shard_map/reduce_max | solution.py:42
  33.5 0.6 fusion.11
  34.1 0.6 fusion.13
  34.7 0.9 %fusion.26 = (f32[8]{0:T(128)S(1)}, f32[8,128]{1,0:T(8,128)S(1)}, f32[8,128]{1,0:T(8,128)S(1)}, f32[8]{0:T(128)S(1)}) fusion(f32[1,8,128,512]{2,3,1,0:T(8,128)S(1)} %get-tuple-element.36, f32[8,128]{1,0:T(8,128)S(1)} %get-tuple-element.35, f32[1,8,128,512]{2,3,1,0:T(8,128)S(1)} %get-tuple-element.34, f32[8,128]{1,0:T(8,128)S(1)} %get-tuple-element.33), kind=kLoop, calls=%fused_computation.82 | loop fusion | flops 3143664 | bytes 4210752 | tf_op jit(solution)/shard_map/reduce_max | solution.py:42
  35.6 0.6 fusion.15
  36.2 0.6 fusion.17
  36.8 1.6 %copy.36 = bf16[1,128,6144]{2,1,0:T(8,128)(2,1)} copy(bf16[1,128,6144]{1,2,0:T(8,128)(2,1)S(1)} %bitcast.205) | data formatting | bytes 3145728
  38.4 0.1 reshape.239
  38.4 39.8 %pmax.7 = f32[48]{0:T(128)S(1)} all-reduce(f32[48]{0:T(128)S(1)} %reshape.239), channel_id=1, replica_groups=mesh['dp'=8,'seq'=4] {'dp','seq'}, use_global_device_ids=true, to_apply=%region_18.21 | all-reduce | flops 48 | bytes 384 | tf_op jit(solution)/shard_map/pmax | solution.py:91
  78.3 0.1 reshape.240
  78.4 0.1 reduce_min.9
  78.5 0.0 copy-start.2
  78.5 0.1 broadcast_in_dim.34
  78.6 0.1 reshape.241
  78.6 0.5 multiply_divide_fusion
  79.2 0.0 copy-done.2
  (11 shorter events, 0.1 us)
Async XLA Ops:
  0.6 12.7 %copy-start = (s32[1,512]{1,0:T(1,128)S(1)}, s32[1,512]{1,0:T(1,128)}, u32[]{:S(2)}) copy-start(s32[1,512]{1,0:T(1,128)} %param.11) | copy-start | bytes 6148
  0.6 18.0 %copy-start.1 = (bf16[1,128,6144]{2,1,0:T(8,128)(2,1)S(1)}, bf16[1,128,6144]{2,1,0:T(8,128)(2,1)}, u32[]{:S(2)}) copy-start(bf16[1,128,6144]{2,1,0:T(8,128)(2,1)} %param.8) | copy-start | bytes 4718596
  3.7 16.8 %collective-permute-start.2 = (bf16[128,1536]{0,1:T(8,128)(2,1)}, bf16[128,1536]{0,1:T(8,128)(2,1)}, u32[]{:S(2)}, u32[]{:S(2)}) collective-permute-start(bf16[128,1536]{0,1:T(8,128)(2,1)} %pad_maximum_fusion), channel_id=1, source_target_pairs={{0,1},{1,2},{2,3},{4,5},{5,6},{6,7},{8,9},{9,10},{10,11},{12,13},{... | collective-permute-start | bytes 1179656 | tf_op jit(solution)/shard_map/ppermute | solution.py:18
  6.8 13.7 %collective-permute-start.1 = (bf16[128,1536]{0,1:T(8,128)(2,1)}, bf16[128,1536]{0,1:T(8,128)(2,1)}, u32[]{:S(2)}, u32[]{:S(2)}) collective-permute-start(bf16[128,1536]{0,1:T(8,128)(2,1)} %pad_maximum_fusion), channel_id=1, source_target_pairs={{0,2},{1,3},{4,6},{5,7},{8,10},{9,11},{12,14},{13,15},{16,18},{17,... | collective-permute-start | bytes 1179656 | tf_op jit(solution)/shard_map/ppermute | solution.py:18
  11.3 15.0 %collective-permute-start = (bf16[128,1536]{0,1:T(8,128)(2,1)}, bf16[128,1536]{0,1:T(8,128)(2,1)}, u32[]{:S(2)}, u32[]{:S(2)}) collective-permute-start(bf16[128,1536]{0,1:T(8,128)(2,1)} %pad_maximum_fusion), channel_id=1, source_target_pairs={{0,3},{4,7},{8,11},{12,15},{16,19},{20,23},{24,27},{28,31}} | collective-permute-start | bytes 1179656 | tf_op jit(solution)/shard_map/ppermute | solution.py:18
  78.5 0.7 copy-start.2
where the time goes:
time: 79.5 us; the launch traced here: 79.2 us
  blocking collectives  39.8 us (50%)
  local copies, waits for them, and re-layouts  10 us (13%)
  starting transfers between devices  9.55 us (12%)
  other arithmetic  7.08 us (9%)
  matrix products  6.15 us (8%)
  waiting for transfers between devices  5.69 us (7%)
  between operations  0.87 us (1%)
    pmax x1, blocking collectives, local(): head_max = lax.pmax(candidates, ('dp', 'seq'))  39.8 us
    ppermute x3, starting transfers between devices, passed_along(): return lax.ppermute(x, axis, pairs)  9.55 us
    ppermute x3, waiting for transfers between devices, passed_along(): return lax.ppermute(x, axis, pairs)  5.69 us
    unnamed x10, local copies, waits for them, and re-layouts  4.78 us
    gather x1, local copies, waits for them, and re-layouts, attend(): key_doc = jnp.take(doc_ids, jnp.maximum(key_pos, 0))  3.51 us
    dot_general x6, matrix products, attend(): jnp.einsum('cgqk,kcd->qcgd', weights, value_block, preferred_element_type...  3.37 us
    dot_general x6, matrix products, attend(): jnp.einsum('qcgd,kcd->cgqk', query_block, key_block, preferred_element_ty...  2.78 us
    reduce_max x3, other arithmetic, attend(): return (mixed, jnp.max(largest[..., 0], axis=-1))  2.7 us
  transfers between devices with their start and end apart: 3, of which 1 were waited for; matrix products, arithmetic and copies ran while one was open for 9% of the time, Pallas kernels for 0%

commit v1 on v0

v1 whole, which is shorter than its diff:
```python
import functools
import math

import jax
import jax.numpy as jnp
from jax import lax
from jax.experimental import pallas as pl
from jax.experimental.pallas import tpu as pltpu
from jax.sharding import PartitionSpec as P

QUERY_HEADS = 48
KEY_VALUE_HEADS = 6
HEAD_SIZE = 128
DOCUMENT_LIMIT = 384
GROUP = QUERY_HEADS // KEY_VALUE_HEADS

clip_level = 6.0
SCALE = HEAD_SIZE ** (-0.5)
SCALE_2 = SCALE * math.log2(math.e)
MASKED = -1e30
NT = (((1,), (1,)), ((), ()))


def reach_of(rows, length, shards):
    reach = (DOCUMENT_LIMIT - 1 + rows - 1) // rows
    documents = length // 256
    least = length - (documents - 1) * DOCUMENT_LIMIT
    if shards == reach + 1 and documents > 1 and least >= rows:
        reach -= 1
    return reach


def fill_bias(seg_ref, bias_ref, rank, reach, rows):
    own = seg_ref[:, pl.ds(pl.multiple_of(rank * rows, rows), rows)]
    query_doc = jnp.broadcast_to(own, (rows, rows))
    key_index = lax.broadcasted_iota(jnp.int32, (rows, rows), 0)
    query_index = lax.broadcasted_iota(jnp.int32, (rows, rows), 1)
    for distance in range(reach + 1):
        block = jnp.maximum(rank - distance, 0)
        docs = seg_ref[:, pl.ds(pl.multiple_of(block * rows, rows), rows)]
        key_doc = jnp.broadcast_to(docs, (rows, rows)).T
        valid = key_doc == query_doc
        if distance == 0:
            valid = valid & (key_index <= query_index)
        else:
            valid = valid & (rank >= distance)
        bias_ref[distance * rows : (distance + 1) * rows, :] = jnp.where(valid, 0.0, MASKED)


def max_kernel(reach, shards_all, rank_ref, seg_ref, q_ref, *refs):
    key_refs, (row_max_ref, head_max_ref, bias_ref) = refs[: reach + 1], refs[reach + 1 :]
    rows = q_ref.shape[0]
    fill_bias(seg_ref, bias_ref, rank_ref[0], reach, rows)
    for column in range(KEY_VALUE_HEADS):
        at = slice(column * HEAD_SIZE, (column + 1) * HEAD_SIZE)
        key_block = jnp.concatenate([k[:, at] for k in key_refs], axis=0)
        for head in range(column * GROUP, (column + 1) * GROUP):
            q = q_ref[:, head * HEAD_SIZE : (head + 1) * HEAD_SIZE]
            logits = lax.dot_general(key_block, q, NT, preferred_element_type=jnp.float32)
            row_max_ref[head : head + 1, :] = jnp.max(
                logits + bias_ref[...], axis=0, keepdims=True
            )
    largest = row_max_ref[...]
    padded = jnp.concatenate([largest, largest, largest], axis=0)[:rows]
    head_max = jnp.max(padded.T, axis=0, keepdims=True) * SCALE
    head_max_ref[...] = jnp.broadcast_to(head_max[None], head_max_ref.shape)


def mix_kernel(reach, rank_ref, seg_ref, q_ref, row_max_ref, *refs):
    key_refs, value_refs = refs[: reach + 1], refs[reach + 1 : 2 * reach + 2]
    out_ref, bias_ref = refs[2 * reach + 2 :]
    rows = q_ref.shape[0]
    fill_bias(seg_ref, bias_ref, rank_ref[0], reach, rows)
    ones = jnp.ones((16, (reach + 1) * rows), jnp.bfloat16)
    for column in range(KEY_VALUE_HEADS):
        at = slice(column * HEAD_SIZE, (column + 1) * HEAD_SIZE)
        key_block = jnp.concatenate([k[:, at] for k in key_refs], axis=0)
        value_block = jnp.concatenate([v[:, at].T for v in value_refs], axis=1)
        value_block = jnp.concatenate([value_block, ones], axis=0)
        for head in range(column * GROUP, (column + 1) * GROUP):
            here = slice(head * HEAD_SIZE, (head + 1) * HEAD_SIZE)
            logits = lax.dot_general(
                key_block, q_ref[:, here], NT, preferred_element_type=jnp.float32
            )
            largest = row_max_ref[head : head + 1, :] * SCALE_2
            expo = jnp.exp2((logits + bias_ref[...]) * SCALE_2 - largest).astype(jnp.bfloat16)
            mixed = jnp.dot(value_block, expo, preferred_element_type=jnp.float32)
            share = 1.0 / mixed[HEAD_SIZE : HEAD_SIZE + 1, :]
            mixed = (mixed[:HEAD_SIZE, :] * share).astype(jnp.bfloat16)
            out_ref[:, here] = mixed.T


def row_maxima(rank, segments, queries, key_blocks, devices):
    reach, rows = len(key_blocks) - 1, queries.shape[0]
    vmem = pl.BlockSpec(memory_space=pltpu.VMEM)
    return pl.pallas_call(
        functools.partial(max_kernel, reach, devices),
        out_shape=(
            jax.ShapeDtypeStruct((QUERY_HEADS, rows), jnp.float32),
            jax.ShapeDtypeStruct((devices, 1, rows), jnp.float32),
        ),
        in_specs=[pl.BlockSpec(memory_space=pltpu.SMEM)] + [vmem] * (reach + 3),
        out_specs=(vmem, vmem),
        scratch_shapes=[pltpu.VMEM(((reach + 1) * rows, rows), jnp.float32)],
        compiler_params=pltpu.CompilerParams(vmem_limit_bytes=24 << 20),
        cost_estimate=pl.CostEstimate(
            flops=2 * QUERY_HEADS * HEAD_SIZE * rows * rows * (reach + 1),
            bytes_accessed=2 * queries.size,
            transcendentals=0,
        ),
        name="row_maxima",
    )(rank, segments, queries, *key_blocks)


def mix(rank, segments, queries, row_max, key_blocks, value_blocks):
    reach, rows = len(key_blocks) - 1, queries.shape[0]
    vmem = pl.BlockSpec(memory_space=pltpu.VMEM)
    return pl.pallas_call(
        functools.partial(mix_kernel, reach),
        out_shape=jax.ShapeDtypeStruct(queries.shape, jnp.bfloat16),
        in_specs=[pl.BlockSpec(memory_space=pltpu.SMEM)] + [vmem] * (2 * reach + 5),
        out_specs=vmem,
        scratch_shapes=[pltpu.VMEM(((reach + 1) * rows, rows), jnp.float32)],
        compiler_params=pltpu.CompilerParams(vmem_limit_bytes=24 << 20),
        cost_estimate=pl.CostEstimate(
            flops=4 * QUERY_HEADS * HEAD_SIZE * rows * rows * (reach + 1),
            bytes_accessed=4 * queries.size,
            transcendentals=QUERY_HEADS * rows * rows * (reach + 1),
        ),
        name="mix",
    )(rank, segments, queries, row_max, *key_blocks, *value_blocks)


def passed_along(x, by):
    shards = lax.axis_size("seq")
    pairs = [(i, i + by) for i in range(shards - by)]
    return lax.ppermute(x, "seq", pairs)


def clip_factors(head_max):
    clipped_logits = clip_level / jnp.maximum(head_max, clip_level)
    key_head_factor = jnp.sqrt(jnp.min(clipped_logits.reshape(KEY_VALUE_HEADS, GROUP), axis=1))
    query_factor = clipped_logits / jnp.repeat(key_head_factor, GROUP)
    return (query_factor, key_head_factor)


def local(queries, keys, values, segments):
    rows, length = queries.shape[1], segments.shape[1]
    shards = lax.axis_size("seq")
    devices = lax.axis_size("dp") * shards
    reach = reach_of(rows, length, shards)
    rank = lax.axis_index("seq").astype(jnp.int32).reshape(1)
    queries, keys, values = queries[0], keys[0], values[0]

    key_blocks = [keys] + [passed_along(keys, d) for d in range(1, reach + 1)]
    value_blocks = [values] + [passed_along(values, d) for d in range(1, reach + 1)]
    row_max, head_max = row_maxima(rank, segments, queries, key_blocks, devices)
    everyone = lax.all_to_all(head_max, ("dp", "seq"), 0, 0)
    attended = mix(rank, segments, queries, row_max, key_blocks, value_blocks)
    query_factor, key_head_factor = clip_factors(
        jnp.max(everyone[:, 0, :QUERY_HEADS], axis=0)
    )
    return (attended[None], query_factor, key_head_factor)


def solution(mesh):
    in_specs = (P("dp", "seq", None), P("dp", "seq", None), P("dp", "seq", None), P("dp", None))
    out_specs = (P("dp", "seq", None), P(), P())
    return jax.shard_map(local, mesh=mesh, in_specs=in_specs, out_specs=out_specs, check_vma=False)
```

time: 79.5 us -> 37.3 us (0.47)
  blocking collectives: 39.8 us -> 0 us
  Pallas kernels: 0 us -> 13.2 us
  starting transfers between devices: 9.55 us -> 18.2 us
  local copies, waits for them, and re-layouts: 10 us -> 3.28 us
  other arithmetic: 7.08 us -> 0.71 us
  matrix products: 6.15 us -> 0 us
  waiting for transfers between devices: 5.69 us -> 0.88 us
    pmax x1 -> x0, blocking collectives: 39.8 us -> none  [local(): head_max = lax.pmax(candidates, ('dp', 'seq'))]
    pallas_call x0 -> x2, Pallas kernels: none -> 13.2 us  [the longest x1 11 us: mix(): pl.pallas_call(functools.partial(mix_kernel, reach), out_shape=jax.ShapeD...]
    all_to_all x0 -> x1, starting transfers between devices: none -> 8.65 us  [local(): everyone = lax.all_to_all(head_max, ('dp', 'seq'), 0, 0)]
    dot_general x12 -> x0, matrix products: 6.15 us -> none  [the longest x6 3.37 us: attend(): jnp.einsum('cgqk,kcd->qcgd', weights, value_block, preferred_element_type...]
    ppermute x3 -> x4, waiting for transfers between devices: 5.69 us -> 0.88 us  [passed_along(): return lax.ppermute(x, 'seq', pairs)]
    gather x2 -> x0, local copies, waits for them, and re-layouts: 4.78 us -> none  [the longest x1 3.51 us: attend(): key_doc = jnp.take(doc_ids, jnp.maximum(key_pos, 0))]
    reduce_max x3 -> x1, other arithmetic: 2.7 us -> 0.05 us  [local(): jnp.max(everyone[:, 0, :QUERY_HEADS], axis=0)]
    concatenate x2 -> x0, other arithmetic: 2.25 us -> none  [the longest x1 1.47 us: local(): window = jnp.concatenate(earlier + [own_pairs], axis=0)]
  transfers between devices with their start and end apart: 3 -> 5, of which waited for: 1 -> 1; matrix products, arithmetic and copies ran while one was open for 9% -> 0% of each run, Pallas kernels for 0% -> 36%
where the time goes in v1:
time: 37.3 us; the launch traced here: 37 us
  starting transfers between devices  18.2 us (49%)
  Pallas kernels  13.2 us (35%)
  local copies, waits for them, and re-layouts  3.28 us (9%)
  waiting for transfers between devices  0.88 us (2%)
  between operations  0.75 us (2%)
  other arithmetic  0.71 us (2%)
    pallas_call x1, Pallas kernels, mix(): pl.pallas_call(functools.partial(mix_kernel, reach), out_shape=jax.ShapeD...  11 us
    ppermute x4, starting transfers between devices, passed_along(): return lax.ppermute(x, 'seq', pairs)  9.54 us
    all_to_all x1, starting transfers between devices, local(): everyone = lax.all_to_all(head_max, ('dp', 'seq'), 0, 0)  8.65 us
    unnamed x16, local copies, waits for them, and re-layouts  3.04 us
    pallas_call x1, Pallas kernels, row_maxima(): pl.pallas_call(functools.partial(max_kernel, reach, devices), out_shape=(...  2.14 us
    ppermute x4, waiting for transfers between devices, passed_along(): return lax.ppermute(x, 'seq', pairs)  0.88 us
  transfers between devices with their start and end apart: 5, of which 1 were waited for; matrix products, arithmetic and copies ran while one was open for 0% of the time, Pallas kernels for 36%

profile of v1, /device:TPU:0, one launch (start us, length us, event | category | flops | bytes accessed | tf_op | source)
XLA Modules:
  0.0 37.0 jit_solution(15800793027582176516)
XLA Ops:
  0.6 0.0 copy-start.6
  0.6 4.9 %collective-permute-start.1 = (bf16[128,768]{1,0:T(8,128)(2,1)}, bf16[128,768]{1,0:T(8,128)(2,1)S(1)}, u32[]{:S(2)}, u32[]{:S(2)}) collective-permute-start(bf16[128,768]{1,0:T(8,128)(2,1)} %bitcast.7), channel_id=1, source_target_pairs={{0,2},{1,3},{4,6},{5,7},{8,10},{9,11},{12,14},{13,15},{16,18},{17,... | collective-permute-start | bytes 589832 | tf_op jit(solution)/shard_map/ppermute | solution.py:137
  5.5 1.5 %collective-permute-start = (bf16[128,768]{1,0:T(8,128)(2,1)}, bf16[128,768]{1,0:T(8,128)(2,1)S(1)}, u32[]{:S(2)}, u32[]{:S(2)}) collective-permute-start(bf16[128,768]{1,0:T(8,128)(2,1)} %bitcast.8), channel_id=1, source_target_pairs={{0,1},{1,2},{2,3},{4,5},{5,6},{6,7},{8,9},{9,10},{10,11},{12,13},{... | collective-permute-start | bytes 589832 | tf_op jit(solution)/shard_map/ppermute | solution.py:137
  7.0 1.7 %collective-permute-start.3 = (bf16[128,768]{1,0:T(8,128)(2,1)}, bf16[128,768]{1,0:T(8,128)(2,1)S(1)}, u32[]{:S(2)}, u32[]{:S(2)}) collective-permute-start(bf16[128,768]{1,0:T(8,128)(2,1)} %bitcast.11), channel_id=1, source_target_pairs={{0,2},{1,3},{4,6},{5,7},{8,10},{9,11},{12,14},{13,15},{16,18},{17,... | collective-permute-start | bytes 589832 | tf_op jit(solution)/shard_map/ppermute | solution.py:137
  8.7 1.5 %collective-permute-start.2 = (bf16[128,768]{1,0:T(8,128)(2,1)}, bf16[128,768]{1,0:T(8,128)(2,1)S(1)}, u32[]{:S(2)}, u32[]{:S(2)}) collective-permute-start(bf16[128,768]{1,0:T(8,128)(2,1)} %bitcast.12), channel_id=1, source_target_pairs={{0,1},{1,2},{2,3},{4,5},{5,6},{6,7},{8,9},{9,10},{10,11},{12,13},{... | collective-permute-start | bytes 589832 | tf_op jit(solution)/shard_map/ppermute | solution.py:137
  10.2 0.9 %collective-permute-done.1.refs_2_ = bf16[128,768]{1,0:T(8,128)(2,1)S(1)} collective-permute-done((bf16[128,768]{1,0:T(8,128)(2,1)}, bf16[128,768]{1,0:T(8,128)(2,1)S(1)}, u32[]{:S(2)}, u32[]{:S(2)}) %collective-permute-start.1) | collective-permute-done | bytes 196640 | tf_op jit(solution)/shard_map/ppermute | solution.py:137
  11.1 0.0 collective-permute-done.refs_1_
  11.1 0.0 copy-start
  11.1 1.4 %copy-done = bf16[1,128,6144]{2,1,0:T(8,128)(2,1)S(1)} copy-done((bf16[1,128,6144]{2,1,0:T(8,128)(2,1)S(1)}, bf16[1,128,6144]{2,1,0:T(8,128)(2,1)}, u32[]{:S(2)}) %copy-start) | copy-done | bytes 1572888
  12.5 0.0 copy-start.2
  12.5 0.9 %copy-done.2 = bf16[1,128,768]{2,1,0:T(8,128)(2,1)S(1)} copy-done((bf16[1,128,768]{2,1,0:T(8,128)(2,1)S(1)}, bf16[1,128,768]{2,1,0:T(8,128)(2,1)}, u32[]{:S(2)}) %copy-start.2) | copy-done | bytes 196632
  13.4 0.0 copy-start.5
  13.4 0.7 %copy-done.5 = s32[1,512]{1,0:T(1,128)S(1)} copy-done((s32[1,512]{1,0:T(1,128)S(1)}, s32[1,512]{1,0:T(1,128)}, u32[]{:S(2)}) %copy-start.5) | copy-done | bytes 2072
  14.1 0.0 copy-start.1
  14.1 0.0 copy-start.3
  14.1 0.0 copy-start.4
  14.1 2.1 %row_maxima.1 = (f32[48,128]{1,0:T(8,128)S(1)}, f32[32,1,128]{2,1,0:T(1,128)}) custom-call(s32[1]{0:T(128)} %bitcast.rank_ref, s32[1,512]{1,0:T(1,128)S(1)} %copy-done.5, bf16[128,6144]{1,0:T(8,128)(2,1)S(1)} %bitcast.5, bf16[128,768]{1,0:T(8,128)(2,1)S(1)} %bitcast.9, bf16[128,768]{1,0:T(8,128)(2,1)S(1)} %collective-permute-done.refs_1_, ...), custom_call_target="tpu_custom_call" | custom-call | flops 603979776 | bytes 1572864 | tf_op jit(solution)/shard_map/row_maxima/pallas_call | solution.py:96
  16.3 8.6 %all-to-all-start = ((f32[32,1,128]{2,1,0:T(1,128)}), f32[32,1,128]{2,1,0:T(1,128)S(1)}, u32[]{:S(2)}, u32[]{:S(2)}) async-start(f32[32,1,128]{2,1,0:T(1,128)} %get-tuple-element.6), calls=%async_computation | async-start | bytes 32768 | tf_op jit(solution)/shard_map/all_to_all | solution.py:158
  24.9 0.0 collective-permute-done.3.refs_5_
  24.9 0.0 collective-permute-done.2.refs_4_
  24.9 0.0 copy-done.6
  24.9 0.0 copy-done.1
  25.0 0.0 copy-done.3
  25.0 0.0 copy-done.4
  25.0 11.0 %mix.1 = bf16[128,6144]{1,0:T(8,128)(2,1)} custom-call(s32[1]{0:T(128)} %bitcast.rank_ref, s32[1,512]{1,0:T(1,128)S(1)} %copy-done.6, bf16[128,6144]{1,0:T(8,128)(2,1)S(1)} %bitcast.6, f32[48,128]{1,0:T(8,128)S(1)} %get-tuple-element.5.row_max_ref, bf16[128,768]{1,0:T(8,128)(2,1)S(1)} %bitcast.10, bf16[128,768]{1,0:T(8,128)(2,1)S(1)} %collective-permute-done.refs_1_, ...), custom_call_target="tpu_custom_call" | custom-call | flops 1207959552 | bytes 3145728 | tf_op jit(solution)/shard_map/mix/pallas_call | solution.py:118
  36.0 0.0 all-to-all-done
  36.0 0.1 slice_reduce_fusion
  36.1 0.1 div.11
  36.2 0.1 reduce_min.9
  36.3 0.0 copy-start.7
  36.3 0.1 broadcast_in_dim.7
  36.4 0.1 reshape.19
  36.4 0.5 %multiply_divide_fusion = f32[48]{0:T(128)} fusion(f32[48]{0:T(128)S(1)} %reshape.19, f32[48]{0:T(128)S(1)} %slice_reduce_fusion), kind=kLoop, calls=%fused_computation.1 | loop fusion | flops 144 | bytes 576 | tf_op jit(solution)/shard_map/div | solution.py:143
  37.0 0.0 copy-done.7
  (2 shorter events, 0.0 us)
Async XLA Ops:
  0.6 24.3 %copy-start.6 = (s32[1,512]{1,0:T(1,128)S(1)}, s32[1,512]{1,0:T(1,128)}, u32[]{:S(2)}) copy-start(s32[1,512]{1,0:T(1,128)} %seg_ref.3) | copy-start | bytes 6148
  0.6 10.5 %collective-permute-start.1 = (bf16[128,768]{1,0:T(8,128)(2,1)}, bf16[128,768]{1,0:T(8,128)(2,1)S(1)}, u32[]{:S(2)}, u32[]{:S(2)}) collective-permute-start(bf16[128,768]{1,0:T(8,128)(2,1)} %bitcast.7), channel_id=1, source_target_pairs={{0,2},{1,3},{4,6},{5,7},{8,10},{9,11},{12,14},{13,15},{16,18},{17,... | collective-permute-start | bytes 589832 | tf_op jit(solution)/shard_map/ppermute | solution.py:137
  5.5 5.6 %collective-permute-start = (bf16[128,768]{1,0:T(8,128)(2,1)}, bf16[128,768]{1,0:T(8,128)(2,1)S(1)}, u32[]{:S(2)}, u32[]{:S(2)}) collective-permute-start(bf16[128,768]{1,0:T(8,128)(2,1)} %bitcast.8), channel_id=1, source_target_pairs={{0,1},{1,2},{2,3},{4,5},{5,6},{6,7},{8,9},{9,10},{10,11},{12,13},{... | collective-permute-start | bytes 589832 | tf_op jit(solution)/shard_map/ppermute | solution.py:137
  7.0 17.9 %collective-permute-start.3 = (bf16[128,768]{1,0:T(8,128)(2,1)}, bf16[128,768]{1,0:T(8,128)(2,1)S(1)}, u32[]{:S(2)}, u32[]{:S(2)}) collective-permute-start(bf16[128,768]{1,0:T(8,128)(2,1)} %bitcast.11), channel_id=1, source_target_pairs={{0,2},{1,3},{4,6},{5,7},{8,10},{9,11},{12,14},{13,15},{16,18},{17,... | collective-permute-start | bytes 589832 | tf_op jit(solution)/shard_map/ppermute | solution.py:137
  8.7 16.2 %collective-permute-start.2 = (bf16[128,768]{1,0:T(8,128)(2,1)}, bf16[128,768]{1,0:T(8,128)(2,1)S(1)}, u32[]{:S(2)}, u32[]{:S(2)}) collective-permute-start(bf16[128,768]{1,0:T(8,128)(2,1)} %bitcast.12), channel_id=1, source_target_pairs={{0,1},{1,2},{2,3},{4,5},{5,6},{6,7},{8,9},{9,10},{10,11},{12,13},{... | collective-permute-start | bytes 589832 | tf_op jit(solution)/shard_map/ppermute | solution.py:137
  11.1 1.4 %copy-start = (bf16[1,128,6144]{2,1,0:T(8,128)(2,1)S(1)}, bf16[1,128,6144]{2,1,0:T(8,128)(2,1)}, u32[]{:S(2)}) copy-start(bf16[1,128,6144]{2,1,0:T(8,128)(2,1)} %param.4) | copy-start | bytes 4718596
  12.5 0.9 %copy-start.2 = (bf16[1,128,768]{2,1,0:T(8,128)(2,1)S(1)}, bf16[1,128,768]{2,1,0:T(8,128)(2,1)}, u32[]{:S(2)}) copy-start(bf16[1,128,768]{2,1,0:T(8,128)(2,1)} %param.5) | copy-start | bytes 589828
  13.4 0.7 %copy-start.5 = (s32[1,512]{1,0:T(1,128)S(1)}, s32[1,512]{1,0:T(1,128)}, u32[]{:S(2)}) copy-start(s32[1,512]{1,0:T(1,128)} %seg_ref.3) | copy-start | bytes 6148
  14.1 10.8 %copy-start.1 = (bf16[1,128,6144]{2,1,0:T(8,128)(2,1)S(1)}, bf16[1,128,6144]{2,1,0:T(8,128)(2,1)}, u32[]{:S(2)}) copy-start(bf16[1,128,6144]{2,1,0:T(8,128)(2,1)} %param.4) | copy-start | bytes 4718596
  14.1 10.8 %copy-start.3 = (bf16[1,128,768]{2,1,0:T(8,128)(2,1)S(1)}, bf16[1,128,768]{2,1,0:T(8,128)(2,1)}, u32[]{:S(2)}) copy-start(bf16[1,128,768]{2,1,0:T(8,128)(2,1)} %param.5) | copy-start | bytes 589828
  14.1 10.8 %copy-start.4 = (bf16[1,128,768]{2,1,0:T(8,128)(2,1)S(1)}, bf16[1,128,768]{2,1,0:T(8,128)(2,1)}, u32[]{:S(2)}) copy-start(bf16[1,128,768]{2,1,0:T(8,128)(2,1)} %param.6) | copy-start | bytes 589828
  16.3 19.7 %all-to-all-start = ((f32[32,1,128]{2,1,0:T(1,128)}), f32[32,1,128]{2,1,0:T(1,128)S(1)}, u32[]{:S(2)}, u32[]{:S(2)}) async-start(f32[32,1,128]{2,1,0:T(1,128)} %get-tuple-element.6), calls=%async_computation | async-start | bytes 32768 | tf_op jit(solution)/shard_map/all_to_all | solution.py:158
  36.3 0.7 %copy-start.7 = (f32[6]{0:T(128)}, f32[6]{0:T(128)S(1)}, u32[]{:S(2)}) copy-start(f32[6]{0:T(128)S(1)} %sqrt.3) | copy-start | bytes 76

commit v2 on v1

v2 whole, which is shorter than its diff:
```python
import functools
import math

import jax
import jax.numpy as jnp
from jax import lax
from jax.experimental import pallas as pl
from jax.experimental.pallas import tpu as pltpu
from jax.sharding import PartitionSpec as P

QUERY_HEADS = 48
KEY_VALUE_HEADS = 6
HEAD_SIZE = 128
DOCUMENT_LIMIT = 384
GROUP = QUERY_HEADS // KEY_VALUE_HEADS

clip_level = 6.0
SCALE = HEAD_SIZE ** (-0.5)
SCALE_2 = SCALE * math.log2(math.e)
MASKED = -1e30
NT = (((1,), (1,)), ((), ()))


def reach_of(rows, length, shards):
    reach = (DOCUMENT_LIMIT - 1 + rows - 1) // rows
    documents = length // 256
    least = length - (documents - 1) * DOCUMENT_LIMIT
    if shards == reach + 1 and documents > 1 and least >= rows:
        reach -= 1
    return reach


def fill_bias(seg_ref, bias_ref, rank, distances, rows):
    own = seg_ref[:, pl.ds(pl.multiple_of(rank * rows, rows), rows)]
    query_doc = jnp.broadcast_to(own, (rows, rows))
    key_index = lax.broadcasted_iota(jnp.int32, (rows, rows), 0)
    query_index = lax.broadcasted_iota(jnp.int32, (rows, rows), 1)
    for place, distance in enumerate(distances):
        block = jnp.maximum(rank - distance, 0)
        docs = seg_ref[:, pl.ds(pl.multiple_of(block * rows, rows), rows)]
        key_doc = jnp.broadcast_to(docs, (rows, rows)).T
        valid = key_doc == query_doc
        if distance == 0:
            valid = valid & (key_index <= query_index)
        else:
            valid = valid & (rank >= distance)
        bias_ref[place * rows : (place + 1) * rows, :] = jnp.where(valid, 0.0, MASKED)


def block_maxima(q_ref, key_refs, bias_ref, head):
    column = head // GROUP
    at = slice(column * HEAD_SIZE, (column + 1) * HEAD_SIZE)
    key_block = jnp.concatenate([k[:, at] for k in key_refs], axis=0)
    q = q_ref[:, head * HEAD_SIZE : (head + 1) * HEAD_SIZE]
    logits = lax.dot_general(key_block, q, NT, preferred_element_type=jnp.float32)
    return jnp.max(logits + bias_ref[...], axis=0, keepdims=True)


def own_max_kernel(rank_ref, seg_ref, q_ref, key_ref, own_max_ref, bias_ref):
    fill_bias(seg_ref, bias_ref, rank_ref[0], (0,), q_ref.shape[0])
    for head in range(QUERY_HEADS):
        own_max_ref[head : head + 1, :] = block_maxima(q_ref, (key_ref,), bias_ref, head)


def max_kernel(reach, rank_ref, seg_ref, q_ref, own_max_ref, *refs):
    key_refs, (row_max_ref, head_max_ref, bias_ref) = refs[:reach], refs[reach:]
    rows = q_ref.shape[0]
    fill_bias(seg_ref, bias_ref, rank_ref[0], range(1, reach + 1), rows)
    for head in range(QUERY_HEADS):
        row_max_ref[head : head + 1, :] = jnp.maximum(
            own_max_ref[head : head + 1, :], block_maxima(q_ref, key_refs, bias_ref, head)
        )
    largest = row_max_ref[...]
    padded = jnp.concatenate([largest, largest, largest], axis=0)[:rows]
    head_max = jnp.max(padded.T, axis=0, keepdims=True) * SCALE
    head_max_ref[...] = jnp.broadcast_to(head_max[None], head_max_ref.shape)


def mix_kernel(reach, rank_ref, seg_ref, q_ref, row_max_ref, *refs):
    key_refs, value_refs = refs[: reach + 1], refs[reach + 1 : 2 * reach + 2]
    out_ref, bias_ref = refs[2 * reach + 2 :]
    rows = q_ref.shape[0]
    fill_bias(seg_ref, bias_ref, rank_ref[0], range(reach + 1), rows)
    for column in range(KEY_VALUE_HEADS):
        at = slice(column * HEAD_SIZE, (column + 1) * HEAD_SIZE)
        key_block = jnp.concatenate([k[:, at] for k in key_refs], axis=0)
        value_block = jnp.concatenate([v[:, at].T for v in value_refs], axis=1)
        for head in range(column * GROUP, (column + 1) * GROUP):
            here = slice(head * HEAD_SIZE, (head + 1) * HEAD_SIZE)
            logits = lax.dot_general(
                key_block, q_ref[:, here], NT, preferred_element_type=jnp.float32
            )
            largest = row_max_ref[head : head + 1, :] * SCALE_2
            expo = jnp.exp2((logits + bias_ref[...]) * SCALE_2 - largest)
            share = 1.0 / jnp.sum(expo, axis=0, keepdims=True)
            mixed = jnp.dot(
                value_block, expo.astype(jnp.bfloat16), preferred_element_type=jnp.float32
            )
            out_ref[:, here] = (mixed * share).astype(jnp.bfloat16).T


VMEM = pl.BlockSpec(memory_space=pltpu.VMEM)


def call(kernel, name, out_shape, blocks, rows, products, exponentials, rank, *arrays):
    several = isinstance(out_shape, tuple)
    pairs = QUERY_HEADS * rows * rows * blocks
    return pl.pallas_call(
        kernel,
        out_shape=out_shape,
        in_specs=[pl.BlockSpec(memory_space=pltpu.SMEM)] + [VMEM] * len(arrays),
        out_specs=(VMEM,) * len(out_shape) if several else VMEM,
        scratch_shapes=[pltpu.VMEM((blocks * rows, rows), jnp.float32)],
        compiler_params=pltpu.CompilerParams(vmem_limit_bytes=24 << 20),
        cost_estimate=pl.CostEstimate(
            flops=2 * products * HEAD_SIZE * pairs,
            bytes_accessed=2 * QUERY_HEADS * HEAD_SIZE * rows * products,
            transcendentals=exponentials * pairs,
        ),
        name=name,
    )(rank, *arrays)


def own_maxima(rank, segments, queries, keys):
    rows = queries.shape[0]
    out_shape = jax.ShapeDtypeStruct((QUERY_HEADS, rows), jnp.float32)
    return call(
        own_max_kernel, "own_maxima", out_shape, 1, rows, 1, 0, rank, segments, queries, keys
    )


def row_maxima(rank, segments, queries, own_max, key_blocks, devices):
    reach, rows = len(key_blocks), queries.shape[0]
    out_shape = (
        jax.ShapeDtypeStruct((QUERY_HEADS, rows), jnp.float32),
        jax.ShapeDtypeStruct((devices, 1, rows), jnp.float32),
    )
    kernel = functools.partial(max_kernel, reach)
    return call(
        kernel, "row_maxima", out_shape, reach, rows, 1, 0, rank, segments, queries, own_max, *key_blocks
    )


def mix(rank, segments, queries, row_max, key_blocks, value_blocks):
    reach, rows = len(key_blocks) - 1, queries.shape[0]
    out_shape = jax.ShapeDtypeStruct(queries.shape, jnp.bfloat16)
    kernel = functools.partial(mix_kernel, reach)
    arrays = (rank, segments, queries, row_max, *key_blocks, *value_blocks)
    return call(kernel, "mix", out_shape, reach + 1, rows, 2, 1, *arrays)


def passed_along(x, by):
    shards = lax.axis_size("seq")
    pairs = [(i, i + by) for i in range(shards - by)]
    return lax.ppermute(x, "seq", pairs)


def clip_factors(head_max):
    clipped_logits = clip_level / jnp.maximum(head_max, clip_level)
    key_head_factor = jnp.sqrt(jnp.min(clipped_logits.reshape(KEY_VALUE_HEADS, GROUP), axis=1))
    query_factor = clipped_logits / jnp.repeat(key_head_factor, GROUP)
    return (query_factor, key_head_factor)


def local(queries, keys, values, segments):
    rows, length = queries.shape[1], segments.shape[1]
    shards = lax.axis_size("seq")
    devices = lax.axis_size("dp") * shards
    reach = reach_of(rows, length, shards)
    rank = lax.axis_index("seq").astype(jnp.int32).reshape(1)
    queries, keys, values = queries[0], keys[0], values[0]

    earlier_keys = [passed_along(keys, d) for d in range(1, reach + 1)]
    own_max = own_maxima(rank, segments, queries, keys)
    sent_values, own_max = lax.optimization_barrier((values, own_max))
    earlier_values = [passed_along(sent_values, d) for d in range(1, reach + 1)]
    row_max, head_max = row_maxima(rank, segments, queries, own_max, earlier_keys, devices)
    everyone = lax.all_to_all(head_max, ("dp", "seq"), 0, 0)
    attended = mix(
        rank, segments, queries, row_max, [keys] + earlier_keys, [values] + earlier_values
    )
    query_factor, key_head_factor = clip_factors(
        jnp.max(everyone[:, 0, :QUERY_HEADS], axis=0)
    )
    return (attended[None], query_factor, key_head_factor)


def solution(mesh):
    in_specs = (P("dp", "seq", None), P("dp", "seq", None), P("dp", "seq", None), P("dp", None))
    out_specs = (P("dp", "seq", None), P(), P())
    return jax.shard_map(local, mesh=mesh, in_specs=in_specs, out_specs=out_specs, check_vma=False)
```

time: 37.3 us -> 29.6 us (0.79)
  Pallas kernels: 13.2 us -> 7.01 us
  starting transfers between devices: 18.2 us -> 14.5 us
  waiting for transfers between devices: 0.88 us -> 3.05 us
    pallas_call x2 -> x3, Pallas kernels: 13.2 us -> 7.01 us  [call(): pl.pallas_call(kernel, out_shape=out_shape, in_specs=[pl.BlockSpec(memory...]
    all_to_all x1, starting transfers between devices: 8.65 us -> 4.92 us  [local(): everyone = lax.all_to_all(head_max, ('dp', 'seq'), 0, 0)]
    all_to_all x1, waiting for transfers between devices: 0.01 us -> 3.04 us  [local(): everyone = lax.all_to_all(head_max, ('dp', 'seq'), 0, 0)]
    ppermute x4, waiting for transfers between devices: 0.88 us -> 0.01 us  [passed_along(): return lax.ppermute(x, 'seq', pairs)]
  transfers between devices with their start and end apart: 5 -> 5, of which waited for: 1 -> 1; matrix products, arithmetic and copies ran while one was open for 0% -> 0% of each run, Pallas kernels for 36% -> 24%
where the time goes in v2:
time: 29.6 us; the launch traced here: 29.3 us
  starting transfers between devices  14.5 us (49%)
  Pallas kernels  7.01 us (24%)
  local copies, waits for them, and re-layouts  3.27 us (11%)
  waiting for transfers between devices  3.05 us (10%)
  between operations  0.77 us (3%)
  other arithmetic  0.71 us (2%)
    ppermute x4, starting transfers between devices, passed_along(): return lax.ppermute(x, 'seq', pairs)  9.54 us
    pallas_call x3, Pallas kernels, call(): pl.pallas_call(kernel, out_shape=out_shape, in_specs=[pl.BlockSpec(memory...  7.01 us
    all_to_all x1, starting transfers between devices, local(): everyone = lax.all_to_all(head_max, ('dp', 'seq'), 0, 0)  4.92 us
    all_to_all x1, waiting for transfers between devices, local(): everyone = lax.all_to_all(head_max, ('dp', 'seq'), 0, 0)  3.04 us
    unnamed x16, local copies, waits for them, and re-layouts  3.03 us
  transfers between devices with their start and end apart: 5, of which 1 were waited for; matrix products, arithmetic and copies ran while one was open for 0% of the time, Pallas kernels for 24%

profile of v2, /device:TPU:0, one launch (start us, length us, event | category | flops | bytes accessed | tf_op | source)
XLA Modules:
  0.0 29.3 jit_solution(3358861045070467139)
XLA Ops:
  0.6 4.9 %collective-permute-start.1 = (bf16[128,768]{1,0:T(8,128)(2,1)}, bf16[128,768]{1,0:T(8,128)(2,1)S(1)}, u32[]{:S(2)}, u32[]{:S(2)}) collective-permute-start(bf16[128,768]{1,0:T(8,128)(2,1)} %bitcast.8), channel_id=1, source_target_pairs={{0,2},{1,3},{4,6},{5,7},{8,10},{9,11},{12,14},{13,15},{16,18},{17,... | collective-permute-start | bytes 589832 | tf_op jit(solution)/shard_map/ppermute | solution.py:155
  5.5 1.5 %collective-permute-start = (bf16[128,768]{1,0:T(8,128)(2,1)}, bf16[128,768]{1,0:T(8,128)(2,1)S(1)}, u32[]{:S(2)}, u32[]{:S(2)}) collective-permute-start(bf16[128,768]{1,0:T(8,128)(2,1)} %bitcast.9), channel_id=1, source_target_pairs={{0,1},{1,2},{2,3},{4,5},{5,6},{6,7},{8,9},{9,10},{10,11},{12,13},{... | collective-permute-start | bytes 589832 | tf_op jit(solution)/shard_map/ppermute | solution.py:155
  7.0 0.0 copy-start
  7.0 1.4 %copy-done = bf16[1,128,6144]{2,1,0:T(8,128)(2,1)S(1)} copy-done((bf16[1,128,6144]{2,1,0:T(8,128)(2,1)S(1)}, bf16[1,128,6144]{2,1,0:T(8,128)(2,1)}, u32[]{:S(2)}) %copy-start) | copy-done | bytes 1572888
  8.4 0.0 copy-start.2
  8.4 0.9 %copy-done.2 = bf16[1,128,768]{2,1,0:T(8,128)(2,1)S(1)} copy-done((bf16[1,128,768]{2,1,0:T(8,128)(2,1)S(1)}, bf16[1,128,768]{2,1,0:T(8,128)(2,1)}, u32[]{:S(2)}) %copy-start.2) | copy-done | bytes 196632
  9.3 0.0 copy-start.4
  9.3 0.7 %copy-done.4 = s32[1,512]{1,0:T(1,128)S(1)} copy-done((s32[1,512]{1,0:T(1,128)S(1)}, s32[1,512]{1,0:T(1,128)}, u32[]{:S(2)}) %copy-start.4) | copy-done | bytes 2072
  10.0 0.0 copy-start.1
  10.0 0.0 copy-start.3
  10.0 0.0 copy-start.5
  10.0 0.0 copy-start.6
  10.0 1.2 %own_maxima.1.own_max_ref = f32[48,128]{1,0:T(8,128)S(1)} custom-call(s32[1]{0:T(128)} %bitcast.rank_ref, s32[1,512]{1,0:T(1,128)S(1)} %copy-done.4, bf16[128,6144]{1,0:T(8,128)(2,1)S(1)} %bitcast.5, bf16[128,768]{1,0:T(8,128)(2,1)S(1)} %bitcast.10), custom_call_target="tpu_custom_call" | custom-call | flops 201326592 | bytes 1572864 | tf_op jit(solution)/shard_map/own_maxima/pallas_call | solution.py:108
  11.2 1.7 %collective-permute-start.3 = (bf16[128,768]{1,0:T(8,128)(2,1)}, bf16[128,768]{1,0:T(8,128)(2,1)S(1)}, u32[]{:S(2)}, u32[]{:S(2)}) collective-permute-start(bf16[128,768]{1,0:T(8,128)(2,1)} %bitcast.12), channel_id=1, source_target_pairs={{0,2},{1,3},{4,6},{5,7},{8,10},{9,11},{12,14},{13,15},{16,18},{17,... | collective-permute-start | bytes 589832 | tf_op jit(solution)/shard_map/ppermute | solution.py:155
  13.0 1.5 %collective-permute-start.2 = (bf16[128,768]{1,0:T(8,128)(2,1)}, bf16[128,768]{1,0:T(8,128)(2,1)S(1)}, u32[]{:S(2)}, u32[]{:S(2)}) collective-permute-start(bf16[128,768]{1,0:T(8,128)(2,1)} %bitcast.13), channel_id=1, source_target_pairs={{0,1},{1,2},{2,3},{4,5},{5,6},{6,7},{8,9},{9,10},{10,11},{12,13},{... | collective-permute-start | bytes 589832 | tf_op jit(solution)/shard_map/ppermute | solution.py:155
  14.5 0.0 collective-permute-done.1.refs_1_.refs_2_
  14.5 0.0 collective-permute-done.refs_0_.refs_1_
  14.5 1.7 %row_maxima.1 = (f32[48,128]{1,0:T(8,128)S(1)}, f32[32,1,128]{2,1,0:T(1,128)}) custom-call(s32[1]{0:T(128)} %bitcast.rank_ref, s32[1,512]{1,0:T(1,128)S(1)} %copy-done.4, bf16[128,6144]{1,0:T(8,128)(2,1)S(1)} %bitcast.6, f32[48,128]{1,0:T(8,128)S(1)} %own_maxima.1.own_max_ref, bf16[128,768]{1,0:T(8,128)(2,1)S(1)} %collective-permute-done.refs_0_.refs_1_, ...), custom_call_target="tpu_custom_call" | custom-call | flops 402653184 | bytes 1572864 | tf_op jit(solution)/shard_map/row_maxima/pallas_call | solution.py:108
  16.2 4.9 %all-to-all-start = ((f32[32,1,128]{2,1,0:T(1,128)}), f32[32,1,128]{2,1,0:T(1,128)S(1)}, u32[]{:S(2)}, u32[]{:S(2)}) async-start(f32[32,1,128]{2,1,0:T(1,128)} %get-tuple-element.10), calls=%async_computation | async-start | bytes 32768 | tf_op jit(solution)/shard_map/all_to_all | solution.py:178
  21.2 0.0 collective-permute-done.3.refs_5_
  21.2 0.0 collective-permute-done.2.refs_4_
  21.2 0.0 copy-done.1
  21.2 0.0 copy-done.3
  21.2 0.0 copy-done.5
  21.2 0.0 copy-done.6
  21.2 4.0 %mix.1 = bf16[128,6144]{1,0:T(8,128)(2,1)} custom-call(s32[1]{0:T(128)} %bitcast.rank_ref, s32[1,512]{1,0:T(1,128)S(1)} %copy-done.5, bf16[128,6144]{1,0:T(8,128)(2,1)S(1)} %bitcast.7, f32[48,128]{1,0:T(8,128)S(1)} %get-tuple-element.8.row_max_ref, bf16[128,768]{1,0:T(8,128)(2,1)S(1)} %bitcast.11, bf16[128,768]{1,0:T(8,128)(2,1)S(1)} %collective-permute-done.refs_0_.refs_1_, ...), custom_call_target="tpu_custom_call" | custom-call | flops 1207959552 | bytes 3145728 | tf_op jit(solution)/shard_map/mix/pallas_call | solution.py:108
  25.3 3.0 %all-to-all-done = f32[32,1,128]{2,1,0:T(1,128)S(1)} async-done(((f32[32,1,128]{2,1,0:T(1,128)}), f32[32,1,128]{2,1,0:T(1,128)S(1)}, u32[]{:S(2)}, u32[]{:S(2)}) %all-to-all-start) | async-done | bytes 16416 | tf_op jit(solution)/shard_map/all_to_all | solution.py:178
  28.3 0.1 slice_reduce_fusion
  28.4 0.1 div.11
  28.4 0.1 reduce_min.9
  28.6 0.0 copy-start.7
  28.6 0.1 broadcast_in_dim.7
  28.7 0.1 reshape.19
  28.7 0.5 %multiply_divide_fusion = f32[48]{0:T(128)} fusion(f32[48]{0:T(128)S(1)} %reshape.19, f32[48]{0:T(128)S(1)} %slice_reduce_fusion), kind=kLoop, calls=%fused_computation.1 | loop fusion | flops 144 | bytes 576 | tf_op jit(solution)/shard_map/div | solution.py:161
  29.3 0.0 copy-done.7
  (2 shorter events, 0.0 us)
Async XLA Ops:
  0.6 13.8 %collective-permute-start.1 = (bf16[128,768]{1,0:T(8,128)(2,1)}, bf16[128,768]{1,0:T(8,128)(2,1)S(1)}, u32[]{:S(2)}, u32[]{:S(2)}) collective-permute-start(bf16[128,768]{1,0:T(8,128)(2,1)} %bitcast.8), channel_id=1, source_target_pairs={{0,2},{1,3},{4,6},{5,7},{8,10},{9,11},{12,14},{13,15},{16,18},{17,... | collective-permute-start | bytes 589832 | tf_op jit(solution)/shard_map/ppermute | solution.py:155
  5.5 9.0 %collective-permute-start = (bf16[128,768]{1,0:T(8,128)(2,1)}, bf16[128,768]{1,0:T(8,128)(2,1)S(1)}, u32[]{:S(2)}, u32[]{:S(2)}) collective-permute-start(bf16[128,768]{1,0:T(8,128)(2,1)} %bitcast.9), channel_id=1, source_target_pairs={{0,1},{1,2},{2,3},{4,5},{5,6},{6,7},{8,9},{9,10},{10,11},{12,13},{... | collective-permute-start | bytes 589832 | tf_op jit(solution)/shard_map/ppermute | solution.py:155
  7.0 1.4 %copy-start = (bf16[1,128,6144]{2,1,0:T(8,128)(2,1)S(1)}, bf16[1,128,6144]{2,1,0:T(8,128)(2,1)}, u32[]{:S(2)}) copy-start(bf16[1,128,6144]{2,1,0:T(8,128)(2,1)} %param.4) | copy-start | bytes 4718596
  8.4 0.9 %copy-start.2 = (bf16[1,128,768]{2,1,0:T(8,128)(2,1)S(1)}, bf16[1,128,768]{2,1,0:T(8,128)(2,1)}, u32[]{:S(2)}) copy-start(bf16[1,128,768]{2,1,0:T(8,128)(2,1)} %param.5) | copy-start | bytes 589828
  9.3 0.7 %copy-start.4 = (s32[1,512]{1,0:T(1,128)S(1)}, s32[1,512]{1,0:T(1,128)}, u32[]{:S(2)}) copy-start(s32[1,512]{1,0:T(1,128)} %seg_ref.5) | copy-start | bytes 6148
  10.0 11.2 %copy-start.1 = (bf16[1,128,6144]{2,1,0:T(8,128)(2,1)S(1)}, bf16[1,128,6144]{2,1,0:T(8,128)(2,1)}, u32[]{:S(2)}) copy-start(bf16[1,128,6144]{2,1,0:T(8,128)(2,1)} %param.4) | copy-start | bytes 4718596
  10.0 11.2 %copy-start.3 = (bf16[1,128,768]{2,1,0:T(8,128)(2,1)S(1)}, bf16[1,128,768]{2,1,0:T(8,128)(2,1)}, u32[]{:S(2)}) copy-start(bf16[1,128,768]{2,1,0:T(8,128)(2,1)} %param.5) | copy-start | bytes 589828
  10.0 11.2 %copy-start.5 = (s32[1,512]{1,0:T(1,128)S(1)}, s32[1,512]{1,0:T(1,128)}, u32[]{:S(2)}) copy-start(s32[1,512]{1,0:T(1,128)} %seg_ref.5) | copy-start | bytes 6148
  10.0 11.2 %copy-start.6 = (bf16[1,128,768]{2,1,0:T(8,128)(2,1)S(1)}, bf16[1,128,768]{2,1,0:T(8,128)(2,1)}, u32[]{:S(2)}) copy-start(bf16[1,128,768]{2,1,0:T(8,128)(2,1)} %param.6) | copy-start | bytes 589828
  11.2 9.9 %collective-permute-start.3 = (bf16[128,768]{1,0:T(8,128)(2,1)}, bf16[128,768]{1,0:T(8,128)(2,1)S(1)}, u32[]{:S(2)}, u32[]{:S(2)}) collective-permute-start(bf16[128,768]{1,0:T(8,128)(2,1)} %bitcast.12), channel_id=1, source_target_pairs={{0,2},{1,3},{4,6},{5,7},{8,10},{9,11},{12,14},{13,15},{16,18},{17,... | collective-permute-start | bytes 589832 | tf_op jit(solution)/shard_map/ppermute | solution.py:155
  13.0 8.2 %collective-permute-start.2 = (bf16[128,768]{1,0:T(8,128)(2,1)}, bf16[128,768]{1,0:T(8,128)(2,1)S(1)}, u32[]{:S(2)}, u32[]{:S(2)}) collective-permute-start(bf16[128,768]{1,0:T(8,128)(2,1)} %bitcast.13), channel_id=1, source_target_pairs={{0,1},{1,2},{2,3},{4,5},{5,6},{6,7},{8,9},{9,10},{10,11},{12,13},{... | collective-permute-start | bytes 589832 | tf_op jit(solution)/shard_map/ppermute | solution.py:155
  16.2 12.1 %all-to-all-start = ((f32[32,1,128]{2,1,0:T(1,128)}), f32[32,1,128]{2,1,0:T(1,128)S(1)}, u32[]{:S(2)}, u32[]{:S(2)}) async-start(f32[32,1,128]{2,1,0:T(1,128)} %get-tuple-element.10), calls=%async_computation | async-start | bytes 32768 | tf_op jit(solution)/shard_map/all_to_all | solution.py:178
  28.6 0.7 %copy-start.7 = (f32[6]{0:T(128)}, f32[6]{0:T(128)S(1)}, u32[]{:S(2)}) copy-start(f32[6]{0:T(128)S(1)} %sqrt.3) | copy-start | bytes 76

commit v3 on v2

--- a/solution.py
+++ b/solution.py
@@ -151,8 +151,7 @@
 
 def passed_along(x, by):
     shards = lax.axis_size("seq")
-    pairs = [(i, i + by) for i in range(shards - by)]
-    return lax.ppermute(x, "seq", pairs)
+    return lax.ppermute(x, "seq", [(i, (i + by) % shards) for i in range(shards)])
 
 
 def clip_factors(head_max):
@@ -170,10 +169,10 @@
     rank = lax.axis_index("seq").astype(jnp.int32).reshape(1)
     queries, keys, values = queries[0], keys[0], values[0]
 
-    earlier_keys = [passed_along(keys, d) for d in range(1, reach + 1)]
+    earlier_keys = [passed_along(keys, d) for d in range(reach, 0, -1)][::-1]
     own_max = own_maxima(rank, segments, queries, keys)
     sent_values, own_max = lax.optimization_barrier((values, own_max))
-    earlier_values = [passed_along(sent_values, d) for d in range(1, reach + 1)]
+    earlier_values = [passed_along(sent_values, d) for d in range(reach, 0, -1)][::-1]
     row_max, head_max = row_maxima(rank, segments, queries, own_max, earlier_keys, devices)
     everyone = lax.all_to_all(head_max, ("dp", "seq"), 0, 0)
     attended = mix(

time: 29.6 us -> 27.3 us (0.922)
  starting transfers between devices: 14.5 us -> 11.3 us
  waiting for transfers between devices: 3.05 us -> 4.09 us
    ppermute x4, starting transfers between devices: 9.54 us -> 4.92 us  [passed_along(): lax.ppermute(x, 'seq', [(i, (i + by) % shards) for i in range(shards)])]
    all_to_all x1, starting transfers between devices: 4.92 us -> 6.36 us  [local(): everyone = lax.all_to_all(head_max, ('dp', 'seq'), 0, 0)]
    ppermute x4, waiting for transfers between devices: 0.01 us -> 1.04 us  [passed_along(): lax.ppermute(x, 'seq', [(i, (i + by) % shards) for i in range(shards)])]
  transfers between devices with their start and end apart: 5 -> 5, of which waited for: 1 -> 2; matrix products, arithmetic and copies ran while one was open for 0% -> 0% of each run, Pallas kernels for 24% -> 26%
where the time goes in v3:
time: 27.3 us; the launch traced here: 27.1 us
  starting transfers between devices  11.3 us (41%)
  Pallas kernels  7 us (26%)
  waiting for transfers between devices  4.09 us (15%)
  local copies, waits for them, and re-layouts  3.28 us (12%)
  other arithmetic  0.71 us (3%)
  between operations  0.71 us (3%)
    pallas_call x3, Pallas kernels, call(): pl.pallas_call(kernel, out_shape=out_shape, in_specs=[pl.BlockSpec(memory...  7 us
    all_to_all x1, starting transfers between devices, local(): everyone = lax.all_to_all(head_max, ('dp', 'seq'), 0, 0)  6.36 us
    ppermute x4, starting transfers between devices, passed_along(): lax.ppermute(x, 'seq', [(i, (i + by) % shards) for i in range(shards)])  4.92 us
    all_to_all x1, waiting for transfers between devices, local(): everyone = lax.all_to_all(head_max, ('dp', 'seq'), 0, 0)  3.05 us
    unnamed x16, local copies, waits for them, and re-layouts  3.04 us
    ppermute x4, waiting for transfers between devices, passed_along(): lax.ppermute(x, 'seq', [(i, (i + by) % shards) for i in range(shards)])  1.04 us
  transfers between devices with their start and end apart: 5, of which 2 were waited for; matrix products, arithmetic and copies ran while one was open for 0% of the time, Pallas kernels for 26%

profile of v3, /device:TPU:0, one launch (start us, length us, event | category | flops | bytes accessed | tf_op | source)
XLA Modules:
  0.0 27.1 jit_solution(1240431246755366504)
XLA Ops:
  0.6 3.0 %collective-permute-start.1 = (bf16[128,768]{1,0:T(8,128)(2,1)}, bf16[128,768]{1,0:T(8,128)(2,1)S(1)}, u32[]{:S(2)}, u32[]{:S(2)}) collective-permute-start(bf16[128,768]{1,0:T(8,128)(2,1)} %bitcast.8), channel_id=1, source_target_pairs={{0,2},{1,3},{2,0},{3,1},{4,6},{5,7},{6,4},{7,5},{8,10},{9,11},{10,... | collective-permute-start | bytes 589832 | tf_op jit(solution)/shard_map/ppermute | solution.py:154
  3.6 0.0 collective-permute-start
  3.6 0.0 copy-start
  3.6 1.4 %copy-done = bf16[1,128,6144]{2,1,0:T(8,128)(2,1)S(1)} copy-done((bf16[1,128,6144]{2,1,0:T(8,128)(2,1)S(1)}, bf16[1,128,6144]{2,1,0:T(8,128)(2,1)}, u32[]{:S(2)}) %copy-start) | copy-done | bytes 1572888
  5.0 0.0 copy-start.2
  5.0 0.9 %copy-done.2 = bf16[1,128,768]{2,1,0:T(8,128)(2,1)S(1)} copy-done((bf16[1,128,768]{2,1,0:T(8,128)(2,1)S(1)}, bf16[1,128,768]{2,1,0:T(8,128)(2,1)}, u32[]{:S(2)}) %copy-start.2) | copy-done | bytes 196632
  6.0 0.0 copy-start.4
  6.0 0.7 %copy-done.4 = s32[1,512]{1,0:T(1,128)S(1)} copy-done((s32[1,512]{1,0:T(1,128)S(1)}, s32[1,512]{1,0:T(1,128)}, u32[]{:S(2)}) %copy-start.4) | copy-done | bytes 2072
  6.7 0.0 copy-start.1
  6.7 0.0 copy-start.3
  6.7 0.0 copy-start.5
  6.7 0.0 copy-start.6
  6.7 1.2 %own_maxima.1.own_max_ref = f32[48,128]{1,0:T(8,128)S(1)} custom-call(s32[1]{0:T(128)} %bitcast.rank_ref, s32[1,512]{1,0:T(1,128)S(1)} %copy-done.4, bf16[128,6144]{1,0:T(8,128)(2,1)S(1)} %bitcast.5, bf16[128,768]{1,0:T(8,128)(2,1)S(1)} %bitcast.10), custom_call_target="tpu_custom_call" | custom-call | flops 201326592 | bytes 1572864 | tf_op jit(solution)/shard_map/own_maxima/pallas_call | solution.py:108
  7.9 0.1 collective-permute-start.3
  8.0 1.8 %collective-permute-start.2 = (bf16[128,768]{1,0:T(8,128)(2,1)}, bf16[128,768]{1,0:T(8,128)(2,1)S(1)}, u32[]{:S(2)}, u32[]{:S(2)}) collective-permute-start(bf16[128,768]{1,0:T(8,128)(2,1)} %bitcast.13), channel_id=1, source_target_pairs={{0,1},{1,2},{2,3},{3,0},{4,5},{5,6},{6,7},{7,4},{8,9},{9,10},{10,1... | collective-permute-start | bytes 589832 | tf_op jit(solution)/shard_map/ppermute | solution.py:154
  9.8 0.0 collective-permute-done.1.refs_1_.refs_2_
  9.8 1.0 %collective-permute-done.refs_0_.refs_1_ = bf16[128,768]{1,0:T(8,128)(2,1)S(1)} collective-permute-done((bf16[128,768]{1,0:T(8,128)(2,1)}, bf16[128,768]{1,0:T(8,128)(2,1)S(1)}, u32[]{:S(2)}, u32[]{:S(2)}) %collective-permute-start) | collective-permute-done | bytes 196640 | tf_op jit(solution)/shard_map/ppermute | solution.py:154
  10.9 1.7 %row_maxima.1 = (f32[48,128]{1,0:T(8,128)S(1)}, f32[32,1,128]{2,1,0:T(1,128)}) custom-call(s32[1]{0:T(128)} %bitcast.rank_ref, s32[1,512]{1,0:T(1,128)S(1)} %copy-done.4, bf16[128,6144]{1,0:T(8,128)(2,1)S(1)} %bitcast.6, f32[48,128]{1,0:T(8,128)S(1)} %own_maxima.1.own_max_ref, bf16[128,768]{1,0:T(8,128)(2,1)S(1)} %collective-permute-done.refs_0_.refs_1_, ...), custom_call_target="tpu_custom_call" | custom-call | flops 402653184 | bytes 1572864 | tf_op jit(solution)/shard_map/row_maxima/pallas_call | solution.py:108
  12.6 6.4 %all-to-all-start = ((f32[32,1,128]{2,1,0:T(1,128)}), f32[32,1,128]{2,1,0:T(1,128)S(1)}, u32[]{:S(2)}, u32[]{:S(2)}) async-start(f32[32,1,128]{2,1,0:T(1,128)} %get-tuple-element.10), calls=%async_computation | async-start | bytes 32768 | tf_op jit(solution)/shard_map/all_to_all | solution.py:177
  19.0 0.0 collective-permute-done.3.refs_5_
  19.0 0.0 collective-permute-done.2.refs_4_
  19.0 0.0 copy-done.1
  19.0 0.0 copy-done.3
  19.0 0.0 copy-done.5
  19.0 0.0 copy-done.6
  19.0 4.0 %mix.1 = bf16[128,6144]{1,0:T(8,128)(2,1)} custom-call(s32[1]{0:T(128)} %bitcast.rank_ref, s32[1,512]{1,0:T(1,128)S(1)} %copy-done.5, bf16[128,6144]{1,0:T(8,128)(2,1)S(1)} %bitcast.7, f32[48,128]{1,0:T(8,128)S(1)} %get-tuple-element.8.row_max_ref, bf16[128,768]{1,0:T(8,128)(2,1)S(1)} %bitcast.11, bf16[128,768]{1,0:T(8,128)(2,1)S(1)} %collective-permute-done.refs_0_.refs_1_, ...), custom_call_target="tpu_custom_call" | custom-call | flops 1207959552 | bytes 3145728 | tf_op jit(solution)/shard_map/mix/pallas_call | solution.py:108
  23.1 3.0 %all-to-all-done = f32[32,1,128]{2,1,0:T(1,128)S(1)} async-done(((f32[32,1,128]{2,1,0:T(1,128)}), f32[32,1,128]{2,1,0:T(1,128)S(1)}, u32[]{:S(2)}, u32[]{:S(2)}) %all-to-all-start) | async-done | bytes 16416 | tf_op jit(solution)/shard_map/all_to_all | solution.py:177
  26.1 0.1 slice_reduce_fusion
  26.2 0.1 div.11
  26.2 0.1 reduce_min.9
  26.4 0.0 copy-start.7
  26.4 0.1 broadcast_in_dim.7
  26.5 0.1 reshape.19
  26.5 0.5 %multiply_divide_fusion = f32[48]{0:T(128)} fusion(f32[48]{0:T(128)S(1)} %reshape.19, f32[48]{0:T(128)S(1)} %slice_reduce_fusion), kind=kLoop, calls=%fused_computation.1 | loop fusion | flops 144 | bytes 576 | tf_op jit(solution)/shard_map/div | solution.py:160
  27.1 0.0 copy-done.7
  (2 shorter events, 0.0 us)
Async XLA Ops:
  0.6 9.2 %collective-permute-start.1 = (bf16[128,768]{1,0:T(8,128)(2,1)}, bf16[128,768]{1,0:T(8,128)(2,1)S(1)}, u32[]{:S(2)}, u32[]{:S(2)}) collective-permute-start(bf16[128,768]{1,0:T(8,128)(2,1)} %bitcast.8), channel_id=1, source_target_pairs={{0,2},{1,3},{2,0},{3,1},{4,6},{5,7},{6,4},{7,5},{8,10},{9,11},{10,... | collective-permute-start | bytes 589832 | tf_op jit(solution)/shard_map/ppermute | solution.py:154
  3.6 7.2 %collective-permute-start = (bf16[128,768]{1,0:T(8,128)(2,1)}, bf16[128,768]{1,0:T(8,128)(2,1)S(1)}, u32[]{:S(2)}, u32[]{:S(2)}) collective-permute-start(bf16[128,768]{1,0:T(8,128)(2,1)} %bitcast.9), channel_id=1, source_target_pairs={{0,1},{1,2},{2,3},{3,0},{4,5},{5,6},{6,7},{7,4},{8,9},{9,10},{10,1... | collective-permute-start | bytes 589832 | tf_op jit(solution)/shard_map/ppermute | solution.py:154
  3.6 1.4 %copy-start = (bf16[1,128,6144]{2,1,0:T(8,128)(2,1)S(1)}, bf16[1,128,6144]{2,1,0:T(8,128)(2,1)}, u32[]{:S(2)}) copy-start(bf16[1,128,6144]{2,1,0:T(8,128)(2,1)} %param.4) | copy-start | bytes 4718596
  5.0 0.9 %copy-start.2 = (bf16[1,128,768]{2,1,0:T(8,128)(2,1)S(1)}, bf16[1,128,768]{2,1,0:T(8,128)(2,1)}, u32[]{:S(2)}) copy-start(bf16[1,128,768]{2,1,0:T(8,128)(2,1)} %param.5) | copy-start | bytes 589828
  6.0 0.7 %copy-start.4 = (s32[1,512]{1,0:T(1,128)S(1)}, s32[1,512]{1,0:T(1,128)}, u32[]{:S(2)}) copy-start(s32[1,512]{1,0:T(1,128)} %seg_ref.5) | copy-start | bytes 6148
  6.7 12.3 %copy-start.1 = (bf16[1,128,6144]{2,1,0:T(8,128)(2,1)S(1)}, bf16[1,128,6144]{2,1,0:T(8,128)(2,1)}, u32[]{:S(2)}) copy-start(bf16[1,128,6144]{2,1,0:T(8,128)(2,1)} %param.4) | copy-start | bytes 4718596
  6.7 12.3 %copy-start.3 = (bf16[1,128,768]{2,1,0:T(8,128)(2,1)S(1)}, bf16[1,128,768]{2,1,0:T(8,128)(2,1)}, u32[]{:S(2)}) copy-start(bf16[1,128,768]{2,1,0:T(8,128)(2,1)} %param.5) | copy-start | bytes 589828
  6.7 12.3 %copy-start.5 = (s32[1,512]{1,0:T(1,128)S(1)}, s32[1,512]{1,0:T(1,128)}, u32[]{:S(2)}) copy-start(s32[1,512]{1,0:T(1,128)} %seg_ref.5) | copy-start | bytes 6148
  6.7 12.3 %copy-start.6 = (bf16[1,128,768]{2,1,0:T(8,128)(2,1)S(1)}, bf16[1,128,768]{2,1,0:T(8,128)(2,1)}, u32[]{:S(2)}) copy-start(bf16[1,128,768]{2,1,0:T(8,128)(2,1)} %param.6) | copy-start | bytes 589828
  7.9 11.1 %collective-permute-start.3 = (bf16[128,768]{1,0:T(8,128)(2,1)}, bf16[128,768]{1,0:T(8,128)(2,1)S(1)}, u32[]{:S(2)}, u32[]{:S(2)}) collective-permute-start(bf16[128,768]{1,0:T(8,128)(2,1)} %bitcast.12), channel_id=1, source_target_pairs={{0,2},{1,3},{2,0},{3,1},{4,6},{5,7},{6,4},{7,5},{8,10},{9,11},{10,... | collective-permute-start | bytes 589832 | tf_op jit(solution)/shard_map/ppermute | solution.py:154
  8.0 10.9 %collective-permute-start.2 = (bf16[128,768]{1,0:T(8,128)(2,1)}, bf16[128,768]{1,0:T(8,128)(2,1)S(1)}, u32[]{:S(2)}, u32[]{:S(2)}) collective-permute-start(bf16[128,768]{1,0:T(8,128)(2,1)} %bitcast.13), channel_id=1, source_target_pairs={{0,1},{1,2},{2,3},{3,0},{4,5},{5,6},{6,7},{7,4},{8,9},{9,10},{10,1... | collective-permute-start | bytes 589832 | tf_op jit(solution)/shard_map/ppermute | solution.py:154
  12.6 13.5 %all-to-all-start = ((f32[32,1,128]{2,1,0:T(1,128)}), f32[32,1,128]{2,1,0:T(1,128)S(1)}, u32[]{:S(2)}, u32[]{:S(2)}) async-start(f32[32,1,128]{2,1,0:T(1,128)} %get-tuple-element.10), calls=%async_computation | async-start | bytes 32768 | tf_op jit(solution)/shard_map/all_to_all | solution.py:177
  26.4 0.7 %copy-start.7 = (f32[6]{0:T(128)}, f32[6]{0:T(128)S(1)}, u32[]{:S(2)}) copy-start(f32[6]{0:T(128)S(1)} %sqrt.3) | copy-start | bytes 76

commit v4 on v3

v4 whole, which is shorter than its diff:
```python
import functools
import math

import jax
import jax.numpy as jnp
from jax import lax
from jax.experimental import pallas as pl
from jax.experimental.pallas import tpu as pltpu
from jax.sharding import PartitionSpec as P

QUERY_HEADS = 48
KEY_VALUE_HEADS = 6
HEAD_SIZE = 128
DOCUMENT_LIMIT = 384
GROUP = QUERY_HEADS // KEY_VALUE_HEADS

clip_level = 6.0
SCALE = HEAD_SIZE ** (-0.5)
SCALE_2 = SCALE * math.log2(math.e)
MASKED = -1e30
NT = (((1,), (1,)), ((), ()))


def reach_of(rows, length, shards):
    reach = (DOCUMENT_LIMIT - 1 + rows - 1) // rows
    documents = length // 256
    least = length - (documents - 1) * DOCUMENT_LIMIT
    if shards == reach + 1 and documents > 1 and least >= rows:
        reach -= 1
    return reach


def fill_bias(seg_ref, bias_ref, rank, reach, rows):
    own = seg_ref[:, pl.ds(pl.multiple_of(rank * rows, rows), rows)]
    query_doc = jnp.broadcast_to(own, (rows, rows))
    key_index = lax.broadcasted_iota(jnp.int32, (rows, rows), 0)
    query_index = lax.broadcasted_iota(jnp.int32, (rows, rows), 1)
    for distance in range(reach + 1):
        block = jnp.maximum(rank - distance, 0)
        docs = seg_ref[:, pl.ds(pl.multiple_of(block * rows, rows), rows)]
        key_doc = jnp.broadcast_to(docs, (rows, rows)).T
        valid = key_doc == query_doc
        if distance == 0:
            valid = valid & (key_index <= query_index)
        else:
            valid = valid & (rank >= distance)
        bias_ref[distance * rows : (distance + 1) * rows, :] = jnp.where(valid, 0.0, MASKED)


def block_maxima(q_ref, key_ref, bias_ref, distance, head):
    rows = q_ref.shape[0]
    column = head // GROUP
    keys = key_ref[:, column * HEAD_SIZE : (column + 1) * HEAD_SIZE]
    q = [q_ref[:, h * HEAD_SIZE : (h + 1) * HEAD_SIZE] for h in (head, head + 1)]
    logits = lax.dot_general(
        keys, jnp.concatenate(q, axis=0), NT, preferred_element_type=jnp.float32
    )
    bias = bias_ref[distance * rows : (distance + 1) * rows, :]
    return [
        jnp.max(logits[:, i * rows : (i + 1) * rows] + bias, axis=0, keepdims=True)
        for i in range(2)
    ]


def own_max_kernel(reach, rank_ref, seg_ref, q_ref, key_ref, own_max_ref, bias_ref):
    fill_bias(seg_ref, bias_ref, rank_ref[0], reach, q_ref.shape[0])
    for head in range(0, QUERY_HEADS, 2):
        first, second = block_maxima(q_ref, key_ref, bias_ref, 0, head)
        own_max_ref[head : head + 1, :] = first
        own_max_ref[head + 1 : head + 2, :] = second


def next_max_kernel(distance, bias_ref, q_ref, max_ref, key_ref, row_max_ref, *head_max_refs):
    rows = q_ref.shape[0]
    for head in range(0, QUERY_HEADS, 2):
        for i, largest in enumerate(block_maxima(q_ref, key_ref, bias_ref, distance, head)):
            at = slice(head + i, head + i + 1)
            row_max_ref[at, :] = jnp.maximum(max_ref[at, :], largest)
    for head_max_ref in head_max_refs:
        largest = row_max_ref[...]
        padded = jnp.concatenate([largest, largest, largest], axis=0)[:rows]
        head_max = jnp.max(padded.T, axis=0, keepdims=True) * SCALE
        head_max_ref[...] = jnp.broadcast_to(head_max[None], head_max_ref.shape)


def mix_kernel(reach, bias_ref, q_ref, row_max_ref, *refs):
    key_refs, value_refs, out_ref = refs[: reach + 1], refs[reach + 1 : 2 * reach + 2], refs[-1]
    for column in range(KEY_VALUE_HEADS):
        at = slice(column * HEAD_SIZE, (column + 1) * HEAD_SIZE)
        key_block = jnp.concatenate([k[:, at] for k in key_refs], axis=0)
        value_block = jnp.concatenate([v[:, at].T for v in value_refs], axis=1)
        for head in range(column * GROUP, (column + 1) * GROUP):
            here = slice(head * HEAD_SIZE, (head + 1) * HEAD_SIZE)
            logits = lax.dot_general(
                key_block, q_ref[:, here], NT, preferred_element_type=jnp.float32
            )
            largest = row_max_ref[head : head + 1, :] * SCALE_2
            expo = jnp.exp2((logits + bias_ref[...]) * SCALE_2 - largest)
            share = 1.0 / jnp.sum(expo, axis=0, keepdims=True)
            mixed = jnp.dot(
                value_block, expo.astype(jnp.bfloat16), preferred_element_type=jnp.float32
            )
            out_ref[:, here] = (mixed * share).astype(jnp.bfloat16).T


VMEM = pl.BlockSpec(memory_space=pltpu.VMEM)


def call(kernel, name, out_shape, blocks, rows, products, *arrays, scalars=0):
    pairs = QUERY_HEADS * rows * rows * blocks
    smem = pl.BlockSpec(memory_space=pltpu.SMEM)
    return pl.pallas_call(
        kernel,
        out_shape=out_shape,
        in_specs=[smem] * scalars + [VMEM] * (len(arrays) - scalars),
        out_specs=(VMEM,) * len(out_shape),
        compiler_params=pltpu.CompilerParams(vmem_limit_bytes=24 << 20),
        cost_estimate=pl.CostEstimate(
            flops=2 * products * HEAD_SIZE * pairs,
            bytes_accessed=2 * QUERY_HEADS * HEAD_SIZE * rows * products,
            transcendentals=(products - 1) * pairs,
        ),
        name=name,
    )(*arrays)


def own_maxima(rank, segments, queries, keys, reach):
    rows = queries.shape[0]
    out_shape = (
        jax.ShapeDtypeStruct((QUERY_HEADS, rows), jnp.float32),
        jax.ShapeDtypeStruct(((reach + 1) * rows, rows), jnp.float32),
    )
    kernel = functools.partial(own_max_kernel, reach)
    return call(
        kernel, "own_maxima", out_shape, 1, rows, 1, rank, segments, queries, keys, scalars=1
    )


def next_maxima(distance, bias, queries, row_max, keys, devices):
    rows = queries.shape[0]
    out_shape = (jax.ShapeDtypeStruct((QUERY_HEADS, rows), jnp.float32),)
    if devices:
        out_shape += (jax.ShapeDtypeStruct((devices, 1, rows), jnp.float32),)
    kernel = functools.partial(next_max_kernel, distance)
    name = f"maxima_{distance}"
    return call(kernel, name, out_shape, 1, rows, 1, bias, queries, row_max, keys)


def mix(bias, queries, row_max, key_blocks, value_blocks):
    reach, rows = len(key_blocks) - 1, queries.shape[0]
    out_shape = (jax.ShapeDtypeStruct(queries.shape, jnp.bfloat16),)
    kernel = functools.partial(mix_kernel, reach)
    arrays = (bias, queries, row_max, *key_blocks, *value_blocks)
    return call(kernel, "mix", out_shape, reach + 1, rows, 2, *arrays)[0]


def passed_along(x, by):
    shards = lax.axis_size("seq")
    return lax.ppermute(x, "seq", [(i, (i + by) % shards) for i in range(shards)])


def clip_factors(head_max):
    clipped_logits = clip_level / jnp.maximum(head_max, clip_level)
    key_head_factor = jnp.sqrt(jnp.min(clipped_logits.reshape(KEY_VALUE_HEADS, GROUP), axis=1))
    query_factor = clipped_logits / jnp.repeat(key_head_factor, GROUP)
    return (query_factor, key_head_factor)


def local(queries, keys, values, segments):
    rows, length = queries.shape[1], segments.shape[1]
    shards = lax.axis_size("seq")
    devices = lax.axis_size("dp") * shards
    reach = reach_of(rows, length, shards)
    rank = lax.axis_index("seq").astype(jnp.int32).reshape(1)
    queries, keys, values = queries[0], keys[0], values[0]

    distances = range(reach, 0, -1)
    key_blocks = {d: passed_along(keys, d) for d in distances}
    row_max, bias = own_maxima(rank, segments, queries, keys, reach)
    value_blocks = {}
    for d in distances:
        if d == 1:
            sent_values, row_max = lax.optimization_barrier((values, row_max))
            value_blocks = {d: passed_along(sent_values, d) for d in distances}
        row_max, *head_max = next_maxima(
            d, bias, queries, row_max, key_blocks[d], devices if d == 1 else 0
        )
    everyone = lax.all_to_all(head_max[0], ("dp", "seq"), 0, 0)
    attended = mix(
        bias,
        queries,
        row_max,
        [keys] + [key_blocks[d] for d in range(1, reach + 1)],
        [values] + [value_blocks[d] for d in range(1, reach + 1)],
    )
    query_factor, key_head_factor = clip_factors(
        jnp.max(everyone[:, 0, :QUERY_HEADS], axis=0)
    )
    return (attended[None], query_factor, key_head_factor)


def solution(mesh):
    in_specs = (P("dp", "seq", None), P("dp", "seq", None), P("dp", "seq", None), P("dp", None))
    out_specs = (P("dp", "seq", None), P(), P())
    return jax.shard_map(local, mesh=mesh, in_specs=in_specs, out_specs=out_specs, check_vma=False)
```

time: 27.3 us -> 31.9 us (1.17)
  waiting for transfers between devices: 4.09 us -> 9.58 us
  Pallas kernels: 7 us -> 6.5 us
  starting transfers between devices: 11.3 us -> 10.9 us
    ppermute x4, waiting for transfers between devices: 1.04 us -> 4.35 us  [passed_along(): lax.ppermute(x, 'seq', [(i, (i + by) % shards) for i in range(shards)])]
    all_to_all x1, waiting for transfers between devices: 3.05 us -> 5.23 us  [local(): everyone = lax.all_to_all(head_max[0], ('dp', 'seq'), 0, 0)]
    pallas_call x3 -> x4, Pallas kernels: 7 us -> 6.5 us  [call(): pl.pallas_call(kernel, out_shape=out_shape, in_specs=[smem] * scalars + [...]
    unnamed x16 -> x14, local copies, waits for them, and re-layouts: 3.04 us -> 3.03 us
  transfers between devices with their start and end apart: 5 -> 5, of which waited for: 2 -> 4; matrix products, arithmetic and copies ran while one was open for 0% -> 3% of each run, Pallas kernels for 26% -> 4%
where the time goes in v4:
time: 31.9 us; the launch traced here: 31.7 us
  starting transfers between devices  10.9 us (34%)
  waiting for transfers between devices  9.58 us (30%)
  Pallas kernels  6.5 us (20%)
  local copies, waits for them, and re-layouts  3.27 us (10%)
  other arithmetic  0.71 us (2%)
  between operations  0.69 us (2%)
    pallas_call x4, Pallas kernels, call(): pl.pallas_call(kernel, out_shape=out_shape, in_specs=[smem] * scalars + [...  6.5 us
    all_to_all x1, starting transfers between devices, local(): everyone = lax.all_to_all(head_max[0], ('dp', 'seq'), 0, 0)  6.1 us
    all_to_all x1, waiting for transfers between devices, local(): everyone = lax.all_to_all(head_max[0], ('dp', 'seq'), 0, 0)  5.23 us
    ppermute x4, starting transfers between devices, passed_along(): lax.ppermute(x, 'seq', [(i, (i + by) % shards) for i in range(shards)])  4.84 us
    ppermute x4, waiting for transfers between devices, passed_along(): lax.ppermute(x, 'seq', [(i, (i + by) % shards) for i in range(shards)])  4.35 us
    unnamed x14, local copies, waits for them, and re-layouts  3.03 us
  transfers between devices with their start and end apart: 5, of which 4 were waited for; matrix products, arithmetic and copies ran while one was open for 3% of the time, Pallas kernels for 4%

profile of v4, /device:TPU:0, one launch (start us, length us, event | category | flops | bytes accessed | tf_op | source)
XLA Modules:
  0.0 31.7 jit_solution(6447373654470973810)
XLA Ops:
  0.6 3.0 %collective-permute-start = (bf16[128,768]{1,0:T(8,128)(2,1)}, bf16[128,768]{1,0:T(8,128)(2,1)S(1)}, u32[]{:S(2)}, u32[]{:S(2)}) collective-permute-start(bf16[128,768]{1,0:T(8,128)(2,1)} %bitcast.9), channel_id=1, source_target_pairs={{0,2},{1,3},{2,0},{3,1},{4,6},{5,7},{6,4},{7,5},{8,10},{9,11},{10,... | collective-permute-start | bytes 589832 | tf_op jit(solution)/shard_map/ppermute | solution.py:159
  3.6 0.0 collective-permute-start.1
  3.6 0.0 copy-start
  3.6 1.4 %copy-done = bf16[1,128,6144]{2,1,0:T(8,128)(2,1)S(1)} copy-done((bf16[1,128,6144]{2,1,0:T(8,128)(2,1)S(1)}, bf16[1,128,6144]{2,1,0:T(8,128)(2,1)}, u32[]{:S(2)}) %copy-start) | copy-done | bytes 1572888
  5.0 0.0 copy-start.2
  5.0 0.9 %copy-done.2 = bf16[1,128,768]{2,1,0:T(8,128)(2,1)S(1)} copy-done((bf16[1,128,768]{2,1,0:T(8,128)(2,1)S(1)}, bf16[1,128,768]{2,1,0:T(8,128)(2,1)}, u32[]{:S(2)}) %copy-start.2) | copy-done | bytes 196632
  6.0 0.0 copy-start.5
  6.0 0.7 %copy-done.5 = s32[1,512]{1,0:T(1,128)S(1)} copy-done((s32[1,512]{1,0:T(1,128)S(1)}, s32[1,512]{1,0:T(1,128)}, u32[]{:S(2)}) %copy-start.5) | copy-done | bytes 2072
  6.7 0.0 copy-start.1
  6.7 0.6 %own_maxima.1 = (f32[48,128]{1,0:T(8,128)S(1)}, f32[384,128]{1,0:T(8,128)S(1)}) custom-call(s32[1]{0:T(128)} %bitcast.rank_ref, s32[1,512]{1,0:T(1,128)S(1)} %copy-done.5, bf16[128,6144]{1,0:T(8,128)(2,1)S(1)} %bitcast.5, bf16[128,768]{1,0:T(8,128)(2,1)S(1)} %bitcast.11), custom_call_target="tpu_custom_call" | custom-call | flops 201326592 | bytes 1572864 | tf_op jit(solution)/shard_map/own_maxima/pallas_call | solution.py:112
  7.3 2.3 %collective-permute-done.key_ref.refs_2_ = bf16[128,768]{1,0:T(8,128)(2,1)S(1)} collective-permute-done((bf16[128,768]{1,0:T(8,128)(2,1)}, bf16[128,768]{1,0:T(8,128)(2,1)S(1)}, u32[]{:S(2)}, u32[]{:S(2)}) %collective-permute-start) | collective-permute-done | bytes 196640 | tf_op jit(solution)/shard_map/ppermute | solution.py:159
  9.6 0.0 copy-done.1
  9.6 0.0 copy-start.4
  9.6 0.0 copy-start.3
  9.6 0.6 %maxima_2.1.max_ref = f32[48,128]{1,0:T(8,128)S(1)} custom-call(f32[384,128]{1,0:T(8,128)S(1)} %get-tuple-element.9.bias_ref, bf16[128,6144]{1,0:T(8,128)(2,1)S(1)} %bitcast.6, f32[48,128]{1,0:T(8,128)S(1)} %get-tuple-element.10.max_ref, bf16[128,768]{1,0:T(8,128)(2,1)S(1)} %collective-permute-done.key_ref.refs_2_), custom_call_target="tpu_custom_call" | custom-call | flops 201326592 | bytes 1572864 | tf_op jit(solution)/shard_map/maxima_2/pallas_call | solution.py:112
  10.2 0.7 %collective-permute-done.1.key_ref.refs_1_ = bf16[128,768]{1,0:T(8,128)(2,1)S(1)} collective-permute-done((bf16[128,768]{1,0:T(8,128)(2,1)}, bf16[128,768]{1,0:T(8,128)(2,1)S(1)}, u32[]{:S(2)}, u32[]{:S(2)}) %collective-permute-start.1) | collective-permute-done | bytes 196640 | tf_op jit(solution)/shard_map/ppermute | solution.py:159
  10.9 1.3 %maxima_1.1 = (f32[48,128]{1,0:T(8,128)S(1)}, f32[32,1,128]{2,1,0:T(1,128)}) custom-call(f32[384,128]{1,0:T(8,128)S(1)} %get-tuple-element.9.bias_ref, bf16[128,6144]{1,0:T(8,128)(2,1)S(1)} %bitcast.7, f32[48,128]{1,0:T(8,128)S(1)} %maxima_2.1.max_ref, bf16[128,768]{1,0:T(8,128)(2,1)S(1)} %collective-permute-done.1.key_ref.refs_1_), custom_call_target="tpu_custom_call" | custom-call | flops 201326592 | bytes 1572864 | tf_op jit(solution)/shard_map/maxima_1/pallas_call | solution.py:112
  12.2 6.1 %all-to-all-start = ((f32[32,1,128]{2,1,0:T(1,128)}), f32[32,1,128]{2,1,0:T(1,128)S(1)}, u32[]{:S(2)}, u32[]{:S(2)}) async-start(f32[32,1,128]{2,1,0:T(1,128)} %get-tuple-element.14), calls=%async_computation | async-start | bytes 32768 | tf_op jit(solution)/shard_map/all_to_all | solution.py:188
  18.3 0.0 copy-done.4
  18.3 1.8 %collective-permute-start.3 = (bf16[128,768]{1,0:T(8,128)(2,1)S(1)}, bf16[128,768]{1,0:T(8,128)(2,1)S(1)}, u32[]{:S(2)}, u32[]{:S(2)}) collective-permute-start(bf16[128,768]{1,0:T(8,128)(2,1)S(1)} %bitcast.13), channel_id=1, source_target_pairs={{0,2},{1,3},{2,0},{3,1},{4,6},{5,7},{6,4},{7,5},{8,10},{9,11},{10,... | collective-permute-start | bytes 589832 | tf_op jit(solution)/shard_map/ppermute | solution.py:159
  20.1 0.0 collective-permute-start.2
  20.1 5.2 %all-to-all-done = f32[32,1,128]{2,1,0:T(1,128)S(1)} async-done(((f32[32,1,128]{2,1,0:T(1,128)}), f32[32,1,128]{2,1,0:T(1,128)S(1)}, u32[]{:S(2)}, u32[]{:S(2)}) %all-to-all-start) | async-done | bytes 16416 | tf_op jit(solution)/shard_map/all_to_all | solution.py:188
  25.3 0.1 slice_reduce_fusion
  25.4 0.1 div.11
  25.5 0.1 reduce_min.9
  25.6 0.0 copy-start.6
  25.6 0.1 broadcast_in_dim.7
  25.7 0.1 reshape.19
  25.8 0.5 %multiply_divide_fusion = f32[48]{0:T(128)} fusion(f32[48]{0:T(128)S(1)} %reshape.19, f32[48]{0:T(128)S(1)} %slice_reduce_fusion), kind=kLoop, calls=%fused_computation.1 | loop fusion | flops 144 | bytes 576 | tf_op jit(solution)/shard_map/div | solution.py:165
  26.3 0.0 collective-permute-done.3.refs_5_
  26.3 1.3 %collective-permute-done.2.refs_4_ = bf16[128,768]{1,0:T(8,128)(2,1)S(1)} collective-permute-done((bf16[128,768]{1,0:T(8,128)(2,1)S(1)}, bf16[128,768]{1,0:T(8,128)(2,1)S(1)}, u32[]{:S(2)}, u32[]{:S(2)}) %collective-permute-start.2) | collective-permute-done | bytes 196640 | tf_op jit(solution)/shard_map/ppermute | solution.py:159
  27.7 0.0 copy-done.3
  27.7 4.0 %mix.1 = bf16[128,6144]{1,0:T(8,128)(2,1)} custom-call(f32[384,128]{1,0:T(8,128)S(1)} %get-tuple-element.9.bias_ref, bf16[128,6144]{1,0:T(8,128)(2,1)S(1)} %bitcast.8, f32[48,128]{1,0:T(8,128)S(1)} %get-tuple-element.12.row_max_ref, bf16[128,768]{1,0:T(8,128)(2,1)S(1)} %bitcast.12, bf16[128,768]{1,0:T(8,128)(2,1)S(1)} %collective-permute-done.1.key_ref.refs_1_, ...), custom_call_target="tpu_custom_call" | custom-call | flops 1207959552 | bytes 3145728 | tf_op jit(solution)/shard_map/mix/pallas_call | solution.py:112
  31.7 0.0 copy-done.6
  (2 shorter events, 0.0 us)
Async XLA Ops:
  0.6 8.9 %collective-permute-start = (bf16[128,768]{1,0:T(8,128)(2,1)}, bf16[128,768]{1,0:T(8,128)(2,1)S(1)}, u32[]{:S(2)}, u32[]{:S(2)}) collective-permute-start(bf16[128,768]{1,0:T(8,128)(2,1)} %bitcast.9), channel_id=1, source_target_pairs={{0,2},{1,3},{2,0},{3,1},{4,6},{5,7},{6,4},{7,5},{8,10},{9,11},{10,... | collective-permute-start | bytes 589832 | tf_op jit(solution)/shard_map/ppermute | solution.py:159
  3.6 7.2 %collective-permute-start.1 = (bf16[128,768]{1,0:T(8,128)(2,1)}, bf16[128,768]{1,0:T(8,128)(2,1)S(1)}, u32[]{:S(2)}, u32[]{:S(2)}) collective-permute-start(bf16[128,768]{1,0:T(8,128)(2,1)} %bitcast.10), channel_id=1, source_target_pairs={{0,1},{1,2},{2,3},{3,0},{4,5},{5,6},{6,7},{7,4},{8,9},{9,10},{10,1... | collective-permute-start | bytes 589832 | tf_op jit(solution)/shard_map/ppermute | solution.py:159
  3.6 1.4 %copy-start = (bf16[1,128,6144]{2,1,0:T(8,128)(2,1)S(1)}, bf16[1,128,6144]{2,1,0:T(8,128)(2,1)}, u32[]{:S(2)}) copy-start(bf16[1,128,6144]{2,1,0:T(8,128)(2,1)} %param.4) | copy-start | bytes 4718596
  5.0 0.9 %copy-start.2 = (bf16[1,128,768]{2,1,0:T(8,128)(2,1)S(1)}, bf16[1,128,768]{2,1,0:T(8,128)(2,1)}, u32[]{:S(2)}) copy-start(bf16[1,128,768]{2,1,0:T(8,128)(2,1)} %param.5) | copy-start | bytes 589828
  6.0 0.7 %copy-start.5 = (s32[1,512]{1,0:T(1,128)S(1)}, s32[1,512]{1,0:T(1,128)}, u32[]{:S(2)}) copy-start(s32[1,512]{1,0:T(1,128)} %seg_ref.1) | copy-start | bytes 6148
  6.7 2.9 %copy-start.1 = (bf16[1,128,6144]{2,1,0:T(8,128)(2,1)S(1)}, bf16[1,128,6144]{2,1,0:T(8,128)(2,1)}, u32[]{:S(2)}) copy-start(bf16[1,128,6144]{2,1,0:T(8,128)(2,1)} %param.4) | copy-start | bytes 4718596
  9.6 8.7 %copy-start.4 = (bf16[1,128,768]{2,1,0:T(8,128)(2,1)S(1)}, bf16[1,128,768]{2,1,0:T(8,128)(2,1)}, u32[]{:S(2)}) copy-start(bf16[1,128,768]{2,1,0:T(8,128)(2,1)} %param.6) | copy-start | bytes 589828
  9.6 18.1 %copy-start.3 = (bf16[1,128,768]{2,1,0:T(8,128)(2,1)S(1)}, bf16[1,128,768]{2,1,0:T(8,128)(2,1)}, u32[]{:S(2)}) copy-start(bf16[1,128,768]{2,1,0:T(8,128)(2,1)} %param.5) | copy-start | bytes 589828
  12.2 13.2 %all-to-all-start = ((f32[32,1,128]{2,1,0:T(1,128)}), f32[32,1,128]{2,1,0:T(1,128)S(1)}, u32[]{:S(2)}, u32[]{:S(2)}) async-start(f32[32,1,128]{2,1,0:T(1,128)} %get-tuple-element.14), calls=%async_computation | async-start | bytes 32768 | tf_op jit(solution)/shard_map/all_to_all | solution.py:188
  18.3 8.0 %collective-permute-start.3 = (bf16[128,768]{1,0:T(8,128)(2,1)S(1)}, bf16[128,768]{1,0:T(8,128)(2,1)S(1)}, u32[]{:S(2)}, u32[]{:S(2)}) collective-permute-start(bf16[128,768]{1,0:T(8,128)(2,1)S(1)} %bitcast.13), channel_id=1, source_target_pairs={{0,2},{1,3},{2,0},{3,1},{4,6},{5,7},{6,4},{7,5},{8,10},{9,11},{10,... | collective-permute-start | bytes 589832 | tf_op jit(solution)/shard_map/ppermute | solution.py:159
  20.1 7.5 %collective-permute-start.2 = (bf16[128,768]{1,0:T(8,128)(2,1)S(1)}, bf16[128,768]{1,0:T(8,128)(2,1)S(1)}, u32[]{:S(2)}, u32[]{:S(2)}) collective-permute-start(bf16[128,768]{1,0:T(8,128)(2,1)S(1)} %bitcast.14), channel_id=1, source_target_pairs={{0,1},{1,2},{2,3},{3,0},{4,5},{5,6},{6,7},{7,4},{8,9},{9,10},{10,1... | collective-permute-start | bytes 589832 | tf_op jit(solution)/shard_map/ppermute | solution.py:159
  25.6 6.1 %copy-start.6 = (f32[6]{0:T(128)}, f32[6]{0:T(128)S(1)}, u32[]{:S(2)}) copy-start(f32[6]{0:T(128)S(1)} %sqrt.3) | copy-start | bytes 76

commit v5 on v3

v5 whole, which is shorter than its diff:
```python
import functools
import math

import jax
import jax.numpy as jnp
from jax import lax
from jax.experimental import pallas as pl
from jax.experimental.pallas import tpu as pltpu
from jax.sharding import PartitionSpec as P

QUERY_HEADS = 48
KEY_VALUE_HEADS = 6
HEAD_SIZE = 128
DOCUMENT_LIMIT = 384
GROUP = QUERY_HEADS // KEY_VALUE_HEADS

clip_level = 6.0
SCALE = HEAD_SIZE ** (-0.5)
SCALE_2 = SCALE * math.log2(math.e)
MASKED = -1e30
NT = (((1,), (1,)), ((), ()))


def reach_of(rows, length, shards):
    reach = (DOCUMENT_LIMIT - 1 + rows - 1) // rows
    documents = length // 256
    least = length - (documents - 1) * DOCUMENT_LIMIT
    if shards == reach + 1 and documents > 1 and least >= rows:
        reach -= 1
    return reach


def fill_bias(seg_ref, bias_ref, rank, shards, pairs, rows):
    docs = {}
    for behind in sorted({b for pair in pairs for b in pair[:2]}):
        block = jnp.clip(rank - behind, 0, shards - 1)
        at = pl.ds(pl.multiple_of(block * rows, rows), rows)
        docs[behind] = jnp.broadcast_to(seg_ref[:, at], (rows, rows))
    key_index = lax.broadcasted_iota(jnp.int32, (rows, rows), 0)
    query_index = lax.broadcasted_iota(jnp.int32, (rows, rows), 1)
    for place, (query_behind, key_behind, parity) in enumerate(pairs):
        valid = docs[key_behind].T == docs[query_behind]
        if key_behind == query_behind:
            valid = valid & (key_index <= query_index)
        valid = valid & (rank >= key_behind)
        if parity is not None:
            valid = valid & (rank % 2 == parity)
        bias_ref[place * rows : (place + 1) * rows, :] = jnp.where(valid, 0.0, MASKED)


def raise_maxima(max_ref, q_ref, key_ref, bias_ref, place, floor_ref=None):
    rows = q_ref.shape[0]
    bias = bias_ref[place * rows : (place + 1) * rows, :]
    for head in range(0, QUERY_HEADS, 2):
        column = head // GROUP
        keys = key_ref[:, column * HEAD_SIZE : (column + 1) * HEAD_SIZE]
        q = [q_ref[:, h * HEAD_SIZE : (h + 1) * HEAD_SIZE] for h in (head, head + 1)]
        logits = lax.dot_general(
            keys, jnp.concatenate(q, axis=0), NT, preferred_element_type=jnp.float32
        )
        for i in range(2):
            at = slice(head + i, head + i + 1)
            largest = jnp.max(logits[:, i * rows : (i + 1) * rows] + bias, axis=0, keepdims=True)
            if floor_ref is not None:
                largest = jnp.maximum(floor_ref[at, :], largest)
            max_ref[at, :] = largest


def store_head_maxima(head_max_ref, max_ref):
    largest = max_ref[...]
    rows = largest.shape[1]
    padded = jnp.concatenate([largest, largest, largest], axis=0)[:rows]
    head_max = jnp.max(padded.T, axis=0, keepdims=True) * SCALE
    head_max_ref[...] = jnp.broadcast_to(head_max[None], head_max_ref.shape)


def first_kernel(
    shards, pairs, seg_hbm, q_hbm, key_hbm, max_ref, bias_ref, q_ref, key_ref, seg_ref, sems
):
    copies = [
        pltpu.make_async_copy(source, target, sems.at[i])
        for i, (source, target) in enumerate(
            ((seg_hbm, seg_ref), (key_hbm, key_ref), (q_hbm, q_ref))
        )
    ]
    for copy in copies:
        copy.start()
    copies[0].wait()
    fill_bias(seg_ref, bias_ref, lax.axis_index("seq"), shards, pairs, q_ref.shape[0])
    copies[1].wait()
    copies[2].wait()
    raise_maxima(max_ref, q_ref, key_ref, bias_ref, 0)


def next_kernel(place, bias_ref, q_ref, before_ref, key_ref, max_ref, *head_max_refs):
    raise_maxima(max_ref, q_ref, key_ref, bias_ref, place, before_ref)
    for head_max_ref in head_max_refs:
        store_head_maxima(head_max_ref, max_ref)


def last_paired_kernel(
    bias_ref, q_ref, partner_ref, before_ref, near_ref, key_ref, max_ref, head_max_ref, all_ref
):
    raise_maxima(max_ref, q_ref, key_ref, bias_ref, 2, before_ref)
    raise_maxima(all_ref, partner_ref, key_ref, bias_ref, 3, near_ref)
    all_ref[...] = jnp.maximum(all_ref[...], max_ref[...])
    store_head_maxima(head_max_ref, all_ref)


def mix_kernel(blocks, bias_ref, q_ref, row_max_ref, *refs):
    key_refs, value_refs, out_ref = refs[:blocks], refs[blocks:-1], refs[-1]
    for column in range(KEY_VALUE_HEADS):
        at = slice(column * HEAD_SIZE, (column + 1) * HEAD_SIZE)
        key_block = jnp.concatenate([k[:, at] for k in key_refs], axis=0)
        value_block = jnp.concatenate([v[:, at].T for v in value_refs], axis=1)
        for head in range(column * GROUP, (column + 1) * GROUP):
            here = slice(head * HEAD_SIZE, (head + 1) * HEAD_SIZE)
            logits = lax.dot_general(
                key_block, q_ref[:, here], NT, preferred_element_type=jnp.float32
            )
            largest = row_max_ref[head : head + 1, :] * SCALE_2
            expo = jnp.exp2((logits + bias_ref[: key_block.shape[0], :]) * SCALE_2 - largest)
            share = 1.0 / jnp.sum(expo, axis=0, keepdims=True)
            mixed = jnp.dot(
                value_block, expo.astype(jnp.bfloat16), preferred_element_type=jnp.float32
            )
            out_ref[:, here] = (mixed * share).astype(jnp.bfloat16).T


def mix_paired_kernel(bias_ref, q_ref, row_max_ref, own, near, far, *refs):
    *value_refs, out_ref, max_ref = refs
    raise_maxima(max_ref, q_ref, near, bias_ref, 1, row_max_ref)
    mix_kernel(3, bias_ref, q_ref, max_ref, own, near, far, *value_refs, out_ref)


VMEM = pl.BlockSpec(memory_space=pltpu.VMEM)


def call(kernel, name, out_shape, blocks, products, *arrays, scratch=()):
    rows = out_shape[0].shape[-1] if products == 1 else out_shape[0].shape[0]
    pairs = QUERY_HEADS * rows * rows * blocks
    return pl.pallas_call(
        kernel,
        out_shape=out_shape,
        in_specs=[VMEM] * len(arrays),
        out_specs=(VMEM,) * len(out_shape),
        scratch_shapes=scratch,
        compiler_params=pltpu.CompilerParams(vmem_limit_bytes=24 << 20),
        cost_estimate=pl.CostEstimate(
            flops=2 * products * HEAD_SIZE * pairs,
            bytes_accessed=2 * QUERY_HEADS * HEAD_SIZE * rows * products,
            transcendentals=(products - 1) * pairs,
        ),
        name=name,
    )(*arrays)


def first_maxima(shards, pairs, segments, queries, keys):
    rows = queries.shape[0]
    hbm = pl.BlockSpec(memory_space=pltpu.HBM)
    out_shape = (
        pltpu.VMEM((QUERY_HEADS, rows), jnp.float32),
        pltpu.VMEM((len(pairs) * rows, rows), jnp.float32),
        pltpu.VMEM(queries.shape, queries.dtype),
        pltpu.VMEM(keys.shape, keys.dtype),
    )
    operands = [
        pltpu.with_memory_space_constraint(x, pltpu.HBM) for x in (segments, queries, keys)
    ]
    return pl.pallas_call(
        functools.partial(first_kernel, shards, pairs),
        out_shape=out_shape,
        in_specs=[hbm] * 3,
        out_specs=(VMEM,) * 4,
        scratch_shapes=[
            pltpu.VMEM(segments.shape, segments.dtype),
            pltpu.SemaphoreType.DMA((3,)),
        ],
        compiler_params=pltpu.CompilerParams(vmem_limit_bytes=24 << 20),
        cost_estimate=pl.CostEstimate(
            flops=2 * QUERY_HEADS * HEAD_SIZE * rows * rows,
            bytes_accessed=2 * QUERY_HEADS * HEAD_SIZE * rows,
            transcendentals=0,
        ),
        name="first_maxima",
    )(*operands)


def in_vmem(x):
    return pltpu.with_memory_space_constraint(x, pltpu.VMEM)


def float32(*shape):
    return jax.ShapeDtypeStruct(shape, jnp.float32)


def like(x):
    return jax.ShapeDtypeStruct(x.shape, x.dtype)


def plan_of_pairs(segments, queries, keys, values, devices):
    rows = queries.shape[0]
    across = [(i, i ^ 2) for i in range(4)]
    swap = [(i, i ^ 1) for i in range(4)]
    rotate = [(i, (i + 1) % 4) for i in range(4)]
    far_keys = lax.ppermute(keys, "seq", across)
    partner_queries = lax.ppermute(queries, "seq", swap)
    pairs = ((0, 0, None), (0, 1, None), (0, 2, None), (1, 2, 1), (-1, 0, 0))
    max_shape = float32(QUERY_HEADS, rows)
    row_max, bias, queries, own_keys = first_maxima(4, pairs, segments, queries, keys)
    sent_keys, values, bias = lax.optimization_barrier((keys, values, bias))
    far_values = lax.ppermute(values, "seq", across)
    near_values = lax.ppermute(values, "seq", rotate)
    near_keys = lax.ppermute(sent_keys, "seq", rotate)
    (near_max,) = call(
        functools.partial(next_kernel, 4),
        "near_maxima",
        (max_shape,),
        1,
        1,
        bias,
        partner_queries,
        row_max,
        own_keys,
    )
    row_max, head_max = call(
        last_paired_kernel,
        "last_maxima",
        (max_shape, float32(devices, 1, rows)),
        2,
        1,
        bias,
        queries,
        partner_queries,
        row_max,
        near_max,
        in_vmem(far_keys),
        scratch=[pltpu.VMEM(max_shape.shape, jnp.float32)],
    )
    everyone = lax.all_to_all(head_max, ("dp", "seq"), 0, 0)
    (attended,) = call(
        mix_paired_kernel,
        "mix",
        (like(queries),),
        3,
        2,
        bias,
        queries,
        row_max,
        own_keys,
        in_vmem(near_keys),
        in_vmem(far_keys),
        in_vmem(values),
        in_vmem(near_values),
        in_vmem(far_values),
        scratch=[pltpu.VMEM(max_shape.shape, jnp.float32)],
    )
    return attended, everyone


def plan_of_rotations(segments, queries, keys, values, devices, reach, shards):
    def passed_along(x, by):
        return lax.ppermute(x, "seq", [(i, (i + by) % shards) for i in range(shards)])

    rows = queries.shape[0]
    distances = range(reach, 0, -1)
    key_blocks = {d: passed_along(keys, d) for d in distances}
    pairs = tuple((0, d, None) for d in range(reach + 1))
    max_shape = float32(QUERY_HEADS, rows)
    row_max, bias, queries, own_keys = first_maxima(
        shards, pairs, segments, queries, keys
    )
    sent_values, bias = lax.optimization_barrier((values, bias))
    value_blocks = {d: passed_along(sent_values, d) for d in distances}
    for d in distances:
        out_shape = (max_shape,) + ((float32(devices, 1, rows),) if d == 1 else ())
        row_max, *head_max = call(
            functools.partial(next_kernel, d),
            f"maxima_{d}",
            out_shape,
            1,
            1,
            bias,
            queries,
            row_max,
            key_blocks[d],
        )
    everyone = lax.all_to_all(head_max[0], ("dp", "seq"), 0, 0)
    (attended,) = call(
        functools.partial(mix_kernel, reach + 1),
        "mix",
        (like(queries),),
        reach + 1,
        2,
        bias,
        queries,
        row_max,
        own_keys,
        *[key_blocks[d] for d in range(1, reach + 1)],
        values,
        *[value_blocks[d] for d in range(1, reach + 1)],
    )
    return attended, everyone


def clip_factors(head_max):
    clipped_logits = clip_level / jnp.maximum(head_max, clip_level)
    key_head_factor = jnp.sqrt(jnp.min(clipped_logits.reshape(KEY_VALUE_HEADS, GROUP), axis=1))
    query_factor = clipped_logits / jnp.repeat(key_head_factor, GROUP)
    return (query_factor, key_head_factor)


def local(queries, keys, values, segments):
    rows, length = queries.shape[1], segments.shape[1]
    shards = lax.axis_size("seq")
    devices = lax.axis_size("dp") * shards
    reach = reach_of(rows, length, shards)
    arrays = (segments, queries[0], keys[0], values[0], devices)
    if shards == 4 and reach == 2:
        attended, everyone = plan_of_pairs(*arrays)
    else:
        attended, everyone = plan_of_rotations(*arrays, reach, shards)
    everyone, attended = lax.optimization_barrier((everyone, attended))
    query_factor, key_head_factor = clip_factors(
        jnp.max(everyone[:, 0, :QUERY_HEADS], axis=0)
    )
    return (attended[None], query_factor, key_head_factor)


def solution(mesh):
    in_specs = (P("dp", "seq", None), P("dp", "seq", None), P("dp", "seq", None), P("dp", None))
    out_specs = (P("dp", "seq", None), P(), P())
    return jax.shard_map(local, mesh=mesh, in_specs=in_specs, out_specs=out_specs, check_vma=False)
```

time: 27.3 us -> 26 us (0.952)
  local copies, waits for them, and re-layouts: 3.28 us -> 0.25 us
  Pallas kernels: 7 us -> 8.91 us
    unnamed x16 -> x6, local copies, waits for them, and re-layouts: 3.04 us -> 0.02 us
    pallas_call x3 -> x4, Pallas kernels: 7 us -> 8.91 us  [the longest x3 6.76 us: call(): pl.pallas_call(kernel, out_shape=out_shape, in_specs=[VMEM] * len(arrays)...]
    all_to_all x1, waiting for transfers between devices: 3.05 us -> 2.6 us  [plan_of_pairs(): everyone = lax.all_to_all(head_max, ('dp', 'seq'), 0, 0)]
    ppermute x4 -> x5, waiting for transfers between devices: 1.04 us -> 1.38 us  [the longest x1 1.27 us: plan_of_pairs(): far_keys = lax.ppermute(keys, 'seq', across)]
    ppermute x4 -> x5, starting transfers between devices: 4.92 us -> 4.99 us  [the longest x1 2.56 us: plan_of_pairs(): far_keys = lax.ppermute(keys, 'seq', across)]
  transfers between devices with their start and end apart: 5 -> 6, of which waited for: 2 -> 3; matrix products, arithmetic and copies ran while one was open for 0% -> 0% of each run, Pallas kernels for 26% -> 34%
where the time goes in v5:
time: 26 us; the launch traced here: 25.9 us
  starting transfers between devices  11.3 us (43%)
  Pallas kernels  8.91 us (34%)
  waiting for transfers between devices  3.98 us (15%)
  between operations  0.72 us (3%)
  other arithmetic  0.71 us (3%)
    pallas_call x3, Pallas kernels, call(): pl.pallas_call(kernel, out_shape=out_shape, in_specs=[VMEM] * len(arrays)...  6.76 us
    all_to_all x1, starting transfers between devices, plan_of_pairs(): everyone = lax.all_to_all(head_max, ('dp', 'seq'), 0, 0)  6.3 us
    all_to_all x1, waiting for transfers between devices, plan_of_pairs(): everyone = lax.all_to_all(head_max, ('dp', 'seq'), 0, 0)  2.6 us
    ppermute x1, starting transfers between devices, plan_of_pairs(): far_keys = lax.ppermute(keys, 'seq', across)  2.56 us
    pallas_call x1, Pallas kernels, first_maxima(): pl.pallas_call(functools.partial(first_kernel, shards, pairs), out_shape=...  2.15 us
    ppermute x1, starting transfers between devices, plan_of_pairs(): near_values = lax.ppermute(values, 'seq', rotate)  1.42 us
    ppermute x1, waiting for transfers between devices, plan_of_pairs(): far_keys = lax.ppermute(keys, 'seq', across)  1.27 us
    div x1, other arithmetic, clip_factors(): query_factor = clipped_logits / jnp.repeat(key_head_factor, GROUP)  0.53 us
  transfers between devices with their start and end apart: 6, of which 3 were waited for; matrix products, arithmetic and copies ran while one was open for 0% of the time, Pallas kernels for 34%

profile of v5, /device:TPU:0, one launch (start us, length us, event | category | flops | bytes accessed | tf_op | source)
XLA Modules:
  0.0 25.9 jit_solution(17004692668034810118)
XLA Ops:
  0.6 0.0 copy-start.1
  0.6 0.0 copy-start
  0.7 0.5 %collective-permute-start = (bf16[128,6144]{1,0:T(8,128)(2,1)}, bf16[128,6144]{1,0:T(8,128)(2,1)S(1)}, u32[]{:S(2)}, u32[]{:S(2)}) collective-permute-start(bf16[128,6144]{1,0:T(8,128)(2,1)} %bitcast.7), channel_id=1, source_target_pairs={{0,1},{1,0},{2,3},{3,2},{4,5},{5,4},{6,7},{7,6},{8,9},{9,8},{10,11... | collective-permute-start | bytes 4718600 | tf_op jit(solution)/shard_map/ppermute | solution.py:207
  1.2 2.6 %collective-permute-start.1 = (bf16[128,768]{1,0:T(8,128)(2,1)}, bf16[128,768]{1,0:T(8,128)(2,1)S(1)}, u32[]{:S(2)}, u32[]{:S(2)}) collective-permute-start(bf16[128,768]{1,0:T(8,128)(2,1)} %bitcast.10), channel_id=1, source_target_pairs={{0,2},{1,3},{2,0},{3,1},{4,6},{5,7},{6,4},{7,5},{8,10},{9,11},{10,... | collective-permute-start | bytes 589832 | tf_op jit(solution)/shard_map/ppermute | solution.py:206
  3.7 2.1 %first_maxima.1 = (f32[48,128]{1,0:T(8,128)S(1)}, f32[640,128]{1,0:T(8,128)S(1)}, bf16[128,6144]{1,0:T(8,128)(2,1)S(1)}, bf16[128,768]{1,0:T(8,128)(2,1)S(1)}) custom-call(s32[1,512]{1,0:T(1,128)} %seg_hbm.1, bf16[128,6144]{1,0:T(8,128)(2,1)} %bitcast.8, bf16[128,768]{1,0:T(8,128)(2,1)} %bitcast.11), custom_call_target="tpu_custom_call" | custom-call | flops 201326592 | bytes 1572864 | tf_op jit(solution)/shard_map/first_maxima/pallas_call | solution.py:170
  5.9 0.0 copy-done.1
  5.9 0.2 collective-permute-start.2
  6.1 0.0 copy-done
  6.1 0.3 %collective-permute-start.4 = (bf16[128,768]{1,0:T(8,128)(2,1)S(1)}, bf16[128,768]{1,0:T(8,128)(2,1)S(1)}, u32[]{:S(2)}, u32[]{:S(2)}) collective-permute-start(bf16[128,768]{1,0:T(8,128)(2,1)S(1)} %bitcast.4), channel_id=1, source_target_pairs={{0,2},{1,3},{2,0},{3,1},{4,6},{5,7},{6,4},{7,5},{8,10},{9,11},{10,... | collective-permute-start | bytes 589832 | tf_op jit(solution)/shard_map/ppermute | solution.py:212
  6.4 1.4 %collective-permute-start.3 = (bf16[128,768]{1,0:T(8,128)(2,1)S(1)}, bf16[128,768]{1,0:T(8,128)(2,1)S(1)}, u32[]{:S(2)}, u32[]{:S(2)}) collective-permute-start(bf16[128,768]{1,0:T(8,128)(2,1)S(1)} %bitcast.5), channel_id=1, source_target_pairs={{0,1},{1,2},{2,3},{3,0},{4,5},{5,6},{6,7},{7,4},{8,9},{9,10},{10,1... | collective-permute-start | bytes 589832 | tf_op jit(solution)/shard_map/ppermute | solution.py:213
  7.8 0.0 collective-permute-done.q_ref.partner_ref
  7.8 0.6 %near_maxima.1.near_ref = f32[48,128]{1,0:T(8,128)S(1)} custom-call(f32[640,128]{1,0:T(8,128)S(1)} %get-tuple-element.15.bias_ref, bf16[128,6144]{1,0:T(8,128)(2,1)S(1)} %collective-permute-done.q_ref.partner_ref, f32[48,128]{1,0:T(8,128)S(1)} %get-tuple-element.17.before_ref, bf16[128,768]{1,0:T(8,128)(2,1)S(1)} %get-tuple-element.18.key_ref.own), custom_call_target="tpu_custom_call" | custom-call | flops 201326592 | bytes 1572864 | tf_op jit(solution)/shard_map/near_maxima/pallas_call | solution.py:142
  8.4 1.3 %collective-permute-done.1.key_ref.far = bf16[128,768]{1,0:T(8,128)(2,1)S(1)} collective-permute-done((bf16[128,768]{1,0:T(8,128)(2,1)}, bf16[128,768]{1,0:T(8,128)(2,1)S(1)}, u32[]{:S(2)}, u32[]{:S(2)}) %collective-permute-start.1) | collective-permute-done | bytes 196640 | tf_op jit(solution)/shard_map/ppermute | solution.py:206
  9.7 1.7 %last_maxima.1 = (f32[48,128]{1,0:T(8,128)S(1)}, f32[32,1,128]{2,1,0:T(1,128)}) custom-call(f32[640,128]{1,0:T(8,128)S(1)} %get-tuple-element.15.bias_ref, bf16[128,6144]{1,0:T(8,128)(2,1)S(1)} %get-tuple-element.16.q_ref, bf16[128,6144]{1,0:T(8,128)(2,1)S(1)} %collective-permute-done.q_ref.partner_ref, f32[48,128]{1,0:T(8,128)S(1)} %get-tuple-element.17.before_ref, ...), custom_call_target="tpu_custom_call" | custom-call | flops 402653184 | bytes 1572864 | tf_op jit(solution)/shard_map/last_maxima/pallas_call | solution.py:142
  11.4 6.3 %all-to-all-start = ((f32[32,1,128]{2,1,0:T(1,128)}), f32[32,1,128]{2,1,0:T(1,128)S(1)}, u32[]{:S(2)}, u32[]{:S(2)}) async-start(f32[32,1,128]{2,1,0:T(1,128)} %get-tuple-element.19), calls=%async_computation | async-start | bytes 32768 | tf_op jit(solution)/shard_map/all_to_all | solution.py:240
  17.7 0.0 collective-permute-done.2.near
  17.8 0.0 collective-permute-done.4.refs_2_
  17.8 0.1 collective-permute-done.3.refs_1_
  17.9 4.4 %mix.1 = bf16[128,6144]{1,0:T(8,128)(2,1)} custom-call(f32[640,128]{1,0:T(8,128)S(1)} %get-tuple-element.15.bias_ref, bf16[128,6144]{1,0:T(8,128)(2,1)S(1)} %get-tuple-element.16.q_ref, f32[48,128]{1,0:T(8,128)S(1)} %get-tuple-element.20.row_max_ref, bf16[128,768]{1,0:T(8,128)(2,1)S(1)} %get-tuple-element.18.key_ref.own, ...), custom_call_target="tpu_custom_call" | custom-call | flops 1207959552 | bytes 3145728 | tf_op jit(solution)/shard_map/mix/pallas_call | solution.py:142
  22.3 2.6 %all-to-all-done = f32[32,1,128]{2,1,0:T(1,128)S(1)} async-done(((f32[32,1,128]{2,1,0:T(1,128)}), f32[32,1,128]{2,1,0:T(1,128)S(1)}, u32[]{:S(2)}, u32[]{:S(2)}) %all-to-all-start) | async-done | bytes 16416 | tf_op jit(solution)/shard_map/all_to_all | solution.py:240
  24.9 0.1 slice_reduce_fusion
  25.0 0.1 div.11
  25.0 0.1 reduce_min.9
  25.2 0.0 copy-start.2
  25.2 0.1 broadcast_in_dim.7
  25.2 0.1 reshape.15
  25.3 0.5 %multiply_divide_fusion = f32[48]{0:T(128)} fusion(f32[48]{0:T(128)S(1)} %reshape.15, f32[48]{0:T(128)S(1)} %slice_reduce_fusion), kind=kLoop, calls=%fused_computation.1 | loop fusion | flops 144 | bytes 576 | tf_op jit(solution)/shard_map/div | solution.py:309
  25.9 0.0 copy-done.2
  (2 shorter events, 0.0 us)
Async XLA Ops:
  0.6 5.3 %copy-start.1 = (bf16[1,128,768]{2,1,0:T(8,128)(2,1)S(1)}, bf16[1,128,768]{2,1,0:T(8,128)(2,1)}, u32[]{:S(2)}) copy-start(bf16[1,128,768]{2,1,0:T(8,128)(2,1)} %param.5) | copy-start | bytes 589828
  0.6 5.5 %copy-start = (bf16[1,128,768]{2,1,0:T(8,128)(2,1)S(1)}, bf16[1,128,768]{2,1,0:T(8,128)(2,1)}, u32[]{:S(2)}) copy-start(bf16[1,128,768]{2,1,0:T(8,128)(2,1)} %param.6) | copy-start | bytes 589828
  0.7 7.2 %collective-permute-start = (bf16[128,6144]{1,0:T(8,128)(2,1)}, bf16[128,6144]{1,0:T(8,128)(2,1)S(1)}, u32[]{:S(2)}, u32[]{:S(2)}) collective-permute-start(bf16[128,6144]{1,0:T(8,128)(2,1)} %bitcast.7), channel_id=1, source_target_pairs={{0,1},{1,0},{2,3},{3,2},{4,5},{5,4},{6,7},{7,6},{8,9},{9,8},{10,11... | collective-permute-start | bytes 4718600 | tf_op jit(solution)/shard_map/ppermute | solution.py:207
  1.2 8.5 %collective-permute-start.1 = (bf16[128,768]{1,0:T(8,128)(2,1)}, bf16[128,768]{1,0:T(8,128)(2,1)S(1)}, u32[]{:S(2)}, u32[]{:S(2)}) collective-permute-start(bf16[128,768]{1,0:T(8,128)(2,1)} %bitcast.10), channel_id=1, source_target_pairs={{0,2},{1,3},{2,0},{3,1},{4,6},{5,7},{6,4},{7,5},{8,10},{9,11},{10,... | collective-permute-start | bytes 589832 | tf_op jit(solution)/shard_map/ppermute | solution.py:206
  5.9 11.9 %collective-permute-start.2 = (bf16[128,768]{1,0:T(8,128)(2,1)S(1)}, bf16[128,768]{1,0:T(8,128)(2,1)S(1)}, u32[]{:S(2)}, u32[]{:S(2)}) collective-permute-start(bf16[128,768]{1,0:T(8,128)(2,1)S(1)} %bitcast.12), channel_id=1, source_target_pairs={{0,1},{1,2},{2,3},{3,0},{4,5},{5,6},{6,7},{7,4},{8,9},{9,10},{10,1... | collective-permute-start | bytes 589832 | tf_op jit(solution)/shard_map/ppermute | solution.py:214
  6.1 11.6 %collective-permute-start.4 = (bf16[128,768]{1,0:T(8,128)(2,1)S(1)}, bf16[128,768]{1,0:T(8,128)(2,1)S(1)}, u32[]{:S(2)}, u32[]{:S(2)}) collective-permute-start(bf16[128,768]{1,0:T(8,128)(2,1)S(1)} %bitcast.4), channel_id=1, source_target_pairs={{0,2},{1,3},{2,0},{3,1},{4,6},{5,7},{6,4},{7,5},{8,10},{9,11},{10,... | collective-permute-start | bytes 589832 | tf_op jit(solution)/shard_map/ppermute | solution.py:212
  6.4 11.5 %collective-permute-start.3 = (bf16[128,768]{1,0:T(8,128)(2,1)S(1)}, bf16[128,768]{1,0:T(8,128)(2,1)S(1)}, u32[]{:S(2)}, u32[]{:S(2)}) collective-permute-start(bf16[128,768]{1,0:T(8,128)(2,1)S(1)} %bitcast.5), channel_id=1, source_target_pairs={{0,1},{1,2},{2,3},{3,0},{4,5},{5,6},{6,7},{7,4},{8,9},{9,10},{10,1... | collective-permute-start | bytes 589832 | tf_op jit(solution)/shard_map/ppermute | solution.py:213
  11.4 13.5 %all-to-all-start = ((f32[32,1,128]{2,1,0:T(1,128)}), f32[32,1,128]{2,1,0:T(1,128)S(1)}, u32[]{:S(2)}, u32[]{:S(2)}) async-start(f32[32,1,128]{2,1,0:T(1,128)} %get-tuple-element.19), calls=%async_computation | async-start | bytes 32768 | tf_op jit(solution)/shard_map/all_to_all | solution.py:240
  25.2 0.7 %copy-start.2 = (f32[6]{0:T(128)}, f32[6]{0:T(128)S(1)}, u32[]{:S(2)}) copy-start(f32[6]{0:T(128)S(1)} %sqrt.3) | copy-start | bytes 76

commit v6 on v5

--- a/solution.py
+++ b/solution.py
@@ -102,8 +102,12 @@
     bias_ref, q_ref, partner_ref, before_ref, near_ref, key_ref, max_ref, head_max_ref, all_ref
 ):
     raise_maxima(max_ref, q_ref, key_ref, bias_ref, 2, before_ref)
-    raise_maxima(all_ref, partner_ref, key_ref, bias_ref, 3, near_ref)
-    all_ref[...] = jnp.maximum(all_ref[...], max_ref[...])
+    all_ref[...] = jnp.maximum(near_ref[...], max_ref[...])
+
+    @pl.when(lax.axis_index("seq") % 2 == 1)
+    def _():
+        raise_maxima(all_ref, partner_ref, key_ref, bias_ref, 3, all_ref)
+
     store_head_maxima(head_max_ref, all_ref)
 
 
@@ -208,10 +212,6 @@
     pairs = ((0, 0, None), (0, 1, None), (0, 2, None), (1, 2, 1), (-1, 0, 0))
     max_shape = float32(QUERY_HEADS, rows)
     row_max, bias, queries, own_keys = first_maxima(4, pairs, segments, queries, keys)
-    sent_keys, values, bias = lax.optimization_barrier((keys, values, bias))
-    far_values = lax.ppermute(values, "seq", across)
-    near_values = lax.ppermute(values, "seq", rotate)
-    near_keys = lax.ppermute(sent_keys, "seq", rotate)
     (near_max,) = call(
         functools.partial(next_kernel, 4),
         "near_maxima",
@@ -223,10 +223,14 @@
         row_max,
         own_keys,
     )
+    sent_keys, values, near_max = lax.optimization_barrier((keys, values, near_max))
+    far_values = lax.ppermute(values, "seq", across)
+    near_values = lax.ppermute(values, "seq", rotate)
+    near_keys = lax.ppermute(sent_keys, "seq", rotate)
     row_max, head_max = call(
         last_paired_kernel,
         "last_maxima",
-        (max_shape, float32(devices, 1, rows)),
+        (max_shape, pltpu.VMEM((devices, 1, rows), jnp.float32)),
         2,
         1,
         bias,

time: 26 us -> 25.4 us (0.977)
  Pallas kernels: 8.91 us -> 8.49 us
    ppermute x1, starting transfers between devices: 0.27 us -> 1.34 us  [plan_of_pairs(): far_values = lax.ppermute(values, 'seq', across)]
    ppermute x1, starting transfers between devices: 1.42 us -> 0.37 us  [plan_of_pairs(): near_values = lax.ppermute(values, 'seq', rotate)]
    all_to_all x1, waiting for transfers between devices: 2.6 us -> 1.8 us  [plan_of_pairs(): everyone = lax.all_to_all(head_max, ('dp', 'seq'), 0, 0)]
    ppermute x1, waiting for transfers between devices: 0.1 us -> 0.9 us  [plan_of_pairs(): near_values = lax.ppermute(values, 'seq', rotate)]
    pallas_call x3, Pallas kernels: 6.76 us -> 6.35 us  [call(): pl.pallas_call(kernel, out_shape=out_shape, in_specs=[VMEM] * len(arrays)...]
where the time goes in v6:
time: 25.4 us; the launch traced here: 25.2 us
  starting transfers between devices  11.3 us (44%)
  Pallas kernels  8.49 us (33%)
  waiting for transfers between devices  3.76 us (15%)
  other arithmetic  0.71 us (3%)
  between operations  0.71 us (3%)
    pallas_call x3, Pallas kernels, call(): pl.pallas_call(kernel, out_shape=out_shape, in_specs=[VMEM] * len(arrays)...  6.35 us
    all_to_all x1, starting transfers between devices, plan_of_pairs(): everyone = lax.all_to_all(head_max, ('dp', 'seq'), 0, 0)  6.24 us
    ppermute x1, starting transfers between devices, plan_of_pairs(): far_keys = lax.ppermute(keys, 'seq', across)  2.58 us
    pallas_call x1, Pallas kernels, first_maxima(): pl.pallas_call(functools.partial(first_kernel, shards, pairs), out_shape=...  2.15 us
    all_to_all x1, waiting for transfers between devices, plan_of_pairs(): everyone = lax.all_to_all(head_max, ('dp', 'seq'), 0, 0)  1.8 us
    ppermute x1, starting transfers between devices, plan_of_pairs(): far_values = lax.ppermute(values, 'seq', across)  1.34 us
    ppermute x1, waiting for transfers between devices, plan_of_pairs(): far_keys = lax.ppermute(keys, 'seq', across)  1.06 us
    ppermute x1, waiting for transfers between devices, plan_of_pairs(): near_values = lax.ppermute(values, 'seq', rotate)  0.9 us
  transfers between devices with their start and end apart: 6, of which 3 were waited for; matrix products, arithmetic and copies ran while one was open for 0% of the time, Pallas kernels for 34%

profile of v6, /device:TPU:0, one launch (start us, length us, event | category | flops | bytes accessed | tf_op | source)
XLA Modules:
  0.0 25.2 jit_solution(9690667844146498290)
XLA Ops:
  0.6 0.5 %collective-permute-start = (bf16[128,6144]{1,0:T(8,128)(2,1)}, bf16[128,6144]{1,0:T(8,128)(2,1)S(1)}, u32[]{:S(2)}, u32[]{:S(2)}) collective-permute-start(bf16[128,6144]{1,0:T(8,128)(2,1)} %bitcast.7), channel_id=1, source_target_pairs={{0,1},{1,0},{2,3},{3,2},{4,5},{5,4},{6,7},{7,6},{8,9},{9,8},{10,11... | collective-permute-start | bytes 4718600 | tf_op jit(solution)/shard_map/ppermute | solution.py:211
  1.1 0.0 copy-start.1
  1.2 0.0 copy-start
  1.2 2.6 %collective-permute-start.1 = (bf16[128,768]{1,0:T(8,128)(2,1)}, bf16[128,768]{1,0:T(8,128)(2,1)S(1)}, u32[]{:S(2)}, u32[]{:S(2)}) collective-permute-start(bf16[128,768]{1,0:T(8,128)(2,1)} %bitcast.10), channel_id=1, source_target_pairs={{0,2},{1,3},{2,0},{3,1},{4,6},{5,7},{6,4},{7,5},{8,10},{9,11},{10,... | collective-permute-start | bytes 589832 | tf_op jit(solution)/shard_map/ppermute | solution.py:210
  3.7 2.1 %first_maxima.1 = (f32[48,128]{1,0:T(8,128)S(1)}, f32[640,128]{1,0:T(8,128)S(1)}, bf16[128,6144]{1,0:T(8,128)(2,1)S(1)}, bf16[128,768]{1,0:T(8,128)(2,1)S(1)}) custom-call(s32[1,512]{1,0:T(1,128)} %seg_hbm.1, bf16[128,6144]{1,0:T(8,128)(2,1)} %bitcast.8, bf16[128,768]{1,0:T(8,128)(2,1)} %bitcast.11), custom_call_target="tpu_custom_call" | custom-call | flops 201326592 | bytes 1572864 | tf_op jit(solution)/shard_map/first_maxima/pallas_call | solution.py:174
  5.9 0.0 collective-permute-done.q_ref.partner_ref
  5.9 0.6 %near_maxima.1.near_ref = f32[48,128]{1,0:T(8,128)S(1)} custom-call(f32[640,128]{1,0:T(8,128)S(1)} %get-tuple-element.14.bias_ref, bf16[128,6144]{1,0:T(8,128)(2,1)S(1)} %collective-permute-done.q_ref.partner_ref, f32[48,128]{1,0:T(8,128)S(1)} %get-tuple-element.16.before_ref, bf16[128,768]{1,0:T(8,128)(2,1)S(1)} %get-tuple-element.17.key_ref.own), custom_call_target="tpu_custom_call" | custom-call | flops 201326592 | bytes 1572864 | tf_op jit(solution)/shard_map/near_maxima/pallas_call | solution.py:146
  6.5 0.0 copy-done.1
  6.5 0.2 collective-permute-start.2
  6.7 0.0 copy-done
  6.7 1.3 %collective-permute-start.4 = (bf16[128,768]{1,0:T(8,128)(2,1)S(1)}, bf16[128,768]{1,0:T(8,128)(2,1)S(1)}, u32[]{:S(2)}, u32[]{:S(2)}) collective-permute-start(bf16[128,768]{1,0:T(8,128)(2,1)S(1)} %bitcast.4), channel_id=1, source_target_pairs={{0,2},{1,3},{2,0},{3,1},{4,6},{5,7},{6,4},{7,5},{8,10},{9,11},{10,... | collective-permute-start | bytes 589832 | tf_op jit(solution)/shard_map/ppermute | solution.py:227
  8.1 0.4 %collective-permute-start.3 = (bf16[128,768]{1,0:T(8,128)(2,1)S(1)}, bf16[128,768]{1,0:T(8,128)(2,1)S(1)}, u32[]{:S(2)}, u32[]{:S(2)}) collective-permute-start(bf16[128,768]{1,0:T(8,128)(2,1)S(1)} %bitcast.5), channel_id=1, source_target_pairs={{0,1},{1,2},{2,3},{3,0},{4,5},{5,6},{6,7},{7,4},{8,9},{9,10},{10,1... | collective-permute-start | bytes 589832 | tf_op jit(solution)/shard_map/ppermute | solution.py:228
  8.4 1.1 %collective-permute-done.1.key_ref.far = bf16[128,768]{1,0:T(8,128)(2,1)S(1)} collective-permute-done((bf16[128,768]{1,0:T(8,128)(2,1)}, bf16[128,768]{1,0:T(8,128)(2,1)S(1)}, u32[]{:S(2)}, u32[]{:S(2)}) %collective-permute-start.1) | collective-permute-done | bytes 196640 | tf_op jit(solution)/shard_map/ppermute | solution.py:210
  9.5 1.3 %last_maxima.1 = (f32[48,128]{1,0:T(8,128)S(1)}, f32[32,1,128]{2,1,0:T(1,128)}) custom-call(f32[640,128]{1,0:T(8,128)S(1)} %get-tuple-element.14.bias_ref, bf16[128,6144]{1,0:T(8,128)(2,1)S(1)} %get-tuple-element.15.q_ref, bf16[128,6144]{1,0:T(8,128)(2,1)S(1)} %collective-permute-done.q_ref.partner_ref, f32[48,128]{1,0:T(8,128)S(1)} %get-tuple-element.16.before_ref, ...), custom_call_target="tpu_custom_call" | custom-call | flops 402653184 | bytes 1572864 | tf_op jit(solution)/shard_map/last_maxima/pallas_call | solution.py:146
  10.8 6.2 %all-to-all-start = ((f32[32,1,128]{2,1,0:T(1,128)}), f32[32,1,128]{2,1,0:T(1,128)S(1)}, u32[]{:S(2)}, u32[]{:S(2)}) async-start(f32[32,1,128]{2,1,0:T(1,128)} %get-tuple-element.19), calls=%async_computation | async-start | bytes 32768 | tf_op jit(solution)/shard_map/all_to_all | solution.py:244
  17.1 0.0 collective-permute-done.2.near
  17.1 0.0 collective-permute-done.4.refs_2_
  17.1 0.9 %collective-permute-done.3.refs_1_ = bf16[128,768]{1,0:T(8,128)(2,1)S(1)} collective-permute-done((bf16[128,768]{1,0:T(8,128)(2,1)S(1)}, bf16[128,768]{1,0:T(8,128)(2,1)S(1)}, u32[]{:S(2)}, u32[]{:S(2)}) %collective-permute-start.3) | collective-permute-done | bytes 196640 | tf_op jit(solution)/shard_map/ppermute | solution.py:228
  18.0 4.4 %mix.1 = bf16[128,6144]{1,0:T(8,128)(2,1)} custom-call(f32[640,128]{1,0:T(8,128)S(1)} %get-tuple-element.14.bias_ref, bf16[128,6144]{1,0:T(8,128)(2,1)S(1)} %get-tuple-element.15.q_ref, f32[48,128]{1,0:T(8,128)S(1)} %get-tuple-element.20.row_max_ref, bf16[128,768]{1,0:T(8,128)(2,1)S(1)} %get-tuple-element.17.key_ref.own, ...), custom_call_target="tpu_custom_call" | custom-call | flops 1207959552 | bytes 3145728 | tf_op jit(solution)/shard_map/mix/pallas_call | solution.py:146
  22.4 1.8 %all-to-all-done = f32[32,1,128]{2,1,0:T(1,128)S(1)} async-done(((f32[32,1,128]{2,1,0:T(1,128)}), f32[32,1,128]{2,1,0:T(1,128)S(1)}, u32[]{:S(2)}, u32[]{:S(2)}) %all-to-all-start) | async-done | bytes 16416 | tf_op jit(solution)/shard_map/all_to_all | solution.py:244
  24.2 0.1 slice_reduce_fusion
  24.3 0.1 div.11
  24.4 0.1 reduce_min.9
  24.5 0.0 copy-start.2
  24.5 0.1 broadcast_in_dim.7
  24.6 0.1 reshape.15
  24.6 0.5 %multiply_divide_fusion = f32[48]{0:T(128)} fusion(f32[48]{0:T(128)S(1)} %reshape.15, f32[48]{0:T(128)S(1)} %slice_reduce_fusion), kind=kLoop, calls=%fused_computation.1 | loop fusion | flops 144 | bytes 576 | tf_op jit(solution)/shard_map/div | solution.py:313
  25.2 0.0 copy-done.2
  (2 shorter events, 0.0 us)
Async XLA Ops:
  0.6 5.3 %collective-permute-start = (bf16[128,6144]{1,0:T(8,128)(2,1)}, bf16[128,6144]{1,0:T(8,128)(2,1)S(1)}, u32[]{:S(2)}, u32[]{:S(2)}) collective-permute-start(bf16[128,6144]{1,0:T(8,128)(2,1)} %bitcast.7), channel_id=1, source_target_pairs={{0,1},{1,0},{2,3},{3,2},{4,5},{5,4},{6,7},{7,6},{8,9},{9,8},{10,11... | collective-permute-start | bytes 4718600 | tf_op jit(solution)/shard_map/ppermute | solution.py:211
  1.1 5.4 %copy-start.1 = (bf16[1,128,768]{2,1,0:T(8,128)(2,1)S(1)}, bf16[1,128,768]{2,1,0:T(8,128)(2,1)}, u32[]{:S(2)}) copy-start(bf16[1,128,768]{2,1,0:T(8,128)(2,1)} %param.5) | copy-start | bytes 589828
  1.2 5.6 %copy-start = (bf16[1,128,768]{2,1,0:T(8,128)(2,1)S(1)}, bf16[1,128,768]{2,1,0:T(8,128)(2,1)}, u32[]{:S(2)}) copy-start(bf16[1,128,768]{2,1,0:T(8,128)(2,1)} %param.6) | copy-start | bytes 589828
  1.2 8.3 %collective-permute-start.1 = (bf16[128,768]{1,0:T(8,128)(2,1)}, bf16[128,768]{1,0:T(8,128)(2,1)S(1)}, u32[]{:S(2)}, u32[]{:S(2)}) collective-permute-start(bf16[128,768]{1,0:T(8,128)(2,1)} %bitcast.10), channel_id=1, source_target_pairs={{0,2},{1,3},{2,0},{3,1},{4,6},{5,7},{6,4},{7,5},{8,10},{9,11},{10,... | collective-permute-start | bytes 589832 | tf_op jit(solution)/shard_map/ppermute | solution.py:210
  6.5 10.6 %collective-permute-start.2 = (bf16[128,768]{1,0:T(8,128)(2,1)S(1)}, bf16[128,768]{1,0:T(8,128)(2,1)S(1)}, u32[]{:S(2)}, u32[]{:S(2)}) collective-permute-start(bf16[128,768]{1,0:T(8,128)(2,1)S(1)} %bitcast.12), channel_id=1, source_target_pairs={{0,1},{1,2},{2,3},{3,0},{4,5},{5,6},{6,7},{7,4},{8,9},{9,10},{10,1... | collective-permute-start | bytes 589832 | tf_op jit(solution)/shard_map/ppermute | solution.py:229
  6.7 10.4 %collective-permute-start.4 = (bf16[128,768]{1,0:T(8,128)(2,1)S(1)}, bf16[128,768]{1,0:T(8,128)(2,1)S(1)}, u32[]{:S(2)}, u32[]{:S(2)}) collective-permute-start(bf16[128,768]{1,0:T(8,128)(2,1)S(1)} %bitcast.4), channel_id=1, source_target_pairs={{0,2},{1,3},{2,0},{3,1},{4,6},{5,7},{6,4},{7,5},{8,10},{9,11},{10,... | collective-permute-start | bytes 589832 | tf_op jit(solution)/shard_map/ppermute | solution.py:227
  8.1 9.9 %collective-permute-start.3 = (bf16[128,768]{1,0:T(8,128)(2,1)S(1)}, bf16[128,768]{1,0:T(8,128)(2,1)S(1)}, u32[]{:S(2)}, u32[]{:S(2)}) collective-permute-start(bf16[128,768]{1,0:T(8,128)(2,1)S(1)} %bitcast.5), channel_id=1, source_target_pairs={{0,1},{1,2},{2,3},{3,0},{4,5},{5,6},{6,7},{7,4},{8,9},{9,10},{10,1... | collective-permute-start | bytes 589832 | tf_op jit(solution)/shard_map/ppermute | solution.py:228
  10.8 13.4 %all-to-all-start = ((f32[32,1,128]{2,1,0:T(1,128)}), f32[32,1,128]{2,1,0:T(1,128)S(1)}, u32[]{:S(2)}, u32[]{:S(2)}) async-start(f32[32,1,128]{2,1,0:T(1,128)} %get-tuple-element.19), calls=%async_computation | async-start | bytes 32768 | tf_op jit(solution)/shard_map/all_to_all | solution.py:244
  24.5 0.7 %copy-start.2 = (f32[6]{0:T(128)}, f32[6]{0:T(128)S(1)}, u32[]{:S(2)}) copy-start(f32[6]{0:T(128)S(1)} %sqrt.3) | copy-start | bytes 76

commit v7 on v6

--- a/solution.py
+++ b/solution.py
@@ -74,8 +74,8 @@
     head_max_ref[...] = jnp.broadcast_to(head_max[None], head_max_ref.shape)
 
 
-def first_kernel(
-    shards, pairs, seg_hbm, q_hbm, key_hbm, max_ref, bias_ref, q_ref, key_ref, seg_ref, sems
+def load_kernel(
+    shards, pairs, seg_hbm, q_hbm, key_hbm, bias_ref, q_ref, key_ref, seg_ref, sems
 ):
     copies = [
         pltpu.make_async_copy(source, target, sems.at[i])
@@ -89,7 +89,13 @@
     fill_bias(seg_ref, bias_ref, lax.axis_index("seq"), shards, pairs, q_ref.shape[0])
     copies[1].wait()
     copies[2].wait()
+
+
+def first_kernel(bias_ref, q_ref, key_ref, *refs):
+    *partner_ref, max_ref = refs[: len(refs) // 2 + 1]
     raise_maxima(max_ref, q_ref, key_ref, bias_ref, 0)
+    if partner_ref:
+        raise_maxima(refs[-1], partner_ref[0], key_ref, bias_ref, 4, max_ref)
 
 
 def next_kernel(place, bias_ref, q_ref, before_ref, key_ref, max_ref, *head_max_refs):
@@ -159,34 +165,30 @@
     )(*arrays)
 
 
-def first_maxima(shards, pairs, segments, queries, keys):
+def load(shards, pairs, segments, queries, keys):
     rows = queries.shape[0]
     hbm = pl.BlockSpec(memory_space=pltpu.HBM)
-    out_shape = (
-        pltpu.VMEM((QUERY_HEADS, rows), jnp.float32),
-        pltpu.VMEM((len(pairs) * rows, rows), jnp.float32),
-        pltpu.VMEM(queries.shape, queries.dtype),
-        pltpu.VMEM(keys.shape, keys.dtype),
-    )
     operands = [
         pltpu.with_memory_space_constraint(x, pltpu.HBM) for x in (segments, queries, keys)
     ]
     return pl.pallas_call(
-        functools.partial(first_kernel, shards, pairs),
-        out_shape=out_shape,
+        functools.partial(load_kernel, shards, pairs),
+        out_shape=(
+            pltpu.VMEM((len(pairs) * rows, rows), jnp.float32),
+            pltpu.VMEM(queries.shape, queries.dtype),
+            pltpu.VMEM(keys.shape, keys.dtype),
+        ),
         in_specs=[hbm] * 3,
-        out_specs=(VMEM,) * 4,
+        out_specs=(VMEM,) * 3,
         scratch_shapes=[
             pltpu.VMEM(segments.shape, segments.dtype),
             pltpu.SemaphoreType.DMA((3,)),
         ],
         compiler_params=pltpu.CompilerParams(vmem_limit_bytes=24 << 20),
         cost_estimate=pl.CostEstimate(
-            flops=2 * QUERY_HEADS * HEAD_SIZE * rows * rows,
-            bytes_accessed=2 * QUERY_HEADS * HEAD_SIZE * rows,
-            transcendentals=0,
+            flops=0, bytes_accessed=2 * (queries.size + keys.size), transcendentals=0
         ),
-        name="first_maxima",
+        name="load",
     )(*operands)
 
 
@@ -211,17 +213,17 @@
     partner_queries = lax.ppermute(queries, "seq", swap)
     pairs = ((0, 0, None), (0, 1, None), (0, 2, None), (1, 2, 1), (-1, 0, 0))
     max_shape = float32(QUERY_HEADS, rows)
-    row_max, bias, queries, own_keys = first_maxima(4, pairs, segments, queries, keys)
-    (near_max,) = call(
-        functools.partial(next_kernel, 4),
-        "near_maxima",
-        (max_shape,),
-        1,
+    bias, queries, own_keys = load(4, pairs, segments, queries, keys)
+    row_max, near_max = call(
+        first_kernel,
+        "first_maxima",
+        (max_shape, max_shape),
+        2,
         1,
         bias,
+        queries,
+        own_keys,
         partner_queries,
-        row_max,
-        own_keys,
     )
     sent_keys, values, near_max = lax.optimization_barrier((keys, values, near_max))
     far_values = lax.ppermute(values, "seq", across)
@@ -271,8 +273,9 @@
     key_blocks = {d: passed_along(keys, d) for d in distances}
     pairs = tuple((0, d, None) for d in range(reach + 1))
     max_shape = float32(QUERY_HEADS, rows)
-    row_max, bias, queries, own_keys = first_maxima(
-        shards, pairs, segments, queries, keys
+    bias, queries, own_keys = load(shards, pairs, segments, queries, keys)
+    (row_max,) = call(
+        first_kernel, "first_maxima", (max_shape,), 1, 1, bias, queries, own_keys
     )
     sent_values, bias = lax.optimization_barrier((values, bias))
     value_blocks = {d: passed_along(sent_values, d) for d in distances}

time: 25.4 us -> 25.2 us (level)
    pallas_call x1, Pallas kernels: 2.15 us -> 1.56 us  [load(): pl.pallas_call(functools.partial(load_kernel, shards, pairs), out_shape=(...]
    ppermute x1, starting transfers between devices: 1.34 us -> 1.91 us  [plan_of_pairs(): far_values = lax.ppermute(values, 'seq', across)]
    pallas_call x3, Pallas kernels: 6.35 us -> 6.74 us  [call(): pl.pallas_call(kernel, out_shape=out_shape, in_specs=[VMEM] * len(arrays)...]
    ppermute x1, starting transfers between devices: 0.37 us -> 0.01 us  [plan_of_pairs(): near_values = lax.ppermute(values, 'seq', rotate)]
  transfers between devices with their start and end apart: 6 -> 6, of which waited for: 3 -> 3; matrix products, arithmetic and copies ran while one was open for 0% -> 0% of each run, Pallas kernels for 34% -> 33%
where the time goes in v7:
time: 25.2 us; the launch traced here: 25 us
  starting transfers between devices  11.3 us (45%)
  Pallas kernels  8.3 us (33%)
  waiting for transfers between devices  3.66 us (15%)
  between operations  0.72 us (3%)
  other arithmetic  0.71 us (3%)
  local copies, waits for them, and re-layouts  0.26 us (1%)
    pallas_call x3, Pallas kernels, call(): pl.pallas_call(kernel, out_shape=out_shape, in_specs=[VMEM] * len(arrays)...  6.74 us
    all_to_all x1, starting transfers between devices, plan_of_pairs(): everyone = lax.all_to_all(head_max, ('dp', 'seq'), 0, 0)  6.11 us
    ppermute x1, starting transfers between devices, plan_of_pairs(): far_keys = lax.ppermute(keys, 'seq', across)  2.56 us
    ppermute x1, starting transfers between devices, plan_of_pairs(): far_values = lax.ppermute(values, 'seq', across)  1.91 us
    all_to_all x1, waiting for transfers between devices, plan_of_pairs(): everyone = lax.all_to_all(head_max, ('dp', 'seq'), 0, 0)  1.73 us
    pallas_call x1, Pallas kernels, load(): pl.pallas_call(functools.partial(load_kernel, shards, pairs), out_shape=(...  1.56 us
    ppermute x1, waiting for transfers between devices, plan_of_pairs(): near_values = lax.ppermute(values, 'seq', rotate)  0.97 us
    ppermute x1, waiting for transfers between devices, plan_of_pairs(): far_keys = lax.ppermute(keys, 'seq', across)  0.95 us
  transfers between devices with their start and end apart: 6, of which 3 were waited for; matrix products, arithmetic and copies ran while one was open for 0% of the time, Pallas kernels for 33%

profile of v7, /device:TPU:0, one launch (start us, length us, event | category | flops | bytes accessed | tf_op | source)
XLA Modules:
  0.0 25.0 jit_solution(2032063501747405180)
XLA Ops:
  0.6 0.5 %collective-permute-start = (bf16[128,6144]{1,0:T(8,128)(2,1)}, bf16[128,6144]{1,0:T(8,128)(2,1)S(1)}, u32[]{:S(2)}, u32[]{:S(2)}) collective-permute-start(bf16[128,6144]{1,0:T(8,128)(2,1)} %bitcast.7), channel_id=1, source_target_pairs={{0,1},{1,0},{2,3},{3,2},{4,5},{5,4},{6,7},{7,6},{8,9},{9,8},{10,11... | collective-permute-start | bytes 4718600 | tf_op jit(solution)/shard_map/ppermute | solution.py:213
  1.1 2.6 %collective-permute-start.1 = (bf16[128,768]{1,0:T(8,128)(2,1)}, bf16[128,768]{1,0:T(8,128)(2,1)S(1)}, u32[]{:S(2)}, u32[]{:S(2)}) collective-permute-start(bf16[128,768]{1,0:T(8,128)(2,1)} %bitcast.10), channel_id=1, source_target_pairs={{0,2},{1,3},{2,0},{3,1},{4,6},{5,7},{6,4},{7,5},{8,10},{9,11},{10,... | collective-permute-start | bytes 589832 | tf_op jit(solution)/shard_map/ppermute | solution.py:212
  3.7 1.6 %load.1 = (f32[640,128]{1,0:T(8,128)S(1)}, bf16[128,6144]{1,0:T(8,128)(2,1)S(1)}, bf16[128,768]{1,0:T(8,128)(2,1)S(1)}) custom-call(s32[1,512]{1,0:T(1,128)} %seg_hbm.1, bf16[128,6144]{1,0:T(8,128)(2,1)} %bitcast.8, bf16[128,768]{1,0:T(8,128)(2,1)} %bitcast.11), custom_call_target="tpu_custom_call" | custom-call | bytes 1769472 | tf_op jit(solution)/shard_map/load/pallas_call | solution.py:174
  5.3 0.0 collective-permute-done.refs_0_.partner_ref
  5.3 0.0 copy-start.1
  5.3 0.0 copy-start
  5.3 1.0 %first_maxima.1 = (f32[48,128]{1,0:T(8,128)S(1)}, f32[48,128]{1,0:T(8,128)S(1)}) custom-call(f32[640,128]{1,0:T(8,128)S(1)} %get-tuple-element.15.bias_ref, bf16[128,6144]{1,0:T(8,128)(2,1)S(1)} %get-tuple-element.16.q_ref, bf16[128,768]{1,0:T(8,128)(2,1)S(1)} %get-tuple-element.17.key_ref.own, bf16[128,6144]{1,0:T(8,128)(2,1)S(1)} %collective-permute-done.refs_0_.partner_ref), custom_call_target="tpu_custom_call" | custom-call | flops 402653184 | bytes 1572864 | tf_op jit(solution)/shard_map/first_maxima/pallas_call | solution.py:152
  6.3 0.0 copy-done.1
  6.3 0.2 collective-permute-start.2
  6.6 0.0 copy-done
  6.6 1.9 %collective-permute-start.4 = (bf16[128,768]{1,0:T(8,128)(2,1)S(1)}, bf16[128,768]{1,0:T(8,128)(2,1)S(1)}, u32[]{:S(2)}, u32[]{:S(2)}) collective-permute-start(bf16[128,768]{1,0:T(8,128)(2,1)S(1)} %bitcast.4), channel_id=1, source_target_pairs={{0,2},{1,3},{2,0},{3,1},{4,6},{5,7},{6,4},{7,5},{8,10},{9,11},{10,... | collective-permute-start | bytes 589832 | tf_op jit(solution)/shard_map/ppermute | solution.py:229
  8.5 0.0 collective-permute-start.3
  8.5 1.0 %collective-permute-done.1.key_ref.far = bf16[128,768]{1,0:T(8,128)(2,1)S(1)} collective-permute-done((bf16[128,768]{1,0:T(8,128)(2,1)}, bf16[128,768]{1,0:T(8,128)(2,1)S(1)}, u32[]{:S(2)}, u32[]{:S(2)}) %collective-permute-start.1) | collective-permute-done | bytes 196640 | tf_op jit(solution)/shard_map/ppermute | solution.py:212
  9.4 1.3 %last_maxima.1 = (f32[48,128]{1,0:T(8,128)S(1)}, f32[32,1,128]{2,1,0:T(1,128)}) custom-call(f32[640,128]{1,0:T(8,128)S(1)} %get-tuple-element.15.bias_ref, bf16[128,6144]{1,0:T(8,128)(2,1)S(1)} %get-tuple-element.16.q_ref, bf16[128,6144]{1,0:T(8,128)(2,1)S(1)} %collective-permute-done.refs_0_.partner_ref, f32[48,128]{1,0:T(8,128)S(1)} %get-tuple-element.18.before_ref, ...), custom_call_target="tpu_custom_call" | custom-call | flops 402653184 | bytes 1572864 | tf_op jit(solution)/shard_map/last_maxima/pallas_call | solution.py:152
  10.7 6.1 %all-to-all-start = ((f32[32,1,128]{2,1,0:T(1,128)}), f32[32,1,128]{2,1,0:T(1,128)S(1)}, u32[]{:S(2)}, u32[]{:S(2)}) async-start(f32[32,1,128]{2,1,0:T(1,128)} %get-tuple-element.21), calls=%async_computation | async-start | bytes 32768 | tf_op jit(solution)/shard_map/all_to_all | solution.py:246
  16.9 0.0 collective-permute-done.2.near
  16.9 0.0 collective-permute-done.4.refs_2_
  16.9 1.0 %collective-permute-done.3.refs_1_ = bf16[128,768]{1,0:T(8,128)(2,1)S(1)} collective-permute-done((bf16[128,768]{1,0:T(8,128)(2,1)S(1)}, bf16[128,768]{1,0:T(8,128)(2,1)S(1)}, u32[]{:S(2)}, u32[]{:S(2)}) %collective-permute-start.3) | collective-permute-done | bytes 196640 | tf_op jit(solution)/shard_map/ppermute | solution.py:230
  17.8 4.4 %mix.1 = bf16[128,6144]{1,0:T(8,128)(2,1)} custom-call(f32[640,128]{1,0:T(8,128)S(1)} %get-tuple-element.15.bias_ref, bf16[128,6144]{1,0:T(8,128)(2,1)S(1)} %get-tuple-element.16.q_ref, f32[48,128]{1,0:T(8,128)S(1)} %get-tuple-element.22.row_max_ref, bf16[128,768]{1,0:T(8,128)(2,1)S(1)} %get-tuple-element.17.key_ref.own, ...), custom_call_target="tpu_custom_call" | custom-call | flops 1207959552 | bytes 3145728 | tf_op jit(solution)/shard_map/mix/pallas_call | solution.py:152
  22.3 1.7 %all-to-all-done = f32[32,1,128]{2,1,0:T(1,128)S(1)} async-done(((f32[32,1,128]{2,1,0:T(1,128)}), f32[32,1,128]{2,1,0:T(1,128)S(1)}, u32[]{:S(2)}, u32[]{:S(2)}) %all-to-all-start) | async-done | bytes 16416 | tf_op jit(solution)/shard_map/all_to_all | solution.py:246
  24.0 0.1 slice_reduce_fusion
  24.1 0.1 div.11
  24.1 0.1 reduce_min.9
  24.3 0.0 copy-start.2
  24.3 0.1 broadcast_in_dim.7
  24.4 0.1 reshape.15
  24.4 0.5 %multiply_divide_fusion = f32[48]{0:T(128)} fusion(f32[48]{0:T(128)S(1)} %reshape.15, f32[48]{0:T(128)S(1)} %slice_reduce_fusion), kind=kLoop, calls=%fused_computation.1 | loop fusion | flops 144 | bytes 576 | tf_op jit(solution)/shard_map/div | solution.py:316
  25.0 0.0 copy-done.2
  (2 shorter events, 0.0 us)
Async XLA Ops:
  0.6 4.7 %collective-permute-start = (bf16[128,6144]{1,0:T(8,128)(2,1)}, bf16[128,6144]{1,0:T(8,128)(2,1)S(1)}, u32[]{:S(2)}, u32[]{:S(2)}) collective-permute-start(bf16[128,6144]{1,0:T(8,128)(2,1)} %bitcast.7), channel_id=1, source_target_pairs={{0,1},{1,0},{2,3},{3,2},{4,5},{5,4},{6,7},{7,6},{8,9},{9,8},{10,11... | collective-permute-start | bytes 4718600 | tf_op jit(solution)/shard_map/ppermute | solution.py:213
  1.1 8.3 %collective-permute-start.1 = (bf16[128,768]{1,0:T(8,128)(2,1)}, bf16[128,768]{1,0:T(8,128)(2,1)S(1)}, u32[]{:S(2)}, u32[]{:S(2)}) collective-permute-start(bf16[128,768]{1,0:T(8,128)(2,1)} %bitcast.10), channel_id=1, source_target_pairs={{0,2},{1,3},{2,0},{3,1},{4,6},{5,7},{6,4},{7,5},{8,10},{9,11},{10,... | collective-permute-start | bytes 589832 | tf_op jit(solution)/shard_map/ppermute | solution.py:212
  5.3 1.0 %copy-start.1 = (bf16[1,128,768]{2,1,0:T(8,128)(2,1)S(1)}, bf16[1,128,768]{2,1,0:T(8,128)(2,1)}, u32[]{:S(2)}) copy-start(bf16[1,128,768]{2,1,0:T(8,128)(2,1)} %param.5) | copy-start | bytes 589828
  5.3 1.3 %copy-start = (bf16[1,128,768]{2,1,0:T(8,128)(2,1)S(1)}, bf16[1,128,768]{2,1,0:T(8,128)(2,1)}, u32[]{:S(2)}) copy-start(bf16[1,128,768]{2,1,0:T(8,128)(2,1)} %param.6) | copy-start | bytes 589828
  6.3 10.5 %collective-permute-start.2 = (bf16[128,768]{1,0:T(8,128)(2,1)S(1)}, bf16[128,768]{1,0:T(8,128)(2,1)S(1)}, u32[]{:S(2)}, u32[]{:S(2)}) collective-permute-start(bf16[128,768]{1,0:T(8,128)(2,1)S(1)} %bitcast.12), channel_id=1, source_target_pairs={{0,1},{1,2},{2,3},{3,0},{4,5},{5,6},{6,7},{7,4},{8,9},{9,10},{10,1... | collective-permute-start | bytes 589832 | tf_op jit(solution)/shard_map/ppermute | solution.py:231
  6.6 10.3 %collective-permute-start.4 = (bf16[128,768]{1,0:T(8,128)(2,1)S(1)}, bf16[128,768]{1,0:T(8,128)(2,1)S(1)}, u32[]{:S(2)}, u32[]{:S(2)}) collective-permute-start(bf16[128,768]{1,0:T(8,128)(2,1)S(1)} %bitcast.4), channel_id=1, source_target_pairs={{0,2},{1,3},{2,0},{3,1},{4,6},{5,7},{6,4},{7,5},{8,10},{9,11},{10,... | collective-permute-start | bytes 589832 | tf_op jit(solution)/shard_map/ppermute | solution.py:229
  8.5 9.4 %collective-permute-start.3 = (bf16[128,768]{1,0:T(8,128)(2,1)S(1)}, bf16[128,768]{1,0:T(8,128)(2,1)S(1)}, u32[]{:S(2)}, u32[]{:S(2)}) collective-permute-start(bf16[128,768]{1,0:T(8,128)(2,1)S(1)} %bitcast.5), channel_id=1, source_target_pairs={{0,1},{1,2},{2,3},{3,0},{4,5},{5,6},{6,7},{7,4},{8,9},{9,10},{10,1... | collective-permute-start | bytes 589832 | tf_op jit(solution)/shard_map/ppermute | solution.py:230
  10.7 13.3 %all-to-all-start = ((f32[32,1,128]{2,1,0:T(1,128)}), f32[32,1,128]{2,1,0:T(1,128)S(1)}, u32[]{:S(2)}, u32[]{:S(2)}) async-start(f32[32,1,128]{2,1,0:T(1,128)} %get-tuple-element.21), calls=%async_computation | async-start | bytes 32768 | tf_op jit(solution)/shard_map/all_to_all | solution.py:246
  24.3 0.7 %copy-start.2 = (f32[6]{0:T(128)}, f32[6]{0:T(128)S(1)}, u32[]{:S(2)}) copy-start(f32[6]{0:T(128)S(1)} %sqrt.3) | copy-start | bytes 76

commit v8 on v7

--- a/solution.py
+++ b/solution.py
@@ -18,6 +18,7 @@
 SCALE = HEAD_SIZE ** (-0.5)
 SCALE_2 = SCALE * math.log2(math.e)
 MASKED = -1e30
+KEY_HEAD_LANE = 64
 NT = (((1,), (1,)), ((), ()))
 
 
@@ -66,12 +67,18 @@
             max_ref[at, :] = largest
 
 
-def store_head_maxima(head_max_ref, max_ref):
+def store_clipped(clipped_ref, max_ref):
     largest = max_ref[...]
     rows = largest.shape[1]
-    padded = jnp.concatenate([largest, largest, largest], axis=0)[:rows]
+    groups = [
+        jnp.max(largest[c * GROUP : (c + 1) * GROUP, :], axis=0, keepdims=True)
+        for c in range(KEY_VALUE_HEADS)
+    ]
+    spare = KEY_HEAD_LANE - QUERY_HEADS
+    padded = jnp.concatenate([largest, largest[:spare], *groups, largest, largest], axis=0)[:rows]
     head_max = jnp.max(padded.T, axis=0, keepdims=True) * SCALE
-    head_max_ref[...] = jnp.broadcast_to(head_max[None], head_max_ref.shape)
+    clipped = clip_level / jnp.maximum(head_max, clip_level)
+    clipped_ref[...] = jnp.broadcast_to(clipped[None], clipped_ref.shape)
 
 
 def load_kernel(
@@ -98,14 +105,14 @@
         raise_maxima(refs[-1], partner_ref[0], key_ref, bias_ref, 4, max_ref)
 
 
-def next_kernel(place, bias_ref, q_ref, before_ref, key_ref, max_ref, *head_max_refs):
+def next_kernel(place, bias_ref, q_ref, before_ref, key_ref, max_ref, *clipped_refs):
     raise_maxima(max_ref, q_ref, key_ref, bias_ref, place, before_ref)
-    for head_max_ref in head_max_refs:
-        store_head_maxima(head_max_ref, max_ref)
+    for clipped_ref in clipped_refs:
+        store_clipped(clipped_ref, max_ref)
 
 
 def last_paired_kernel(
-    bias_ref, q_ref, partner_ref, before_ref, near_ref, key_ref, max_ref, head_max_ref, all_ref
+    bias_ref, q_ref, partner_ref, before_ref, near_ref, key_ref, max_ref, clipped_ref, all_ref
 ):
     raise_maxima(max_ref, q_ref, key_ref, bias_ref, 2, before_ref)
     all_ref[...] = jnp.maximum(near_ref[...], max_ref[...])
@@ -114,7 +121,7 @@
     def _():
         raise_maxima(all_ref, partner_ref, key_ref, bias_ref, 3, all_ref)
 
-    store_head_maxima(head_max_ref, all_ref)
+    store_clipped(clipped_ref, all_ref)
 
 
 def mix_kernel(blocks, bias_ref, q_ref, row_max_ref, *refs):
@@ -229,7 +236,7 @@
     far_values = lax.ppermute(values, "seq", across)
     near_values = lax.ppermute(values, "seq", rotate)
     near_keys = lax.ppermute(sent_keys, "seq", rotate)
-    row_max, head_max = call(
+    row_max, clipped = call(
         last_paired_kernel,
         "last_maxima",
         (max_shape, pltpu.VMEM((devices, 1, rows), jnp.float32)),
@@ -243,7 +250,7 @@
         in_vmem(far_keys),
         scratch=[pltpu.VMEM(max_shape.shape, jnp.float32)],
     )
-    everyone = lax.all_to_all(head_max, ("dp", "seq"), 0, 0)
+    everyone = lax.all_to_all(clipped, ("dp", "seq"), 0, 0)
     (attended,) = call(
         mix_paired_kernel,
         "mix",
@@ -281,7 +288,7 @@
     value_blocks = {d: passed_along(sent_values, d) for d in distances}
     for d in distances:
         out_shape = (max_shape,) + ((float32(devices, 1, rows),) if d == 1 else ())
-        row_max, *head_max = call(
+        row_max, *clipped = call(
             functools.partial(next_kernel, d),
             f"maxima_{d}",
             out_shape,
@@ -292,7 +299,7 @@
             row_max,
             key_blocks[d],
         )
-    everyone = lax.all_to_all(head_max[0], ("dp", "seq"), 0, 0)
+    everyone = lax.all_to_all(clipped[0], ("dp", "seq"), 0, 0)
     (attended,) = call(
         functools.partial(mix_kernel, reach + 1),
         "mix",
@@ -310,11 +317,9 @@
     return attended, everyone
 
 
-def clip_factors(head_max):
-    clipped_logits = clip_level / jnp.maximum(head_max, clip_level)
-    key_head_factor = jnp.sqrt(jnp.min(clipped_logits.reshape(KEY_VALUE_HEADS, GROUP), axis=1))
-    query_factor = clipped_logits / jnp.repeat(key_head_factor, GROUP)
-    return (query_factor, key_head_factor)
+def clip_factors(clipped, smallest):
+    key_head_factor = jnp.sqrt(smallest)
+    return (clipped / jnp.repeat(key_head_factor, GROUP), key_head_factor)
 
 
 def local(queries, keys, values, segments):
@@ -328,8 +333,9 @@
     else:
         attended, everyone = plan_of_rotations(*arrays, reach, shards)
     everyone, attended = lax.optimization_barrier((everyone, attended))
+    clipped = jnp.min(everyone[:, 0, :], axis=0)
     query_factor, key_head_factor = clip_factors(
-        jnp.max(everyone[:, 0, :QUERY_HEADS], axis=0)
+        clipped[:QUERY_HEADS], clipped[KEY_HEAD_LANE : KEY_HEAD_LANE + KEY_VALUE_HEADS]
     )
     return (attended[None], query_factor, key_head_factor)
 

time: 25.2 us -> 25 us (level)
    div x2 -> x1, other arithmetic: 0.53 us -> 0.53 us  [clip_factors(): return (clipped / jnp.repeat(key_head_factor, GROUP), key_head_factor)]
  transfers between devices with their start and end apart: 6 -> 6, of which waited for: 3 -> 3; matrix products, arithmetic and copies ran while one was open for 0% -> 0% of each run, Pallas kernels for 33% -> 34%
where the time goes in v8:
time: 25 us; the launch traced here: 24.8 us
  starting transfers between devices  11.3 us (45%)
  Pallas kernels  8.32 us (33%)
  waiting for transfers between devices  3.66 us (15%)
  between operations  0.71 us (3%)
  other arithmetic  0.58 us (2%)
  local copies, waits for them, and re-layouts  0.25 us (1%)
    pallas_call x3, Pallas kernels, call(): pl.pallas_call(kernel, out_shape=out_shape, in_specs=[VMEM] * len(arrays)...  6.76 us
    all_to_all x1, starting transfers between devices, plan_of_pairs(): everyone = lax.all_to_all(clipped, ('dp', 'seq'), 0, 0)  6.11 us
    ppermute x1, starting transfers between devices, plan_of_pairs(): far_keys = lax.ppermute(keys, 'seq', across)  2.56 us
    ppermute x1, starting transfers between devices, plan_of_pairs(): far_values = lax.ppermute(values, 'seq', across)  1.91 us
    all_to_all x1, waiting for transfers between devices, plan_of_pairs(): everyone = lax.all_to_all(clipped, ('dp', 'seq'), 0, 0)  1.75 us
    pallas_call x1, Pallas kernels, load(): pl.pallas_call(functools.partial(load_kernel, shards, pairs), out_shape=(...  1.56 us
    ppermute x1, waiting for transfers between devices, plan_of_pairs(): far_keys = lax.ppermute(keys, 'seq', across)  0.95 us
    ppermute x1, waiting for transfers between devices, plan_of_pairs(): near_values = lax.ppermute(values, 'seq', rotate)  0.95 us
  transfers between devices with their start and end apart: 6, of which 3 were waited for; matrix products, arithmetic and copies ran while one was open for 0% of the time, Pallas kernels for 34%

profile of v8, /device:TPU:0, one launch (start us, length us, event | category | flops | bytes accessed | tf_op | source)
XLA Modules:
  0.0 24.8 jit_solution(17410769860104301748)
XLA Ops:
  0.6 0.5 %collective-permute-start = (bf16[128,6144]{1,0:T(8,128)(2,1)}, bf16[128,6144]{1,0:T(8,128)(2,1)S(1)}, u32[]{:S(2)}, u32[]{:S(2)}) collective-permute-start(bf16[128,6144]{1,0:T(8,128)(2,1)} %bitcast.7), channel_id=1, source_target_pairs={{0,1},{1,0},{2,3},{3,2},{4,5},{5,4},{6,7},{7,6},{8,9},{9,8},{10,11... | collective-permute-start | bytes 4718600 | tf_op jit(solution)/shard_map/ppermute | solution.py:220
  1.1 2.6 %collective-permute-start.1 = (bf16[128,768]{1,0:T(8,128)(2,1)}, bf16[128,768]{1,0:T(8,128)(2,1)S(1)}, u32[]{:S(2)}, u32[]{:S(2)}) collective-permute-start(bf16[128,768]{1,0:T(8,128)(2,1)} %bitcast.10), channel_id=1, source_target_pairs={{0,2},{1,3},{2,0},{3,1},{4,6},{5,7},{6,4},{7,5},{8,10},{9,11},{10,... | collective-permute-start | bytes 589832 | tf_op jit(solution)/shard_map/ppermute | solution.py:219
  3.7 1.6 %load.1 = (f32[640,128]{1,0:T(8,128)S(1)}, bf16[128,6144]{1,0:T(8,128)(2,1)S(1)}, bf16[128,768]{1,0:T(8,128)(2,1)S(1)}) custom-call(s32[1,512]{1,0:T(1,128)} %seg_hbm.1, bf16[128,6144]{1,0:T(8,128)(2,1)} %bitcast.8, bf16[128,768]{1,0:T(8,128)(2,1)} %bitcast.11), custom_call_target="tpu_custom_call" | custom-call | bytes 1769472 | tf_op jit(solution)/shard_map/load/pallas_call | solution.py:181
  5.3 0.0 collective-permute-done.refs_0_.partner_ref
  5.3 0.0 copy-start.1
  5.3 0.0 copy-start
  5.3 1.0 %first_maxima.1 = (f32[48,128]{1,0:T(8,128)S(1)}, f32[48,128]{1,0:T(8,128)S(1)}) custom-call(f32[640,128]{1,0:T(8,128)S(1)} %get-tuple-element.15.bias_ref, bf16[128,6144]{1,0:T(8,128)(2,1)S(1)} %get-tuple-element.16.q_ref, bf16[128,768]{1,0:T(8,128)(2,1)S(1)} %get-tuple-element.17.key_ref.own, bf16[128,6144]{1,0:T(8,128)(2,1)S(1)} %collective-permute-done.refs_0_.partner_ref), custom_call_target="tpu_custom_call" | custom-call | flops 402653184 | bytes 1572864 | tf_op jit(solution)/shard_map/first_maxima/pallas_call | solution.py:159
  6.3 0.0 copy-done.1
  6.3 0.2 collective-permute-start.2
  6.6 0.0 copy-done
  6.6 1.9 %collective-permute-start.4 = (bf16[128,768]{1,0:T(8,128)(2,1)S(1)}, bf16[128,768]{1,0:T(8,128)(2,1)S(1)}, u32[]{:S(2)}, u32[]{:S(2)}) collective-permute-start(bf16[128,768]{1,0:T(8,128)(2,1)S(1)} %bitcast.4), channel_id=1, source_target_pairs={{0,2},{1,3},{2,0},{3,1},{4,6},{5,7},{6,4},{7,5},{8,10},{9,11},{10,... | collective-permute-start | bytes 589832 | tf_op jit(solution)/shard_map/ppermute | solution.py:236
  8.5 0.0 collective-permute-start.3
  8.5 1.0 %collective-permute-done.1.key_ref.far = bf16[128,768]{1,0:T(8,128)(2,1)S(1)} collective-permute-done((bf16[128,768]{1,0:T(8,128)(2,1)}, bf16[128,768]{1,0:T(8,128)(2,1)S(1)}, u32[]{:S(2)}, u32[]{:S(2)}) %collective-permute-start.1) | collective-permute-done | bytes 196640 | tf_op jit(solution)/shard_map/ppermute | solution.py:219
  9.4 1.3 %last_maxima.1 = (f32[48,128]{1,0:T(8,128)S(1)}, f32[32,1,128]{2,1,0:T(1,128)}) custom-call(f32[640,128]{1,0:T(8,128)S(1)} %get-tuple-element.15.bias_ref, bf16[128,6144]{1,0:T(8,128)(2,1)S(1)} %get-tuple-element.16.q_ref, bf16[128,6144]{1,0:T(8,128)(2,1)S(1)} %collective-permute-done.refs_0_.partner_ref, f32[48,128]{1,0:T(8,128)S(1)} %get-tuple-element.18.before_ref, ...), custom_call_target="tpu_custom_call" | custom-call | flops 402653184 | bytes 1572864 | tf_op jit(solution)/shard_map/last_maxima/pallas_call | solution.py:159
  10.8 6.1 %all-to-all-start = ((f32[32,1,128]{2,1,0:T(1,128)}), f32[32,1,128]{2,1,0:T(1,128)S(1)}, u32[]{:S(2)}, u32[]{:S(2)}) async-start(f32[32,1,128]{2,1,0:T(1,128)} %get-tuple-element.21), calls=%async_computation | async-start | bytes 32768 | tf_op jit(solution)/shard_map/all_to_all | solution.py:253
  16.9 0.0 collective-permute-done.2.near
  16.9 0.0 collective-permute-done.4.refs_2_
  16.9 0.9 %collective-permute-done.3.refs_1_ = bf16[128,768]{1,0:T(8,128)(2,1)S(1)} collective-permute-done((bf16[128,768]{1,0:T(8,128)(2,1)S(1)}, bf16[128,768]{1,0:T(8,128)(2,1)S(1)}, u32[]{:S(2)}, u32[]{:S(2)}) %collective-permute-start.3) | collective-permute-done | bytes 196640 | tf_op jit(solution)/shard_map/ppermute | solution.py:237
  17.8 4.4 %mix.1 = bf16[128,6144]{1,0:T(8,128)(2,1)} custom-call(f32[640,128]{1,0:T(8,128)S(1)} %get-tuple-element.15.bias_ref, bf16[128,6144]{1,0:T(8,128)(2,1)S(1)} %get-tuple-element.16.q_ref, f32[48,128]{1,0:T(8,128)S(1)} %get-tuple-element.22.row_max_ref, bf16[128,768]{1,0:T(8,128)(2,1)S(1)} %get-tuple-element.17.key_ref.own, ...), custom_call_target="tpu_custom_call" | custom-call | flops 1207959552 | bytes 3145728 | tf_op jit(solution)/shard_map/mix/pallas_call | solution.py:159
  22.3 1.8 %all-to-all-done = f32[32,1,128]{2,1,0:T(1,128)S(1)} async-done(((f32[32,1,128]{2,1,0:T(1,128)}), f32[32,1,128]{2,1,0:T(1,128)S(1)}, u32[]{:S(2)}, u32[]{:S(2)}) %all-to-all-start) | async-done | bytes 16416 | tf_op jit(solution)/shard_map/all_to_all | solution.py:253
  24.0 0.1 reduce_min.9
  24.1 0.1 slice_sqrt_fusion
  24.2 0.0 copy-start.2
  24.2 0.1 broadcast_in_dim.7
  24.2 0.1 reshape.9
  24.3 0.5 %slice_divide_fusion = f32[48]{0:T(128)} fusion(f32[48]{0:T(128)S(1)} %reshape.9, f32[128]{0:T(128)S(1)} %reduce_min.9), kind=kLoop, calls=%fused_computation.1 | loop fusion | flops 48 | bytes 576 | tf_op jit(solution)/shard_map/div | solution.py:322
  24.8 0.0 copy-done.2
Async XLA Ops:
  0.6 4.7 %collective-permute-start = (bf16[128,6144]{1,0:T(8,128)(2,1)}, bf16[128,6144]{1,0:T(8,128)(2,1)S(1)}, u32[]{:S(2)}, u32[]{:S(2)}) collective-permute-start(bf16[128,6144]{1,0:T(8,128)(2,1)} %bitcast.7), channel_id=1, source_target_pairs={{0,1},{1,0},{2,3},{3,2},{4,5},{5,4},{6,7},{7,6},{8,9},{9,8},{10,11... | collective-permute-start | bytes 4718600 | tf_op jit(solution)/shard_map/ppermute | solution.py:220
  1.1 8.3 %collective-permute-start.1 = (bf16[128,768]{1,0:T(8,128)(2,1)}, bf16[128,768]{1,0:T(8,128)(2,1)S(1)}, u32[]{:S(2)}, u32[]{:S(2)}) collective-permute-start(bf16[128,768]{1,0:T(8,128)(2,1)} %bitcast.10), channel_id=1, source_target_pairs={{0,2},{1,3},{2,0},{3,1},{4,6},{5,7},{6,4},{7,5},{8,10},{9,11},{10,... | collective-permute-start | bytes 589832 | tf_op jit(solution)/shard_map/ppermute | solution.py:219
  5.3 1.0 %copy-start.1 = (bf16[1,128,768]{2,1,0:T(8,128)(2,1)S(1)}, bf16[1,128,768]{2,1,0:T(8,128)(2,1)}, u32[]{:S(2)}) copy-start(bf16[1,128,768]{2,1,0:T(8,128)(2,1)} %param.5) | copy-start | bytes 589828
  5.3 1.3 %copy-start = (bf16[1,128,768]{2,1,0:T(8,128)(2,1)S(1)}, bf16[1,128,768]{2,1,0:T(8,128)(2,1)}, u32[]{:S(2)}) copy-start(bf16[1,128,768]{2,1,0:T(8,128)(2,1)} %param.6) | copy-start | bytes 589828
  6.3 10.5 %collective-permute-start.2 = (bf16[128,768]{1,0:T(8,128)(2,1)S(1)}, bf16[128,768]{1,0:T(8,128)(2,1)S(1)}, u32[]{:S(2)}, u32[]{:S(2)}) collective-permute-start(bf16[128,768]{1,0:T(8,128)(2,1)S(1)} %bitcast.12), channel_id=1, source_target_pairs={{0,1},{1,2},{2,3},{3,0},{4,5},{5,6},{6,7},{7,4},{8,9},{9,10},{10,1... | collective-permute-start | bytes 589832 | tf_op jit(solution)/shard_map/ppermute | solution.py:238
  6.6 10.3 %collective-permute-start.4 = (bf16[128,768]{1,0:T(8,128)(2,1)S(1)}, bf16[128,768]{1,0:T(8,128)(2,1)S(1)}, u32[]{:S(2)}, u32[]{:S(2)}) collective-permute-start(bf16[128,768]{1,0:T(8,128)(2,1)S(1)} %bitcast.4), channel_id=1, source_target_pairs={{0,2},{1,3},{2,0},{3,1},{4,6},{5,7},{6,4},{7,5},{8,10},{9,11},{10,... | collective-permute-start | bytes 589832 | tf_op jit(solution)/shard_map/ppermute | solution.py:236
  8.5 9.4 %collective-permute-start.3 = (bf16[128,768]{1,0:T(8,128)(2,1)S(1)}, bf16[128,768]{1,0:T(8,128)(2,1)S(1)}, u32[]{:S(2)}, u32[]{:S(2)}) collective-permute-start(bf16[128,768]{1,0:T(8,128)(2,1)S(1)} %bitcast.5), channel_id=1, source_target_pairs={{0,1},{1,2},{2,3},{3,0},{4,5},{5,6},{6,7},{7,4},{8,9},{9,10},{10,1... | collective-permute-start | bytes 589832 | tf_op jit(solution)/shard_map/ppermute | solution.py:237
  10.8 13.3 %all-to-all-start = ((f32[32,1,128]{2,1,0:T(1,128)}), f32[32,1,128]{2,1,0:T(1,128)S(1)}, u32[]{:S(2)}, u32[]{:S(2)}) async-start(f32[32,1,128]{2,1,0:T(1,128)} %get-tuple-element.21), calls=%async_computation | async-start | bytes 32768 | tf_op jit(solution)/shard_map/all_to_all | solution.py:253
  24.2 0.7 %copy-start.2 = (f32[6]{0:T(128)}, f32[6]{0:T(128)S(1)}, u32[]{:S(2)}) copy-start(f32[6]{0:T(128)S(1)} %slice_sqrt_fusion) | copy-start | bytes 76

commit v9 on v8

--- a/solution.py
+++ b/solution.py
@@ -78,7 +78,7 @@
     padded = jnp.concatenate([largest, largest[:spare], *groups, largest, largest], axis=0)[:rows]
     head_max = jnp.max(padded.T, axis=0, keepdims=True) * SCALE
     clipped = clip_level / jnp.maximum(head_max, clip_level)
-    clipped_ref[...] = jnp.broadcast_to(clipped[None], clipped_ref.shape)
+    clipped_ref[...] = jnp.broadcast_to(clipped, clipped_ref.shape)
 
 
 def load_kernel(
@@ -239,7 +239,7 @@
     row_max, clipped = call(
         last_paired_kernel,
         "last_maxima",
-        (max_shape, pltpu.VMEM((devices, 1, rows), jnp.float32)),
+        (max_shape, float32(devices, rows)),
         2,
         1,
         bias,
@@ -250,7 +250,7 @@
         in_vmem(far_keys),
         scratch=[pltpu.VMEM(max_shape.shape, jnp.float32)],
     )
-    everyone = lax.all_to_all(clipped, ("dp", "seq"), 0, 0)
+    everyone = lax.all_to_all(clipped, ("dp", "seq"), 0, 0, tiled=True)
     (attended,) = call(
         mix_paired_kernel,
         "mix",
@@ -287,7 +287,7 @@
     sent_values, bias = lax.optimization_barrier((values, bias))
     value_blocks = {d: passed_along(sent_values, d) for d in distances}
     for d in distances:
-        out_shape = (max_shape,) + ((float32(devices, 1, rows),) if d == 1 else ())
+        out_shape = (max_shape,) + ((float32(devices, rows),) if d == 1 else ())
         row_max, *clipped = call(
             functools.partial(next_kernel, d),
             f"maxima_{d}",
@@ -299,7 +299,7 @@
             row_max,
             key_blocks[d],
         )
-    everyone = lax.all_to_all(clipped[0], ("dp", "seq"), 0, 0)
+    everyone = lax.all_to_all(clipped[0], ("dp", "seq"), 0, 0, tiled=True)
     (attended,) = call(
         functools.partial(mix_kernel, reach + 1),
         "mix",
@@ -333,7 +333,7 @@
     else:
         attended, everyone = plan_of_rotations(*arrays, reach, shards)
     everyone, attended = lax.optimization_barrier((everyone, attended))
-    clipped = jnp.min(everyone[:, 0, :], axis=0)
+    clipped = jnp.min(everyone, axis=0)
     query_factor, key_head_factor = clip_factors(
         clipped[:QUERY_HEADS], clipped[KEY_HEAD_LANE : KEY_HEAD_LANE + KEY_VALUE_HEADS]
     )

time: 25 us -> 25 us (level)
  no operation moved by 1% of the time
where the time goes in v9:
time: 25 us; the launch traced here: 24.8 us
  starting transfers between devices  11.3 us (45%)
  Pallas kernels  8.32 us (33%)
  waiting for transfers between devices  3.66 us (15%)
  between operations  0.71 us (3%)
  other arithmetic  0.55 us (2%)
  local copies, waits for them, and re-layouts  0.25 us (1%)
    pallas_call x3, Pallas kernels, call(): pl.pallas_call(kernel, out_shape=out_shape, in_specs=[VMEM] * len(arrays)...  6.76 us
    all_to_all x1, starting transfers between devices, plan_of_pairs(): everyone = lax.all_to_all(clipped, ('dp', 'seq'), 0, 0, tiled=True)  6.11 us
    ppermute x1, starting transfers between devices, plan_of_pairs(): far_keys = lax.ppermute(keys, 'seq', across)  2.56 us
    ppermute x1, starting transfers between devices, plan_of_pairs(): far_values = lax.ppermute(values, 'seq', across)  1.91 us
    all_to_all x1, waiting for transfers between devices, plan_of_pairs(): everyone = lax.all_to_all(clipped, ('dp', 'seq'), 0, 0, tiled=True)  1.75 us
    pallas_call x1, Pallas kernels, load(): pl.pallas_call(functools.partial(load_kernel, shards, pairs), out_shape=(...  1.56 us
    ppermute x1, waiting for transfers between devices, plan_of_pairs(): near_values = lax.ppermute(values, 'seq', rotate)  0.95 us
    ppermute x1, waiting for transfers between devices, plan_of_pairs(): far_keys = lax.ppermute(keys, 'seq', across)  0.95 us
  transfers between devices with their start and end apart: 6, of which 3 were waited for; matrix products, arithmetic and copies ran while one was open for 0% of the time, Pallas kernels for 34%

profile of v9, /device:TPU:0, one launch (start us, length us, event | category | flops | bytes accessed | tf_op | source)
XLA Modules:
  0.0 24.8 jit_solution(7501776445385782553)
XLA Ops:
  0.6 0.5 %collective-permute-start = (bf16[128,6144]{1,0:T(8,128)(2,1)}, bf16[128,6144]{1,0:T(8,128)(2,1)S(1)}, u32[]{:S(2)}, u32[]{:S(2)}) collective-permute-start(bf16[128,6144]{1,0:T(8,128)(2,1)} %bitcast.11), channel_id=1, source_target_pairs={{0,1},{1,0},{2,3},{3,2},{4,5},{5,4},{6,7},{7,6},{8,9},{9,8},{10,11... | collective-permute-start | bytes 4718600 | tf_op jit(solution)/shard_map/ppermute | solution.py:220
  1.1 2.6 %collective-permute-start.1 = (bf16[128,768]{1,0:T(8,128)(2,1)}, bf16[128,768]{1,0:T(8,128)(2,1)S(1)}, u32[]{:S(2)}, u32[]{:S(2)}) collective-permute-start(bf16[128,768]{1,0:T(8,128)(2,1)} %bitcast.14), channel_id=1, source_target_pairs={{0,2},{1,3},{2,0},{3,1},{4,6},{5,7},{6,4},{7,5},{8,10},{9,11},{10,... | collective-permute-start | bytes 589832 | tf_op jit(solution)/shard_map/ppermute | solution.py:219
  3.7 1.6 %load.1 = (f32[640,128]{1,0:T(8,128)S(1)}, bf16[128,6144]{1,0:T(8,128)(2,1)S(1)}, bf16[128,768]{1,0:T(8,128)(2,1)S(1)}) custom-call(s32[1,512]{1,0:T(1,128)} %seg_hbm.1, bf16[128,6144]{1,0:T(8,128)(2,1)} %bitcast.12, bf16[128,768]{1,0:T(8,128)(2,1)} %bitcast.15), custom_call_target="tpu_custom_call" | custom-call | bytes 1769472 | tf_op jit(solution)/shard_map/load/pallas_call | solution.py:181
  5.3 0.0 collective-permute-done.refs_0_.partner_ref
  5.3 0.0 copy-start.1
  5.3 0.0 copy-start
  5.3 1.0 %first_maxima.1 = (f32[48,128]{1,0:T(8,128)S(1)}, f32[48,128]{1,0:T(8,128)S(1)}) custom-call(f32[640,128]{1,0:T(8,128)S(1)} %get-tuple-element.15.bias_ref, bf16[128,6144]{1,0:T(8,128)(2,1)S(1)} %get-tuple-element.16.q_ref, bf16[128,768]{1,0:T(8,128)(2,1)S(1)} %get-tuple-element.17.key_ref.own, bf16[128,6144]{1,0:T(8,128)(2,1)S(1)} %collective-permute-done.refs_0_.partner_ref), custom_call_target="tpu_custom_call" | custom-call | flops 402653184 | bytes 1572864 | tf_op jit(solution)/shard_map/first_maxima/pallas_call | solution.py:159
  6.3 0.0 copy-done.1
  6.3 0.2 collective-permute-start.2
  6.6 0.0 copy-done
  6.6 1.9 %collective-permute-start.4 = (bf16[128,768]{1,0:T(8,128)(2,1)S(1)}, bf16[128,768]{1,0:T(8,128)(2,1)S(1)}, u32[]{:S(2)}, u32[]{:S(2)}) collective-permute-start(bf16[128,768]{1,0:T(8,128)(2,1)S(1)} %bitcast.8), channel_id=1, source_target_pairs={{0,2},{1,3},{2,0},{3,1},{4,6},{5,7},{6,4},{7,5},{8,10},{9,11},{10,... | collective-permute-start | bytes 589832 | tf_op jit(solution)/shard_map/ppermute | solution.py:236
  8.5 0.0 collective-permute-start.3
  8.5 1.0 %collective-permute-done.1.key_ref.far = bf16[128,768]{1,0:T(8,128)(2,1)S(1)} collective-permute-done((bf16[128,768]{1,0:T(8,128)(2,1)}, bf16[128,768]{1,0:T(8,128)(2,1)S(1)}, u32[]{:S(2)}, u32[]{:S(2)}) %collective-permute-start.1) | collective-permute-done | bytes 196640 | tf_op jit(solution)/shard_map/ppermute | solution.py:219
  9.4 1.3 %last_maxima.1 = (f32[48,128]{1,0:T(8,128)S(1)}, f32[32,128]{1,0:T(8,128)}) custom-call(f32[640,128]{1,0:T(8,128)S(1)} %get-tuple-element.15.bias_ref, bf16[128,6144]{1,0:T(8,128)(2,1)S(1)} %get-tuple-element.16.q_ref, bf16[128,6144]{1,0:T(8,128)(2,1)S(1)} %collective-permute-done.refs_0_.partner_ref, f32[48,128]{1,0:T(8,128)S(1)} %get-tuple-element.18.before_ref, ...), custom_call_target="tpu_custom_call" | custom-call | flops 402653184 | bytes 1572864 | tf_op jit(solution)/shard_map/last_maxima/pallas_call | solution.py:159
  10.8 6.1 %all-to-all-start = ((f32[32,1,128]{2,1,0:T(1,128)}), f32[32,1,128]{2,1,0:T(1,128)S(1)}, u32[]{:S(2)}, u32[]{:S(2)}) async-start(f32[32,1,128]{2,1,0:T(1,128)} %bitcast.4), calls=%async_computation | async-start | bytes 32768 | tf_op jit(solution)/shard_map/all_to_all | solution.py:253
  16.9 0.0 collective-permute-done.2.near
  16.9 0.0 collective-permute-done.4.refs_2_
  16.9 1.0 %collective-permute-done.3.refs_1_ = bf16[128,768]{1,0:T(8,128)(2,1)S(1)} collective-permute-done((bf16[128,768]{1,0:T(8,128)(2,1)S(1)}, bf16[128,768]{1,0:T(8,128)(2,1)S(1)}, u32[]{:S(2)}, u32[]{:S(2)}) %collective-permute-start.3) | collective-permute-done | bytes 196640 | tf_op jit(solution)/shard_map/ppermute | solution.py:237
  17.8 4.4 %mix.1 = bf16[128,6144]{1,0:T(8,128)(2,1)} custom-call(f32[640,128]{1,0:T(8,128)S(1)} %get-tuple-element.15.bias_ref, bf16[128,6144]{1,0:T(8,128)(2,1)S(1)} %get-tuple-element.16.q_ref, f32[48,128]{1,0:T(8,128)S(1)} %get-tuple-element.22.row_max_ref, bf16[128,768]{1,0:T(8,128)(2,1)S(1)} %get-tuple-element.17.key_ref.own, ...), custom_call_target="tpu_custom_call" | custom-call | flops 1207959552 | bytes 3145728 | tf_op jit(solution)/shard_map/mix/pallas_call | solution.py:159
  22.3 1.7 %all-to-all-done = f32[32,1,128]{2,1,0:T(1,128)S(1)} async-done(((f32[32,1,128]{2,1,0:T(1,128)}), f32[32,1,128]{2,1,0:T(1,128)S(1)}, u32[]{:S(2)}, u32[]{:S(2)}) %all-to-all-start) | async-done | bytes 16416 | tf_op jit(solution)/shard_map/all_to_all | solution.py:253
  24.0 0.1 slice_sqrt_fusion
  24.1 0.0 copy-start.2
  24.1 0.1 broadcast_in_dim.7
  24.2 0.1 reshape.11
  24.3 0.5 %slice_divide_fusion = f32[48]{0:T(128)} fusion(f32[48]{0:T(128)S(1)} %reshape.11, f32[128]{0:T(128)S(1)} %reduce_min.9), kind=kLoop, calls=%fused_computation.1 | loop fusion | flops 48 | bytes 576 | tf_op jit(solution)/shard_map/div | solution.py:322
  24.8 0.0 copy-done.2
  (1 shorter events, 0.0 us)
Async XLA Ops:
  0.6 4.7 %collective-permute-start = (bf16[128,6144]{1,0:T(8,128)(2,1)}, bf16[128,6144]{1,0:T(8,128)(2,1)S(1)}, u32[]{:S(2)}, u32[]{:S(2)}) collective-permute-start(bf16[128,6144]{1,0:T(8,128)(2,1)} %bitcast.11), channel_id=1, source_target_pairs={{0,1},{1,0},{2,3},{3,2},{4,5},{5,4},{6,7},{7,6},{8,9},{9,8},{10,11... | collective-permute-start | bytes 4718600 | tf_op jit(solution)/shard_map/ppermute | solution.py:220
  1.1 8.3 %collective-permute-start.1 = (bf16[128,768]{1,0:T(8,128)(2,1)}, bf16[128,768]{1,0:T(8,128)(2,1)S(1)}, u32[]{:S(2)}, u32[]{:S(2)}) collective-permute-start(bf16[128,768]{1,0:T(8,128)(2,1)} %bitcast.14), channel_id=1, source_target_pairs={{0,2},{1,3},{2,0},{3,1},{4,6},{5,7},{6,4},{7,5},{8,10},{9,11},{10,... | collective-permute-start | bytes 589832 | tf_op jit(solution)/shard_map/ppermute | solution.py:219
  5.3 1.0 %copy-start.1 = (bf16[1,128,768]{2,1,0:T(8,128)(2,1)S(1)}, bf16[1,128,768]{2,1,0:T(8,128)(2,1)}, u32[]{:S(2)}) copy-start(bf16[1,128,768]{2,1,0:T(8,128)(2,1)} %param.5) | copy-start | bytes 589828
  5.3 1.3 %copy-start = (bf16[1,128,768]{2,1,0:T(8,128)(2,1)S(1)}, bf16[1,128,768]{2,1,0:T(8,128)(2,1)}, u32[]{:S(2)}) copy-start(bf16[1,128,768]{2,1,0:T(8,128)(2,1)} %param.6) | copy-start | bytes 589828
  6.3 10.5 %collective-permute-start.2 = (bf16[128,768]{1,0:T(8,128)(2,1)S(1)}, bf16[128,768]{1,0:T(8,128)(2,1)S(1)}, u32[]{:S(2)}, u32[]{:S(2)}) collective-permute-start(bf16[128,768]{1,0:T(8,128)(2,1)S(1)} %bitcast.16), channel_id=1, source_target_pairs={{0,1},{1,2},{2,3},{3,0},{4,5},{5,6},{6,7},{7,4},{8,9},{9,10},{10,1... | collective-permute-start | bytes 589832 | tf_op jit(solution)/shard_map/ppermute | solution.py:238
  6.6 10.3 %collective-permute-start.4 = (bf16[128,768]{1,0:T(8,128)(2,1)S(1)}, bf16[128,768]{1,0:T(8,128)(2,1)S(1)}, u32[]{:S(2)}, u32[]{:S(2)}) collective-permute-start(bf16[128,768]{1,0:T(8,128)(2,1)S(1)} %bitcast.8), channel_id=1, source_target_pairs={{0,2},{1,3},{2,0},{3,1},{4,6},{5,7},{6,4},{7,5},{8,10},{9,11},{10,... | collective-permute-start | bytes 589832 | tf_op jit(solution)/shard_map/ppermute | solution.py:236
  8.5 9.4 %collective-permute-start.3 = (bf16[128,768]{1,0:T(8,128)(2,1)S(1)}, bf16[128,768]{1,0:T(8,128)(2,1)S(1)}, u32[]{:S(2)}, u32[]{:S(2)}) collective-permute-start(bf16[128,768]{1,0:T(8,128)(2,1)S(1)} %bitcast.9), channel_id=1, source_target_pairs={{0,1},{1,2},{2,3},{3,0},{4,5},{5,6},{6,7},{7,4},{8,9},{9,10},{10,1... | collective-permute-start | bytes 589832 | tf_op jit(solution)/shard_map/ppermute | solution.py:237
  10.8 13.3 %all-to-all-start = ((f32[32,1,128]{2,1,0:T(1,128)}), f32[32,1,128]{2,1,0:T(1,128)S(1)}, u32[]{:S(2)}, u32[]{:S(2)}) async-start(f32[32,1,128]{2,1,0:T(1,128)} %bitcast.4), calls=%async_computation | async-start | bytes 32768 | tf_op jit(solution)/shard_map/all_to_all | solution.py:253
  24.1 0.7 %copy-start.2 = (f32[6]{0:T(128)}, f32[6]{0:T(128)S(1)}, u32[]{:S(2)}) copy-start(f32[6]{0:T(128)S(1)} %slice_sqrt_fusion) | copy-start | bytes 76

commit v10 on v9

--- a/solution.py
+++ b/solution.py
@@ -19,6 +19,7 @@
 SCALE_2 = SCALE * math.log2(math.e)
 MASKED = -1e30
 KEY_HEAD_LANE = 64
+WIDE = 4
 NT = (((1,), (1,)), ((), ()))
 
 
@@ -52,14 +53,14 @@
 def raise_maxima(max_ref, q_ref, key_ref, bias_ref, place, floor_ref=None):
     rows = q_ref.shape[0]
     bias = bias_ref[place * rows : (place + 1) * rows, :]
-    for head in range(0, QUERY_HEADS, 2):
+    for head in range(0, QUERY_HEADS, WIDE):
         column = head // GROUP
         keys = key_ref[:, column * HEAD_SIZE : (column + 1) * HEAD_SIZE]
-        q = [q_ref[:, h * HEAD_SIZE : (h + 1) * HEAD_SIZE] for h in (head, head + 1)]
+        q = [q_ref[:, h * HEAD_SIZE : (h + 1) * HEAD_SIZE] for h in range(head, head + WIDE)]
         logits = lax.dot_general(
             keys, jnp.concatenate(q, axis=0), NT, preferred_element_type=jnp.float32
         )
-        for i in range(2):
+        for i in range(WIDE):
             at = slice(head + i, head + i + 1)
             largest = jnp.max(logits[:, i * rows : (i + 1) * rows] + bias, axis=0, keepdims=True)
             if floor_ref is not None:

time: 25 us -> 25 us (level)
  no operation moved by 1% of the time
where the time goes in v10:
time: 25 us; the launch traced here: 24.8 us
  starting transfers between devices  11.3 us (45%)
  Pallas kernels  8.32 us (33%)
  waiting for transfers between devices  3.66 us (15%)
  between operations  0.71 us (3%)
  other arithmetic  0.55 us (2%)
  local copies, waits for them, and re-layouts  0.25 us (1%)
    pallas_call x3, Pallas kernels, call(): pl.pallas_call(kernel, out_shape=out_shape, in_specs=[VMEM] * len(arrays)...  6.76 us
    all_to_all x1, starting transfers between devices, plan_of_pairs(): everyone = lax.all_to_all(clipped, ('dp', 'seq'), 0, 0, tiled=True)  6.11 us
    ppermute x1, starting transfers between devices, plan_of_pairs(): far_keys = lax.ppermute(keys, 'seq', across)  2.56 us
    ppermute x1, starting transfers between devices, plan_of_pairs(): far_values = lax.ppermute(values, 'seq', across)  1.91 us
    all_to_all x1, waiting for transfers between devices, plan_of_pairs(): everyone = lax.all_to_all(clipped, ('dp', 'seq'), 0, 0, tiled=True)  1.74 us
    pallas_call x1, Pallas kernels, load(): pl.pallas_call(functools.partial(load_kernel, shards, pairs), out_shape=(...  1.56 us
    ppermute x1, waiting for transfers between devices, plan_of_pairs(): near_values = lax.ppermute(values, 'seq', rotate)  0.95 us
    ppermute x1, waiting for transfers between devices, plan_of_pairs(): far_keys = lax.ppermute(keys, 'seq', across)  0.95 us
  transfers between devices with their start and end apart: 6, of which 3 were waited for; matrix products, arithmetic and copies ran while one was open for 0% of the time, Pallas kernels for 34%

profile of v10, /device:TPU:0, one launch (start us, length us, event | category | flops | bytes accessed | tf_op | source)
XLA Modules:
  0.0 24.8 jit_solution(15189283290202809955)
XLA Ops:
  0.6 0.5 %collective-permute-start = (bf16[128,6144]{1,0:T(8,128)(2,1)}, bf16[128,6144]{1,0:T(8,128)(2,1)S(1)}, u32[]{:S(2)}, u32[]{:S(2)}) collective-permute-start(bf16[128,6144]{1,0:T(8,128)(2,1)} %bitcast.11), channel_id=1, source_target_pairs={{0,1},{1,0},{2,3},{3,2},{4,5},{5,4},{6,7},{7,6},{8,9},{9,8},{10,11... | collective-permute-start | bytes 4718600 | tf_op jit(solution)/shard_map/ppermute | solution.py:221
  1.1 2.6 %collective-permute-start.1 = (bf16[128,768]{1,0:T(8,128)(2,1)}, bf16[128,768]{1,0:T(8,128)(2,1)S(1)}, u32[]{:S(2)}, u32[]{:S(2)}) collective-permute-start(bf16[128,768]{1,0:T(8,128)(2,1)} %bitcast.14), channel_id=1, source_target_pairs={{0,2},{1,3},{2,0},{3,1},{4,6},{5,7},{6,4},{7,5},{8,10},{9,11},{10,... | collective-permute-start | bytes 589832 | tf_op jit(solution)/shard_map/ppermute | solution.py:220
  3.7 1.6 %load.1 = (f32[640,128]{1,0:T(8,128)S(1)}, bf16[128,6144]{1,0:T(8,128)(2,1)S(1)}, bf16[128,768]{1,0:T(8,128)(2,1)S(1)}) custom-call(s32[1,512]{1,0:T(1,128)} %seg_hbm.1, bf16[128,6144]{1,0:T(8,128)(2,1)} %bitcast.12, bf16[128,768]{1,0:T(8,128)(2,1)} %bitcast.15), custom_call_target="tpu_custom_call" | custom-call | bytes 1769472 | tf_op jit(solution)/shard_map/load/pallas_call | solution.py:182
  5.3 0.0 collective-permute-done.refs_0_.partner_ref
  5.3 0.0 copy-start.1
  5.3 0.0 copy-start
  5.3 1.0 %first_maxima.1 = (f32[48,128]{1,0:T(8,128)S(1)}, f32[48,128]{1,0:T(8,128)S(1)}) custom-call(f32[640,128]{1,0:T(8,128)S(1)} %get-tuple-element.15.bias_ref, bf16[128,6144]{1,0:T(8,128)(2,1)S(1)} %get-tuple-element.16.q_ref, bf16[128,768]{1,0:T(8,128)(2,1)S(1)} %get-tuple-element.17.key_ref.own, bf16[128,6144]{1,0:T(8,128)(2,1)S(1)} %collective-permute-done.refs_0_.partner_ref), custom_call_target="tpu_custom_call" | custom-call | flops 402653184 | bytes 1572864 | tf_op jit(solution)/shard_map/first_maxima/pallas_call | solution.py:160
  6.3 0.0 copy-done.1
  6.3 0.2 collective-permute-start.2
  6.6 0.0 copy-done
  6.6 1.9 %collective-permute-start.4 = (bf16[128,768]{1,0:T(8,128)(2,1)S(1)}, bf16[128,768]{1,0:T(8,128)(2,1)S(1)}, u32[]{:S(2)}, u32[]{:S(2)}) collective-permute-start(bf16[128,768]{1,0:T(8,128)(2,1)S(1)} %bitcast.8), channel_id=1, source_target_pairs={{0,2},{1,3},{2,0},{3,1},{4,6},{5,7},{6,4},{7,5},{8,10},{9,11},{10,... | collective-permute-start | bytes 589832 | tf_op jit(solution)/shard_map/ppermute | solution.py:237
  8.5 0.0 collective-permute-start.3
  8.5 1.0 %collective-permute-done.1.key_ref.far = bf16[128,768]{1,0:T(8,128)(2,1)S(1)} collective-permute-done((bf16[128,768]{1,0:T(8,128)(2,1)}, bf16[128,768]{1,0:T(8,128)(2,1)S(1)}, u32[]{:S(2)}, u32[]{:S(2)}) %collective-permute-start.1) | collective-permute-done | bytes 196640 | tf_op jit(solution)/shard_map/ppermute | solution.py:220
  9.4 1.3 %last_maxima.1 = (f32[48,128]{1,0:T(8,128)S(1)}, f32[32,128]{1,0:T(8,128)}) custom-call(f32[640,128]{1,0:T(8,128)S(1)} %get-tuple-element.15.bias_ref, bf16[128,6144]{1,0:T(8,128)(2,1)S(1)} %get-tuple-element.16.q_ref, bf16[128,6144]{1,0:T(8,128)(2,1)S(1)} %collective-permute-done.refs_0_.partner_ref, f32[48,128]{1,0:T(8,128)S(1)} %get-tuple-element.18.before_ref, ...), custom_call_target="tpu_custom_call" | custom-call | flops 402653184 | bytes 1572864 | tf_op jit(solution)/shard_map/last_maxima/pallas_call | solution.py:160
  10.8 6.1 %all-to-all-start = ((f32[32,1,128]{2,1,0:T(1,128)}), f32[32,1,128]{2,1,0:T(1,128)S(1)}, u32[]{:S(2)}, u32[]{:S(2)}) async-start(f32[32,1,128]{2,1,0:T(1,128)} %bitcast.4), calls=%async_computation | async-start | bytes 32768 | tf_op jit(solution)/shard_map/all_to_all | solution.py:254
  16.9 0.0 collective-permute-done.2.near
  16.9 0.0 collective-permute-done.4.refs_2_
  16.9 1.0 %collective-permute-done.3.refs_1_ = bf16[128,768]{1,0:T(8,128)(2,1)S(1)} collective-permute-done((bf16[128,768]{1,0:T(8,128)(2,1)S(1)}, bf16[128,768]{1,0:T(8,128)(2,1)S(1)}, u32[]{:S(2)}, u32[]{:S(2)}) %collective-permute-start.3) | collective-permute-done | bytes 196640 | tf_op jit(solution)/shard_map/ppermute | solution.py:238
  17.8 4.4 %mix.1 = bf16[128,6144]{1,0:T(8,128)(2,1)} custom-call(f32[640,128]{1,0:T(8,128)S(1)} %get-tuple-element.15.bias_ref, bf16[128,6144]{1,0:T(8,128)(2,1)S(1)} %get-tuple-element.16.q_ref, f32[48,128]{1,0:T(8,128)S(1)} %get-tuple-element.22.row_max_ref, bf16[128,768]{1,0:T(8,128)(2,1)S(1)} %get-tuple-element.17.key_ref.own, ...), custom_call_target="tpu_custom_call" | custom-call | flops 1207959552 | bytes 3145728 | tf_op jit(solution)/shard_map/mix/pallas_call | solution.py:160
  22.3 1.7 %all-to-all-done = f32[32,1,128]{2,1,0:T(1,128)S(1)} async-done(((f32[32,1,128]{2,1,0:T(1,128)}), f32[32,1,128]{2,1,0:T(1,128)S(1)}, u32[]{:S(2)}, u32[]{:S(2)}) %all-to-all-start) | async-done | bytes 16416 | tf_op jit(solution)/shard_map/all_to_all | solution.py:254
  24.0 0.1 slice_sqrt_fusion
  24.1 0.0 copy-start.2
  24.1 0.1 broadcast_in_dim.7
  24.2 0.1 reshape.11
  24.3 0.5 %slice_divide_fusion = f32[48]{0:T(128)} fusion(f32[48]{0:T(128)S(1)} %reshape.11, f32[128]{0:T(128)S(1)} %reduce_min.9), kind=kLoop, calls=%fused_computation.1 | loop fusion | flops 48 | bytes 576 | tf_op jit(solution)/shard_map/div | solution.py:323
  24.8 0.0 copy-done.2
  (1 shorter events, 0.0 us)
Async XLA Ops:
  0.6 4.7 %collective-permute-start = (bf16[128,6144]{1,0:T(8,128)(2,1)}, bf16[128,6144]{1,0:T(8,128)(2,1)S(1)}, u32[]{:S(2)}, u32[]{:S(2)}) collective-permute-start(bf16[128,6144]{1,0:T(8,128)(2,1)} %bitcast.11), channel_id=1, source_target_pairs={{0,1},{1,0},{2,3},{3,2},{4,5},{5,4},{6,7},{7,6},{8,9},{9,8},{10,11... | collective-permute-start | bytes 4718600 | tf_op jit(solution)/shard_map/ppermute | solution.py:221
  1.1 8.3 %collective-permute-start.1 = (bf16[128,768]{1,0:T(8,128)(2,1)}, bf16[128,768]{1,0:T(8,128)(2,1)S(1)}, u32[]{:S(2)}, u32[]{:S(2)}) collective-permute-start(bf16[128,768]{1,0:T(8,128)(2,1)} %bitcast.14), channel_id=1, source_target_pairs={{0,2},{1,3},{2,0},{3,1},{4,6},{5,7},{6,4},{7,5},{8,10},{9,11},{10,... | collective-permute-start | bytes 589832 | tf_op jit(solution)/shard_map/ppermute | solution.py:220
  5.3 1.0 %copy-start.1 = (bf16[1,128,768]{2,1,0:T(8,128)(2,1)S(1)}, bf16[1,128,768]{2,1,0:T(8,128)(2,1)}, u32[]{:S(2)}) copy-start(bf16[1,128,768]{2,1,0:T(8,128)(2,1)} %param.5) | copy-start | bytes 589828
  5.3 1.3 %copy-start = (bf16[1,128,768]{2,1,0:T(8,128)(2,1)S(1)}, bf16[1,128,768]{2,1,0:T(8,128)(2,1)}, u32[]{:S(2)}) copy-start(bf16[1,128,768]{2,1,0:T(8,128)(2,1)} %param.6) | copy-start | bytes 589828
  6.3 10.5 %collective-permute-start.2 = (bf16[128,768]{1,0:T(8,128)(2,1)S(1)}, bf16[128,768]{1,0:T(8,128)(2,1)S(1)}, u32[]{:S(2)}, u32[]{:S(2)}) collective-permute-start(bf16[128,768]{1,0:T(8,128)(2,1)S(1)} %bitcast.16), channel_id=1, source_target_pairs={{0,1},{1,2},{2,3},{3,0},{4,5},{5,6},{6,7},{7,4},{8,9},{9,10},{10,1... | collective-permute-start | bytes 589832 | tf_op jit(solution)/shard_map/ppermute | solution.py:239
  6.6 10.3 %collective-permute-start.4 = (bf16[128,768]{1,0:T(8,128)(2,1)S(1)}, bf16[128,768]{1,0:T(8,128)(2,1)S(1)}, u32[]{:S(2)}, u32[]{:S(2)}) collective-permute-start(bf16[128,768]{1,0:T(8,128)(2,1)S(1)} %bitcast.8), channel_id=1, source_target_pairs={{0,2},{1,3},{2,0},{3,1},{4,6},{5,7},{6,4},{7,5},{8,10},{9,11},{10,... | collective-permute-start | bytes 589832 | tf_op jit(solution)/shard_map/ppermute | solution.py:237
  8.5 9.4 %collective-permute-start.3 = (bf16[128,768]{1,0:T(8,128)(2,1)S(1)}, bf16[128,768]{1,0:T(8,128)(2,1)S(1)}, u32[]{:S(2)}, u32[]{:S(2)}) collective-permute-start(bf16[128,768]{1,0:T(8,128)(2,1)S(1)} %bitcast.9), channel_id=1, source_target_pairs={{0,1},{1,2},{2,3},{3,0},{4,5},{5,6},{6,7},{7,4},{8,9},{9,10},{10,1... | collective-permute-start | bytes 589832 | tf_op jit(solution)/shard_map/ppermute | solution.py:238
  10.8 13.3 %all-to-all-start = ((f32[32,1,128]{2,1,0:T(1,128)}), f32[32,1,128]{2,1,0:T(1,128)S(1)}, u32[]{:S(2)}, u32[]{:S(2)}) async-start(f32[32,1,128]{2,1,0:T(1,128)} %bitcast.4), calls=%async_computation | async-start | bytes 32768 | tf_op jit(solution)/shard_map/all_to_all | solution.py:254
  24.1 0.7 %copy-start.2 = (f32[6]{0:T(128)}, f32[6]{0:T(128)S(1)}, u32[]{:S(2)}) copy-start(f32[6]{0:T(128)S(1)} %slice_sqrt_fusion) | copy-start | bytes 76

commit v11 on v8

--- a/solution.py
+++ b/solution.py
@@ -18,7 +18,7 @@
 SCALE = HEAD_SIZE ** (-0.5)
 SCALE_2 = SCALE * math.log2(math.e)
 MASKED = -1e30
-KEY_HEAD_LANE = 64
+GROUP_LANE, KEY_HEAD_LANE = 48, 96
 NT = (((1,), (1,)), ((), ()))
 
 
@@ -74,8 +74,8 @@
         jnp.max(largest[c * GROUP : (c + 1) * GROUP, :], axis=0, keepdims=True)
         for c in range(KEY_VALUE_HEADS)
     ]
-    spare = KEY_HEAD_LANE - QUERY_HEADS
-    padded = jnp.concatenate([largest, largest[:spare], *groups, largest, largest], axis=0)[:rows]
+    repeated = [jnp.broadcast_to(g, (GROUP, rows)) for g in groups]
+    padded = jnp.concatenate([largest, *repeated, *groups, largest], axis=0)[:rows]
     head_max = jnp.max(padded.T, axis=0, keepdims=True) * SCALE
     clipped = clip_level / jnp.maximum(head_max, clip_level)
     clipped_ref[...] = jnp.broadcast_to(clipped[None], clipped_ref.shape)
@@ -317,11 +317,6 @@
     return attended, everyone
 
 
-def clip_factors(clipped, smallest):
-    key_head_factor = jnp.sqrt(smallest)
-    return (clipped / jnp.repeat(key_head_factor, GROUP), key_head_factor)
-
-
 def local(queries, keys, values, segments):
     rows, length = queries.shape[1], segments.shape[1]
     shards = lax.axis_size("seq")
@@ -334,9 +329,10 @@
         attended, everyone = plan_of_rotations(*arrays, reach, shards)
     everyone, attended = lax.optimization_barrier((everyone, attended))
     clipped = jnp.min(everyone[:, 0, :], axis=0)
-    query_factor, key_head_factor = clip_factors(
-        clipped[:QUERY_HEADS], clipped[KEY_HEAD_LANE : KEY_HEAD_LANE + KEY_VALUE_HEADS]
-    )
+    key_head_factor = jnp.sqrt(clipped[KEY_HEAD_LANE : KEY_HEAD_LANE + KEY_VALUE_HEADS])
+    smallest = clipped[GROUP_LANE : GROUP_LANE + QUERY_HEADS]
+    floor = key_head_factor[0] * 0.0
+    query_factor = clipped[:QUERY_HEADS] / jnp.maximum(jnp.sqrt(smallest), floor)
     return (attended[None], query_factor, key_head_factor)
 
 

time: 25 us -> 25 us (level)
  no operation moved by 1% of the time
where the time goes in v11:
time: 25 us; the launch traced here: 24.8 us
  starting transfers between devices  11.3 us (45%)
  Pallas kernels  8.32 us (33%)
  waiting for transfers between devices  3.66 us (15%)
  between operations  0.76 us (3%)
  other arithmetic  0.65 us (3%)
    pallas_call x3, Pallas kernels, call(): pl.pallas_call(kernel, out_shape=out_shape, in_specs=[VMEM] * len(arrays)...  6.76 us
    all_to_all x1, starting transfers between devices, plan_of_pairs(): everyone = lax.all_to_all(clipped, ('dp', 'seq'), 0, 0)  6.11 us
    ppermute x1, starting transfers between devices, plan_of_pairs(): far_keys = lax.ppermute(keys, 'seq', across)  2.56 us
    ppermute x1, starting transfers between devices, plan_of_pairs(): far_values = lax.ppermute(values, 'seq', across)  1.91 us
    all_to_all x1, waiting for transfers between devices, plan_of_pairs(): everyone = lax.all_to_all(clipped, ('dp', 'seq'), 0, 0)  1.75 us
    pallas_call x1, Pallas kernels, load(): pl.pallas_call(functools.partial(load_kernel, shards, pairs), out_shape=(...  1.56 us
    ppermute x1, waiting for transfers between devices, plan_of_pairs(): far_keys = lax.ppermute(keys, 'seq', across)  0.95 us
    ppermute x1, waiting for transfers between devices, plan_of_pairs(): near_values = lax.ppermute(values, 'seq', rotate)  0.95 us
  transfers between devices with their start and end apart: 6, of which 3 were waited for; matrix products, arithmetic and copies ran while one was open for 0% of the time, Pallas kernels for 34%

profile of v11, /device:TPU:0, one launch (start us, length us, event | category | flops | bytes accessed | tf_op | source)
XLA Modules:
  0.0 24.8 jit_solution(5141373991351490135)
XLA Ops:
  0.6 0.5 %collective-permute-start = (bf16[128,6144]{1,0:T(8,128)(2,1)}, bf16[128,6144]{1,0:T(8,128)(2,1)S(1)}, u32[]{:S(2)}, u32[]{:S(2)}) collective-permute-start(bf16[128,6144]{1,0:T(8,128)(2,1)} %bitcast.9), channel_id=1, source_target_pairs={{0,1},{1,0},{2,3},{3,2},{4,5},{5,4},{6,7},{7,6},{8,9},{9,8},{10,11... | collective-permute-start | bytes 4718600 | tf_op jit(solution)/shard_map/ppermute | solution.py:220
  1.1 2.6 %collective-permute-start.1 = (bf16[128,768]{1,0:T(8,128)(2,1)}, bf16[128,768]{1,0:T(8,128)(2,1)S(1)}, u32[]{:S(2)}, u32[]{:S(2)}) collective-permute-start(bf16[128,768]{1,0:T(8,128)(2,1)} %bitcast.12), channel_id=1, source_target_pairs={{0,2},{1,3},{2,0},{3,1},{4,6},{5,7},{6,4},{7,5},{8,10},{9,11},{10,... | collective-permute-start | bytes 589832 | tf_op jit(solution)/shard_map/ppermute | solution.py:219
  3.7 1.6 %load.1 = (f32[640,128]{1,0:T(8,128)S(1)}, bf16[128,6144]{1,0:T(8,128)(2,1)S(1)}, bf16[128,768]{1,0:T(8,128)(2,1)S(1)}) custom-call(s32[1,512]{1,0:T(1,128)} %seg_hbm.1, bf16[128,6144]{1,0:T(8,128)(2,1)} %bitcast.10, bf16[128,768]{1,0:T(8,128)(2,1)} %bitcast.13), custom_call_target="tpu_custom_call" | custom-call | bytes 1769472 | tf_op jit(solution)/shard_map/load/pallas_call | solution.py:181
  5.3 0.0 collective-permute-done.refs_0_.partner_ref
  5.3 0.0 copy-start.1
  5.3 0.0 copy-start
  5.3 1.0 %first_maxima.1 = (f32[48,128]{1,0:T(8,128)S(1)}, f32[48,128]{1,0:T(8,128)S(1)}) custom-call(f32[640,128]{1,0:T(8,128)S(1)} %get-tuple-element.15.bias_ref, bf16[128,6144]{1,0:T(8,128)(2,1)S(1)} %get-tuple-element.16.q_ref, bf16[128,768]{1,0:T(8,128)(2,1)S(1)} %get-tuple-element.17.key_ref.own, bf16[128,6144]{1,0:T(8,128)(2,1)S(1)} %collective-permute-done.refs_0_.partner_ref), custom_call_target="tpu_custom_call" | custom-call | flops 402653184 | bytes 1572864 | tf_op jit(solution)/shard_map/first_maxima/pallas_call | solution.py:159
  6.3 0.0 copy-done.1
  6.3 0.2 collective-permute-start.2
  6.6 0.0 copy-done
  6.6 1.9 %collective-permute-start.4 = (bf16[128,768]{1,0:T(8,128)(2,1)S(1)}, bf16[128,768]{1,0:T(8,128)(2,1)S(1)}, u32[]{:S(2)}, u32[]{:S(2)}) collective-permute-start(bf16[128,768]{1,0:T(8,128)(2,1)S(1)} %bitcast.6), channel_id=1, source_target_pairs={{0,2},{1,3},{2,0},{3,1},{4,6},{5,7},{6,4},{7,5},{8,10},{9,11},{10,... | collective-permute-start | bytes 589832 | tf_op jit(solution)/shard_map/ppermute | solution.py:236
  8.5 0.0 collective-permute-start.3
  8.5 1.0 %collective-permute-done.1.key_ref.far = bf16[128,768]{1,0:T(8,128)(2,1)S(1)} collective-permute-done((bf16[128,768]{1,0:T(8,128)(2,1)}, bf16[128,768]{1,0:T(8,128)(2,1)S(1)}, u32[]{:S(2)}, u32[]{:S(2)}) %collective-permute-start.1) | collective-permute-done | bytes 196640 | tf_op jit(solution)/shard_map/ppermute | solution.py:219
  9.4 1.3 %last_maxima.1 = (f32[48,128]{1,0:T(8,128)S(1)}, f32[32,1,128]{2,1,0:T(1,128)}) custom-call(f32[640,128]{1,0:T(8,128)S(1)} %get-tuple-element.15.bias_ref, bf16[128,6144]{1,0:T(8,128)(2,1)S(1)} %get-tuple-element.16.q_ref, bf16[128,6144]{1,0:T(8,128)(2,1)S(1)} %collective-permute-done.refs_0_.partner_ref, f32[48,128]{1,0:T(8,128)S(1)} %get-tuple-element.18.before_ref, ...), custom_call_target="tpu_custom_call" | custom-call | flops 402653184 | bytes 1572864 | tf_op jit(solution)/shard_map/last_maxima/pallas_call | solution.py:159
  10.8 6.1 %all-to-all-start = ((f32[32,1,128]{2,1,0:T(1,128)}), f32[32,1,128]{2,1,0:T(1,128)S(1)}, u32[]{:S(2)}, u32[]{:S(2)}) async-start(f32[32,1,128]{2,1,0:T(1,128)} %get-tuple-element.21), calls=%async_computation | async-start | bytes 32768 | tf_op jit(solution)/shard_map/all_to_all | solution.py:253
  16.9 0.0 collective-permute-done.2.near
  16.9 0.0 collective-permute-done.4.refs_2_
  16.9 0.9 %collective-permute-done.3.refs_1_ = bf16[128,768]{1,0:T(8,128)(2,1)S(1)} collective-permute-done((bf16[128,768]{1,0:T(8,128)(2,1)S(1)}, bf16[128,768]{1,0:T(8,128)(2,1)S(1)}, u32[]{:S(2)}, u32[]{:S(2)}) %collective-permute-start.3) | collective-permute-done | bytes 196640 | tf_op jit(solution)/shard_map/ppermute | solution.py:237
  17.8 4.4 %mix.1 = bf16[128,6144]{1,0:T(8,128)(2,1)} custom-call(f32[640,128]{1,0:T(8,128)S(1)} %get-tuple-element.15.bias_ref, bf16[128,6144]{1,0:T(8,128)(2,1)S(1)} %get-tuple-element.16.q_ref, f32[48,128]{1,0:T(8,128)S(1)} %get-tuple-element.22.row_max_ref, bf16[128,768]{1,0:T(8,128)(2,1)S(1)} %get-tuple-element.17.key_ref.own, ...), custom_call_target="tpu_custom_call" | custom-call | flops 1207959552 | bytes 3145728 | tf_op jit(solution)/shard_map/mix/pallas_call | solution.py:159
  22.3 1.8 %all-to-all-done = f32[32,1,128]{2,1,0:T(1,128)S(1)} async-done(((f32[32,1,128]{2,1,0:T(1,128)}), f32[32,1,128]{2,1,0:T(1,128)S(1)}, u32[]{:S(2)}, u32[]{:S(2)}) %all-to-all-start) | async-done | bytes 16416 | tf_op jit(solution)/shard_map/all_to_all | solution.py:253
  24.0 0.1 reduce_min.9
  24.1 0.1 slice_sqrt_fusion
  24.2 0.0 copy-start.2
  24.2 0.6 %maximum_divide_fusion = f32[48]{0:T(128)} fusion(f32[128]{0:T(128)S(1)} %reduce_min.9, f32[]{:T(128)} %bitcast.4), kind=kLoop, calls=%fused_computation | loop fusion | flops 96 | bytes 580 | tf_op jit(solution)/shard_map/div | solution.py:335
  24.8 0.0 copy-done.2
Async XLA Ops:
  0.6 4.7 %collective-permute-start = (bf16[128,6144]{1,0:T(8,128)(2,1)}, bf16[128,6144]{1,0:T(8,128)(2,1)S(1)}, u32[]{:S(2)}, u32[]{:S(2)}) collective-permute-start(bf16[128,6144]{1,0:T(8,128)(2,1)} %bitcast.9), channel_id=1, source_target_pairs={{0,1},{1,0},{2,3},{3,2},{4,5},{5,4},{6,7},{7,6},{8,9},{9,8},{10,11... | collective-permute-start | bytes 4718600 | tf_op jit(solution)/shard_map/ppermute | solution.py:220
  1.1 8.3 %collective-permute-start.1 = (bf16[128,768]{1,0:T(8,128)(2,1)}, bf16[128,768]{1,0:T(8,128)(2,1)S(1)}, u32[]{:S(2)}, u32[]{:S(2)}) collective-permute-start(bf16[128,768]{1,0:T(8,128)(2,1)} %bitcast.12), channel_id=1, source_target_pairs={{0,2},{1,3},{2,0},{3,1},{4,6},{5,7},{6,4},{7,5},{8,10},{9,11},{10,... | collective-permute-start | bytes 589832 | tf_op jit(solution)/shard_map/ppermute | solution.py:219
  5.3 1.0 %copy-start.1 = (bf16[1,128,768]{2,1,0:T(8,128)(2,1)S(1)}, bf16[1,128,768]{2,1,0:T(8,128)(2,1)}, u32[]{:S(2)}) copy-start(bf16[1,128,768]{2,1,0:T(8,128)(2,1)} %param.5) | copy-start | bytes 589828
  5.3 1.3 %copy-start = (bf16[1,128,768]{2,1,0:T(8,128)(2,1)S(1)}, bf16[1,128,768]{2,1,0:T(8,128)(2,1)}, u32[]{:S(2)}) copy-start(bf16[1,128,768]{2,1,0:T(8,128)(2,1)} %param.6) | copy-start | bytes 589828
  6.3 10.5 %collective-permute-start.2 = (bf16[128,768]{1,0:T(8,128)(2,1)S(1)}, bf16[128,768]{1,0:T(8,128)(2,1)S(1)}, u32[]{:S(2)}, u32[]{:S(2)}) collective-permute-start(bf16[128,768]{1,0:T(8,128)(2,1)S(1)} %bitcast.14), channel_id=1, source_target_pairs={{0,1},{1,2},{2,3},{3,0},{4,5},{5,6},{6,7},{7,4},{8,9},{9,10},{10,1... | collective-permute-start | bytes 589832 | tf_op jit(solution)/shard_map/ppermute | solution.py:238
  6.6 10.3 %collective-permute-start.4 = (bf16[128,768]{1,0:T(8,128)(2,1)S(1)}, bf16[128,768]{1,0:T(8,128)(2,1)S(1)}, u32[]{:S(2)}, u32[]{:S(2)}) collective-permute-start(bf16[128,768]{1,0:T(8,128)(2,1)S(1)} %bitcast.6), channel_id=1, source_target_pairs={{0,2},{1,3},{2,0},{3,1},{4,6},{5,7},{6,4},{7,5},{8,10},{9,11},{10,... | collective-permute-start | bytes 589832 | tf_op jit(solution)/shard_map/ppermute | solution.py:236
  8.5 9.4 %collective-permute-start.3 = (bf16[128,768]{1,0:T(8,128)(2,1)S(1)}, bf16[128,768]{1,0:T(8,128)(2,1)S(1)}, u32[]{:S(2)}, u32[]{:S(2)}) collective-permute-start(bf16[128,768]{1,0:T(8,128)(2,1)S(1)} %bitcast.7), channel_id=1, source_target_pairs={{0,1},{1,2},{2,3},{3,0},{4,5},{5,6},{6,7},{7,4},{8,9},{9,10},{10,1... | collective-permute-start | bytes 589832 | tf_op jit(solution)/shard_map/ppermute | solution.py:237
  10.8 13.3 %all-to-all-start = ((f32[32,1,128]{2,1,0:T(1,128)}), f32[32,1,128]{2,1,0:T(1,128)S(1)}, u32[]{:S(2)}, u32[]{:S(2)}) async-start(f32[32,1,128]{2,1,0:T(1,128)} %get-tuple-element.21), calls=%async_computation | async-start | bytes 32768 | tf_op jit(solution)/shard_map/all_to_all | solution.py:253
  24.2 0.7 %copy-start.2 = (f32[6]{0:T(128)}, f32[6]{0:T(128)S(1)}, u32[]{:S(2)}) copy-start(f32[6]{0:T(128)S(1)} %slice_sqrt_fusion) | copy-start | bytes 76

commit v12 on v8

--- a/solution.py
+++ b/solution.py
@@ -233,9 +233,10 @@
         partner_queries,
     )
     sent_keys, values, near_max = lax.optimization_barrier((keys, values, near_max))
+    near_keys = lax.ppermute(sent_keys, "seq", rotate)
+    near_values = lax.ppermute(values, "seq", rotate)
+    values, near_max = lax.optimization_barrier((values, near_max))
     far_values = lax.ppermute(values, "seq", across)
-    near_values = lax.ppermute(values, "seq", rotate)
-    near_keys = lax.ppermute(sent_keys, "seq", rotate)
     row_max, clipped = call(
         last_paired_kernel,
         "last_maxima",

time: 25 us -> 25.1 us (level)
  transfers between devices with their start and end apart: 6 -> 6, of which waited for: 3 -> 3; matrix products, arithmetic and copies ran while one was open for 0% -> 0% of each run, Pallas kernels for 34% -> 33%
where the time goes in v12:
time: 25.1 us; the launch traced here: 24.9 us
  starting transfers between devices  11.4 us (45%)
  Pallas kernels  8.32 us (33%)
  waiting for transfers between devices  3.61 us (14%)
  between operations  0.71 us (3%)
  other arithmetic  0.58 us (2%)
    pallas_call x3, Pallas kernels, call(): pl.pallas_call(kernel, out_shape=out_shape, in_specs=[VMEM] * len(arrays)...  6.76 us
    all_to_all x1, starting transfers between devices, plan_of_pairs(): everyone = lax.all_to_all(clipped, ('dp', 'seq'), 0, 0)  6.13 us
    ppermute x1, starting transfers between devices, plan_of_pairs(): far_keys = lax.ppermute(keys, 'seq', across)  2.56 us
    ppermute x1, starting transfers between devices, plan_of_pairs(): far_values = lax.ppermute(values, 'seq', across)  2.01 us
    all_to_all x1, waiting for transfers between devices, plan_of_pairs(): everyone = lax.all_to_all(clipped, ('dp', 'seq'), 0, 0)  1.79 us
    pallas_call x1, Pallas kernels, load(): pl.pallas_call(functools.partial(load_kernel, shards, pairs), out_shape=(...  1.56 us
    ppermute x1, waiting for transfers between devices, plan_of_pairs(): near_values = lax.ppermute(values, 'seq', rotate)  0.91 us
    ppermute x1, waiting for transfers between devices, plan_of_pairs(): far_keys = lax.ppermute(keys, 'seq', across)  0.9 us
  transfers between devices with their start and end apart: 6, of which 3 were waited for; matrix products, arithmetic and copies ran while one was open for 0% of the time, Pallas kernels for 33%

profile of v12, /device:TPU:0, one launch (start us, length us, event | category | flops | bytes accessed | tf_op | source)
XLA Modules:
  0.0 24.9 jit_solution(17932763124556955843)
XLA Ops:
  0.6 0.5 %collective-permute-start = (bf16[128,6144]{1,0:T(8,128)(2,1)}, bf16[128,6144]{1,0:T(8,128)(2,1)S(1)}, u32[]{:S(2)}, u32[]{:S(2)}) collective-permute-start(bf16[128,6144]{1,0:T(8,128)(2,1)} %bitcast.7), channel_id=1, source_target_pairs={{0,1},{1,0},{2,3},{3,2},{4,5},{5,4},{6,7},{7,6},{8,9},{9,8},{10,11... | collective-permute-start | bytes 4718600 | tf_op jit(solution)/shard_map/ppermute | solution.py:220
  1.1 2.6 %collective-permute-start.1 = (bf16[128,768]{1,0:T(8,128)(2,1)}, bf16[128,768]{1,0:T(8,128)(2,1)S(1)}, u32[]{:S(2)}, u32[]{:S(2)}) collective-permute-start(bf16[128,768]{1,0:T(8,128)(2,1)} %bitcast.10), channel_id=1, source_target_pairs={{0,2},{1,3},{2,0},{3,1},{4,6},{5,7},{6,4},{7,5},{8,10},{9,11},{10,... | collective-permute-start | bytes 589832 | tf_op jit(solution)/shard_map/ppermute | solution.py:219
  3.7 1.6 %load.1 = (f32[640,128]{1,0:T(8,128)S(1)}, bf16[128,6144]{1,0:T(8,128)(2,1)S(1)}, bf16[128,768]{1,0:T(8,128)(2,1)S(1)}) custom-call(s32[1,512]{1,0:T(1,128)} %seg_hbm.1, bf16[128,6144]{1,0:T(8,128)(2,1)} %bitcast.8, bf16[128,768]{1,0:T(8,128)(2,1)} %bitcast.11), custom_call_target="tpu_custom_call" | custom-call | bytes 1769472 | tf_op jit(solution)/shard_map/load/pallas_call | solution.py:181
  5.3 0.0 collective-permute-done.refs_0_.partner_ref
  5.3 0.0 copy-start
  5.3 0.0 copy-start.1
  5.3 1.0 %first_maxima.1 = (f32[48,128]{1,0:T(8,128)S(1)}, f32[48,128]{1,0:T(8,128)S(1)}) custom-call(f32[640,128]{1,0:T(8,128)S(1)} %get-tuple-element.17.bias_ref, bf16[128,6144]{1,0:T(8,128)(2,1)S(1)} %get-tuple-element.18.q_ref, bf16[128,768]{1,0:T(8,128)(2,1)S(1)} %get-tuple-element.19.key_ref.own, bf16[128,6144]{1,0:T(8,128)(2,1)S(1)} %collective-permute-done.refs_0_.partner_ref), custom_call_target="tpu_custom_call" | custom-call | flops 402653184 | bytes 1572864 | tf_op jit(solution)/shard_map/first_maxima/pallas_call | solution.py:159
  6.3 0.0 copy-done
  6.3 2.0 %collective-permute-start.4 = (bf16[128,768]{1,0:T(8,128)(2,1)S(1)}, bf16[128,768]{1,0:T(8,128)(2,1)S(1)}, u32[]{:S(2)}, u32[]{:S(2)}) collective-permute-start(bf16[128,768]{1,0:T(8,128)(2,1)S(1)} %bitcast.4), channel_id=1, source_target_pairs={{0,2},{1,3},{2,0},{3,1},{4,6},{5,7},{6,4},{7,5},{8,10},{9,11},{10,... | collective-permute-start | bytes 589832 | tf_op jit(solution)/shard_map/ppermute | solution.py:239
  8.3 0.0 copy-done.1
  8.3 0.0 collective-permute-start.2
  8.3 0.2 collective-permute-start.3
  8.5 0.9 %collective-permute-done.1.key_ref.far = bf16[128,768]{1,0:T(8,128)(2,1)S(1)} collective-permute-done((bf16[128,768]{1,0:T(8,128)(2,1)}, bf16[128,768]{1,0:T(8,128)(2,1)S(1)}, u32[]{:S(2)}, u32[]{:S(2)}) %collective-permute-start.1) | collective-permute-done | bytes 196640 | tf_op jit(solution)/shard_map/ppermute | solution.py:219
  9.4 1.3 %last_maxima.1 = (f32[48,128]{1,0:T(8,128)S(1)}, f32[32,1,128]{2,1,0:T(1,128)}) custom-call(f32[640,128]{1,0:T(8,128)S(1)} %get-tuple-element.17.bias_ref, bf16[128,6144]{1,0:T(8,128)(2,1)S(1)} %get-tuple-element.18.q_ref, bf16[128,6144]{1,0:T(8,128)(2,1)S(1)} %collective-permute-done.refs_0_.partner_ref, f32[48,128]{1,0:T(8,128)S(1)} %get-tuple-element.20.before_ref, ...), custom_call_target="tpu_custom_call" | custom-call | flops 402653184 | bytes 1572864 | tf_op jit(solution)/shard_map/last_maxima/pallas_call | solution.py:159
  10.8 6.1 %all-to-all-start = ((f32[32,1,128]{2,1,0:T(1,128)}), f32[32,1,128]{2,1,0:T(1,128)S(1)}, u32[]{:S(2)}, u32[]{:S(2)}) async-start(f32[32,1,128]{2,1,0:T(1,128)} %get-tuple-element.25), calls=%async_computation | async-start | bytes 32768 | tf_op jit(solution)/shard_map/all_to_all | solution.py:254
  16.9 0.0 collective-permute-done.4.refs_2_
  16.9 0.0 collective-permute-done.2.near
  16.9 0.9 %collective-permute-done.3.refs_1_ = bf16[128,768]{1,0:T(8,128)(2,1)S(1)} collective-permute-done((bf16[128,768]{1,0:T(8,128)(2,1)S(1)}, bf16[128,768]{1,0:T(8,128)(2,1)S(1)}, u32[]{:S(2)}, u32[]{:S(2)}) %collective-permute-start.3) | collective-permute-done | bytes 196640 | tf_op jit(solution)/shard_map/ppermute | solution.py:237
  17.8 4.4 %mix.1 = bf16[128,6144]{1,0:T(8,128)(2,1)} custom-call(f32[640,128]{1,0:T(8,128)S(1)} %get-tuple-element.17.bias_ref, bf16[128,6144]{1,0:T(8,128)(2,1)S(1)} %get-tuple-element.18.q_ref, f32[48,128]{1,0:T(8,128)S(1)} %get-tuple-element.26.row_max_ref, bf16[128,768]{1,0:T(8,128)(2,1)S(1)} %get-tuple-element.19.key_ref.own, ...), custom_call_target="tpu_custom_call" | custom-call | flops 1207959552 | bytes 3145728 | tf_op jit(solution)/shard_map/mix/pallas_call | solution.py:159
  22.3 1.8 %all-to-all-done = f32[32,1,128]{2,1,0:T(1,128)S(1)} async-done(((f32[32,1,128]{2,1,0:T(1,128)}), f32[32,1,128]{2,1,0:T(1,128)S(1)}, u32[]{:S(2)}, u32[]{:S(2)}) %all-to-all-start) | async-done | bytes 16416 | tf_op jit(solution)/shard_map/all_to_all | solution.py:254
  24.1 0.1 reduce_min.9
  24.1 0.1 slice_sqrt_fusion
  24.2 0.0 copy-start.2
  24.2 0.1 broadcast_in_dim.7
  24.3 0.1 reshape.9
  24.3 0.5 %slice_divide_fusion = f32[48]{0:T(128)} fusion(f32[48]{0:T(128)S(1)} %reshape.9, f32[128]{0:T(128)S(1)} %reduce_min.9), kind=kLoop, calls=%fused_computation.1 | loop fusion | flops 48 | bytes 576 | tf_op jit(solution)/shard_map/div | solution.py:323
  24.9 0.0 copy-done.2
Async XLA Ops:
  0.6 4.7 %collective-permute-start = (bf16[128,6144]{1,0:T(8,128)(2,1)}, bf16[128,6144]{1,0:T(8,128)(2,1)S(1)}, u32[]{:S(2)}, u32[]{:S(2)}) collective-permute-start(bf16[128,6144]{1,0:T(8,128)(2,1)} %bitcast.7), channel_id=1, source_target_pairs={{0,1},{1,0},{2,3},{3,2},{4,5},{5,4},{6,7},{7,6},{8,9},{9,8},{10,11... | collective-permute-start | bytes 4718600 | tf_op jit(solution)/shard_map/ppermute | solution.py:220
  1.1 8.3 %collective-permute-start.1 = (bf16[128,768]{1,0:T(8,128)(2,1)}, bf16[128,768]{1,0:T(8,128)(2,1)S(1)}, u32[]{:S(2)}, u32[]{:S(2)}) collective-permute-start(bf16[128,768]{1,0:T(8,128)(2,1)} %bitcast.10), channel_id=1, source_target_pairs={{0,2},{1,3},{2,0},{3,1},{4,6},{5,7},{6,4},{7,5},{8,10},{9,11},{10,... | collective-permute-start | bytes 589832 | tf_op jit(solution)/shard_map/ppermute | solution.py:219
  5.3 1.0 %copy-start = (bf16[1,128,768]{2,1,0:T(8,128)(2,1)S(1)}, bf16[1,128,768]{2,1,0:T(8,128)(2,1)}, u32[]{:S(2)}) copy-start(bf16[1,128,768]{2,1,0:T(8,128)(2,1)} %param.6) | copy-start | bytes 589828
  5.3 3.0 %copy-start.1 = (bf16[1,128,768]{2,1,0:T(8,128)(2,1)S(1)}, bf16[1,128,768]{2,1,0:T(8,128)(2,1)}, u32[]{:S(2)}) copy-start(bf16[1,128,768]{2,1,0:T(8,128)(2,1)} %param.5) | copy-start | bytes 589828
  6.3 10.6 %collective-permute-start.4 = (bf16[128,768]{1,0:T(8,128)(2,1)S(1)}, bf16[128,768]{1,0:T(8,128)(2,1)S(1)}, u32[]{:S(2)}, u32[]{:S(2)}) collective-permute-start(bf16[128,768]{1,0:T(8,128)(2,1)S(1)} %bitcast.4), channel_id=1, source_target_pairs={{0,2},{1,3},{2,0},{3,1},{4,6},{5,7},{6,4},{7,5},{8,10},{9,11},{10,... | collective-permute-start | bytes 589832 | tf_op jit(solution)/shard_map/ppermute | solution.py:239
  8.3 8.6 %collective-permute-start.2 = (bf16[128,768]{1,0:T(8,128)(2,1)S(1)}, bf16[128,768]{1,0:T(8,128)(2,1)S(1)}, u32[]{:S(2)}, u32[]{:S(2)}) collective-permute-start(bf16[128,768]{1,0:T(8,128)(2,1)S(1)} %bitcast.12), channel_id=1, source_target_pairs={{0,1},{1,2},{2,3},{3,0},{4,5},{5,6},{6,7},{7,4},{8,9},{9,10},{10,1... | collective-permute-start | bytes 589832 | tf_op jit(solution)/shard_map/ppermute | solution.py:236
  8.3 9.5 %collective-permute-start.3 = (bf16[128,768]{1,0:T(8,128)(2,1)S(1)}, bf16[128,768]{1,0:T(8,128)(2,1)S(1)}, u32[]{:S(2)}, u32[]{:S(2)}) collective-permute-start(bf16[128,768]{1,0:T(8,128)(2,1)S(1)} %bitcast.5), channel_id=1, source_target_pairs={{0,1},{1,2},{2,3},{3,0},{4,5},{5,6},{6,7},{7,4},{8,9},{9,10},{10,1... | collective-permute-start | bytes 589832 | tf_op jit(solution)/shard_map/ppermute | solution.py:237
  10.8 13.3 %all-to-all-start = ((f32[32,1,128]{2,1,0:T(1,128)}), f32[32,1,128]{2,1,0:T(1,128)S(1)}, u32[]{:S(2)}, u32[]{:S(2)}) async-start(f32[32,1,128]{2,1,0:T(1,128)} %get-tuple-element.25), calls=%async_computation | async-start | bytes 32768 | tf_op jit(solution)/shard_map/all_to_all | solution.py:254
  24.2 0.7 %copy-start.2 = (f32[6]{0:T(128)}, f32[6]{0:T(128)S(1)}, u32[]{:S(2)}) copy-start(f32[6]{0:T(128)S(1)} %slice_sqrt_fusion) | copy-start | bytes 76
